TPU v7x, 512 devices: a whole 4x8x8 slice. The times are simulated.
512 devices in a mesh: lon: 32 (over z_hi, y, core), lat: 16 (over x, z_lo).
Axes of the slice: x: 4, y: 8, z: 8 (z_hi: 2, z_lo: 4; z = z_hi * 4 + z_lo), core: 2. Of those that a mesh axis runs over, the one named last changes fastest.
Arguments:
- potential_warmth_degrees: float32 [8, 1536, 4096], P(None, 'lat', 'lon'), may hold values from -1.8 to 28
- dissolved_salt_content: float32 [8, 1536, 4096], P(None, 'lat', 'lon'), may hold values from 18 to 37
- zonal_edge_current: float32 [8, 1536, 4096], P(None, 'lat', 'lon'), may hold values from -3 to 3
- meridional_edge_current: float32 [8, 1536, 4096], P(None, 'lat', 'lon'), may hold values from -3 to 3
- wet_grid_flag: int32 [8, 1536, 4096], P(None, 'lat', 'lon'), may hold values from 0 to 1, as said below
- zonal_wet_edge_flag: int32 [8, 1536, 4096], P(None, 'lat', 'lon'), may hold values from 0 to 1, as said below
- meridional_wet_edge_flag: int32 [8, 1536, 4096], P(None, 'lat', 'lon'), may hold values from 0 to 1, as said below
- bottom_tier_count: int32 [1536, 4096], P('lat', 'lon'), may hold values from 0 to 8, as said below
- zonal_grid_spacing: float32 [1536, 4096], P('lat', 'lon'), may hold values from 1800 to 7000
- meridional_grid_spacing: float32 [1536, 4096], P('lat', 'lon'), may hold values from 1800 to 7000
Outputs:
- temperature_after: float32 [8, 1536, 4096], P(None, 'lat', 'lon')
- salinity_after: float32 [8, 1536, 4096], P(None, 'lat', 'lon')
- zonal_after: float32 [8, 1536, 4096], P(None, 'lat', 'lon')
- meridional_after: float32 [8, 1536, 4096], P(None, 'lat', 'lon')
Inputs may be any that keep to these rules, and one draw needn't show every extreme that they name: wet_grid_flag[k, j, i] is 1 exactly where k < bottom_tier_count[j, i]. zonal_wet_edge_flag is wet_grid_flag times wet_grid_flag of the cell to the east (east of column 4095 is column 0). meridional_wet_edge_flag is wet_grid_flag times wet_grid_flag of the cell to the north; north of row 1535 at column i lies row 1535 at column 4095 - i. `bottom_tier_count`: some column is all land and some column is sea at every level.
All inputs are finite; a program needn't handle non-finite values.
Results may differ from a plain program's by a relative error of at most 0.00002.
Values sent between devices are 32-bit elements; how exact they have to be, the bound alone decides.
No kernel may reach another device: no remote copies, remote signals or barrier semaphores. Data moves between devices by JAX's collectives and lax.ppermute only.
A program may use at most 64 MiB of HBM per device.

v0:
```python
import math

import jax
import jax.numpy as jnp
from jax import lax
from jax.sharding import PartitionSpec as P

GRAVITY = 9.81
REFERENCE_DENSITY = 1026.0
TIME_STEP = 360.0
LATERAL = 300.0
VERTICAL = 0.001
ROTATION = 7.292e-05


def with_halo(array, sides, width, wrap):
    for axis, dim in sides:
        peers, length = (lax.axis_size(axis), array.shape[dim])
        up = [(i, (i + 1) % peers) for i in range(peers if wrap else peers - 1)]
        down = [(j, i) for i, j in up]
        last = lax.slice_in_dim(array, length - width, length, axis=dim)
        initial = lax.slice_in_dim(array, 0, width, axis=dim)
        before = lax.ppermute(last, axis, up)
        after = lax.ppermute(initial, axis, down)
        array = jnp.concatenate([before, array, after], axis=dim)
    return array


def partner_2(array, axis, stride):
    return lax.ppermute(array, axis, [(i, i ^ 1 << stride) for i in range(lax.axis_size(axis))])


def tier_dimensions(tier_pile):
    index = jnp.arange(tier_pile).astype(jnp.float32)
    tier_depth_extent = 6.0 + 4.0 * index
    depths = 2.0 * index * index + 6.0 * index + 3.0
    spacing = 4.0 * index + 4.0
    return (tier_depth_extent, depths, spacing)


def sea_density(heat, salt, depths):
    anom_t = heat - 10.0
    anom_s = salt - 35.0
    first = -0.1655 * (1.0 + 0.5 * 0.05952 * anom_t + 0.0001497 * depths) * anom_t
    second = 0.76554 * (1.0 - 0.5 * 0.00054914 * anom_s - 1.109e-05 * depths) * anom_s
    return first + second - 0.0024341 * anom_t * anom_s


def edge_amounts(
    potential_warmth_degrees,
    dissolved_salt_content,
    zonal_edge_current,
    meridional_edge_current,
    zonal_edge_amount,
    meridional_edge_amount,
    zonal_grid_spacing,
    meridional_grid_spacing,
):
    tier_depth_extent = tier_dimensions(potential_warmth_degrees.shape[0])[0][:, None, None]
    zonal_water_flux = (
        meridional_grid_spacing * tier_depth_extent * zonal_edge_current * zonal_edge_amount
    )
    meridional_water_flux = (
        zonal_grid_spacing * tier_depth_extent * meridional_edge_current * meridional_edge_amount
    )
    zonal_diffusive_coefficient = (
        LATERAL
        * meridional_grid_spacing
        * tier_depth_extent
        / zonal_grid_spacing
        * zonal_edge_amount
    )
    meridional_diffusive_coefficient = (
        LATERAL
        * zonal_grid_spacing
        * tier_depth_extent
        / meridional_grid_spacing
        * meridional_edge_amount
    )
    return jnp.concatenate(
        [
            potential_warmth_degrees,
            dissolved_salt_content,
            zonal_water_flux,
            meridional_water_flux,
            zonal_diffusive_coefficient,
            meridional_diffusive_coefficient,
        ],
        axis=0,
    )


def fold_signs(tier_pile):
    base = jnp.array([1.0, 1.0, -1.0, -1.0, 1.0, 1.0], dtype=jnp.float32)
    return jnp.repeat(base, tier_pile)


def centre(field):
    return field[:, 1:-1, 1:-1]


def to_east(field):
    return field[:, 1:-1, 2:]


def to_west(field):
    return field[:, 1:-1, :-2]


def to_north(field):
    return field[:, 2:, 1:-1]


def to_south(field):
    return field[:, :-2, 1:-1]


def south_east(field):
    return field[:, :-2, 2:]


def north_west(field):
    return field[:, 2:, :-2]


def advance(
    extended,
    zonal_edge_current,
    meridional_edge_current,
    sea_cells,
    zonal_edge_amount,
    meridional_edge_amount,
    bottom_tier_count,
    zonal_grid_spacing,
    meridional_grid_spacing,
    coriolis,
):
    tier_pile = zonal_edge_current.shape[0]
    tier_depth_extent, depths, spacing = tier_dimensions(tier_pile)
    thick_col = tier_depth_extent[:, None, None]
    spacing_col = spacing[1:, None, None]
    heat_ext, salt_ext, utr_ext, vtr_ext, gx_ext, gy_ext = [extended[number] for number in range(6)]
    density = sea_density(heat_ext, salt_ext, depths[:, None, None])
    weighted = density * thick_col
    pressure = GRAVITY / REFERENCE_DENSITY * (jnp.cumsum(weighted, axis=0) - 0.5 * weighted)
    press_x = -(to_east(pressure) - centre(pressure)) / zonal_grid_spacing
    press_y = -(to_north(pressure) - centre(pressure)) / meridional_grid_spacing
    east_tr = centre(utr_ext)
    north_tr = centre(vtr_ext)
    converge = east_tr - to_west(utr_ext) + north_tr - to_south(vtr_ext)
    upward = -jnp.cumsum(converge[::-1], axis=0)[::-1]
    cell_area = zonal_grid_spacing * meridional_grid_spacing
    level_index = jnp.arange(tier_pile)
    wet_face = (level_index[:, None, None] < bottom_tier_count[None]).astype(jnp.float32)
    no_flux = jnp.zeros_like(upward[:1])

    def tracer(field_ext):
        field = centre(field_ext)
        flux_east = east_tr * (field + to_east(field_ext)) * 0.5 - centre(gx_ext) * (
            to_east(field_ext) - field
        )
        flux_west = to_west(utr_ext) * (to_west(field_ext) + field) * 0.5 - to_west(gx_ext) * (
            field - to_west(field_ext)
        )
        flux_north = north_tr * (field + to_north(field_ext)) * 0.5 - centre(gy_ext) * (
            to_north(field_ext) - field
        )
        flux_south = to_south(vtr_ext) * (to_south(field_ext) + field) * 0.5 - to_south(gy_ext) * (
            field - to_south(field_ext)
        )
        interior = (
            upward[1:] * (field[:-1] + field[1:]) * 0.5
            - VERTICAL * cell_area * (field[:-1] - field[1:]) / spacing_col * wet_face[1:]
        )
        vertical = jnp.concatenate([upward[:1] * field[:1], interior, no_flux], axis=0)
        net_flux = flux_east - flux_west + flux_north - flux_south + vertical[:-1] - vertical[1:]
        return (field - TIME_STEP * net_flux / (cell_area * thick_col)) * sea_cells

    def viscous(velocity, face):
        interior = VERTICAL * (velocity[:-1] - velocity[1:]) / spacing_col * face[:-1] * face[1:]
        stress = jnp.concatenate([no_flux, interior, no_flux], axis=0)
        return (stress[:-1] - stress[1:]) / thick_col

    coriolis_col = coriolis[:, None]
    cor_u = (
        coriolis_col
        * (north_tr + to_east(vtr_ext) + to_south(vtr_ext) + south_east(vtr_ext))
        / (4.0 * zonal_grid_spacing * thick_col)
    )
    cor_v = (
        -coriolis_col
        * (east_tr + to_west(utr_ext) + to_north(utr_ext) + north_west(utr_ext))
        / (4.0 * meridional_grid_spacing * thick_col)
    )
    zonal_after = (
        zonal_edge_current
        + TIME_STEP * (press_x + cor_u + viscous(zonal_edge_current, zonal_edge_amount))
    ) * zonal_edge_amount
    meridional_after = (
        meridional_edge_current
        + TIME_STEP * (press_y + cor_v + viscous(meridional_edge_current, meridional_edge_amount))
    ) * meridional_edge_amount
    return (tracer(heat_ext), tracer(salt_ext), zonal_after, meridional_after)


def coriolis_rows(first_row, meridional_lines, total_rows):
    global_row = first_row + jnp.arange(meridional_lines).astype(jnp.float32)
    latitude = 10.0 + 78.0 * (global_row + 0.5) / total_rows
    return 2.0 * ROTATION * jnp.sin(latitude * (math.pi / 180.0))


def along_lon(piled_tiers):
    return with_halo(piled_tiers, (("lon", 2),), 1, True)


def along_lat(piled_tiers):
    return with_halo(piled_tiers, (("lat", 1),), 1, False)


def mirrored_row(top_row):
    partner = top_row
    for bit_number in range(lax.axis_size("lon").bit_length() - 1):
        partner = partner_2(partner, "lon", bit_number)
    return partner[:, ::-1]


def with_fold(extended, signs):
    mirror = mirrored_row(extended[:, -2, :]) * signs[:, None]
    top_device = lax.axis_index("lat") == lax.axis_size("lat") - 1
    last_row = jnp.where(top_device, mirror, extended[:, -1, :])
    return jnp.concatenate([extended[:, :-1, :], last_row[:, None, :]], axis=1)


def per_device(
    potential_warmth_degrees,
    dissolved_salt_content,
    zonal_edge_current,
    meridional_edge_current,
    wet_grid_flag,
    zonal_wet_edge_flag,
    meridional_wet_edge_flag,
    bottom_tier_count,
    zonal_grid_spacing,
    meridional_grid_spacing,
):
    tier_pile = potential_warmth_degrees.shape[0]
    meridional_lines = potential_warmth_degrees.shape[1]
    sea_cells = wet_grid_flag.astype(jnp.float32)
    zonal_edge_amount = zonal_wet_edge_flag.astype(jnp.float32)
    meridional_edge_amount = meridional_wet_edge_flag.astype(jnp.float32)
    piled_tiers = edge_amounts(
        potential_warmth_degrees,
        dissolved_salt_content,
        zonal_edge_current,
        meridional_edge_current,
        zonal_edge_amount,
        meridional_edge_amount,
        zonal_grid_spacing,
        meridional_grid_spacing,
    )
    signs = fold_signs(tier_pile)
    extended = with_fold(along_lat(along_lon(piled_tiers)), signs)
    extended = extended.reshape(6, tier_pile, extended.shape[1], extended.shape[2])
    first_row = (lax.axis_index("lat") * meridional_lines).astype(jnp.float32)
    coriolis = coriolis_rows(
        first_row, meridional_lines, meridional_lines * lax.axis_size("lat") * 1.0
    )
    return advance(
        extended,
        zonal_edge_current,
        meridional_edge_current,
        sea_cells,
        zonal_edge_amount,
        meridional_edge_amount,
        bottom_tier_count,
        zonal_grid_spacing,
        meridional_grid_spacing,
        coriolis,
    )


def solution(mesh):
    placed = (
        P(None, "lat", "lon"),
        P(None, "lat", "lon"),
        P(None, "lat", "lon"),
        P(None, "lat", "lon"),
        P(None, "lat", "lon"),
        P(None, "lat", "lon"),
        P(None, "lat", "lon"),
        P("lat", "lon"),
        P("lat", "lon"),
        P("lat", "lon"),
    )
    return jax.shard_map(
        per_device,
        mesh=mesh,
        in_specs=placed,
        out_specs=(
            P(None, "lat", "lon"),
            P(None, "lat", "lon"),
            P(None, "lat", "lon"),
            P(None, "lat", "lon"),
        ),
        check_vma=False,
    )
```

profile of v0, /device:TPU:6, one launch (start us, length us, event | category | flops | bytes accessed | tf_op | source)
XLA Modules:
  0.0 122.1 jit_solution(2526715707889872417)
XLA Ops:
  0.7 2.1 %fusion.56 = (f32[8,96,128]{2,0,1:T(8,128)}, f32[48,96,128]{2,0,1:T(8,128)S(1)}) fusion(f32[8,96,128]{2,1,0:T(8,128)} %param.11), kind=kLoop, calls=%fused_computation.123 | loop fusion | bytes 1179648 | tf_op args[0]
  2.8 2.0 %fusion.55 = (f32[8,96,128]{2,0,1:T(8,128)}, f32[48,96,128]{2,0,1:T(8,128)S(1)}) fusion(f32[8,96,128]{2,1,0:T(8,128)} %param.12, f32[48,96,128]{2,0,1:T(8,128)S(1)} %get-tuple-element.32), kind=kLoop, calls=%fused_computation.122 | loop fusion | bytes 1179648 | tf_op args[1]
  4.8 0.7 broadcast_multiply_fusion
  5.5 1.2 constant_dynamic-update-slice_fusion.3
  6.7 1.3 %constant_dynamic-update-slice_fusion.2 = (f32[48,96,128]{2,0,1:T(8,128)S(1)}, f32[8,96,128]{2,0,1:T(8,128)}, f32[8,96,128]{2,0,1:T(8,128)}) fusion(f32[48,96,128]{2,0,1:T(8,128)S(1)} %get-tuple-element.18, s32[8,96,128]{2,1,0:T(8,128)S(1)} %copy-done.4, f32[8,96,128]{2,1,0:T(8,128)S(1)} %copy-done.24, f32[8]{0:T(128)S(1)} %fusion.52, ...), kind=kLoop, calls=%fused_computation.109 | loop fusion | flops 393216 | bytes 2015744
  8.6 2.9 %fusion.54 = (f32[48,96,1]{2,0,1:T(8,128)}, f32[48,96,1]{2,0,1:T(8,128)}) fusion(f32[48,96,128]{2,0,1:T(8,128)S(1)} %constant_dynamic-update-slice_fusion), kind=kLoop, calls=%fused_computation.121 | loop fusion | bytes 73728 | tf_op jit(solution)/shard_map/slice | solution.py:21
  11.5 3.1 %copy.70 = f32[48,96,1]{1,0,2:T(8,128)} copy(f32[48,96,1]{2,0,1:T(8,128)} %get-tuple-element.22) | data formatting | bytes 36864 | tf_op jit(solution)/shard_map/slice | solution.py:21
  14.6 1.9 %collective-permute-start.1 = (f32[48,96,1]{1,0,2:T(8,128)}, f32[48,96,1]{1,0,2:T(8,128)}, u32[]{:S(2)}, u32[]{:S(2)}) collective-permute-start(f32[48,96,1]{1,0,2:T(8,128)} %copy.70), channel_id=1, source_target_pairs={{0,16},{16,32},{32,48},{48,64},{64,80},{80,96},{96,112},{112,128},... | collective-permute-start | bytes 55304 | tf_op jit(solution)/shard_map/ppermute | solution.py:23
  16.5 3.1 %copy.66 = f32[48,96,1]{1,0,2:T(8,128)} copy(f32[48,96,1]{2,0,1:T(8,128)} %get-tuple-element.23) | data formatting | bytes 36864 | tf_op jit(solution)/shard_map/slice | solution.py:22
  19.6 13.2 %collective-permute-start = (f32[48,96,1]{1,0,2:T(8,128)}, f32[48,96,1]{1,0,2:T(8,128)}, u32[]{:S(2)}, u32[]{:S(2)}) collective-permute-start(f32[48,96,1]{1,0,2:T(8,128)} %copy.66), channel_id=1, source_target_pairs={{16,0},{32,16},{48,32},{64,48},{80,64},{96,80},{112,96},{128,112},... | collective-permute-start | bytes 55304 | tf_op jit(solution)/shard_map/ppermute | solution.py:24
  32.9 1.0 copy_convert_fusion.2
  34.0 3.0 %copy.71 = f32[48,96,1]{2,0,1:T(8,128)} copy(f32[48,96,1]{1,0,2:T(8,128)} %collective-permute-done.1) | data formatting | bytes 36864 | tf_op jit(solution)/shard_map/ppermute | solution.py:23
  37.0 3.1 %copy.67 = f32[48,96,1]{2,0,1:T(8,128)} copy(f32[48,96,1]{1,0,2:T(8,128)} %collective-permute-done) | data formatting | bytes 36864 | tf_op jit(solution)/shard_map/ppermute | solution.py:24
  40.1 1.6 %pad_maximum_fusion.23 = (f32[48,1,130]{2,0,1:T(8,128)}, f32[48,1,130]{2,0,1:T(8,128)S(1)}) fusion(f32[48,96,1]{2,0,1:T(8,128)} %copy.67, f32[48,96,128]{2,0,1:T(8,128)S(1)} %constant_dynamic-update-slice_fusion, f32[48,96,1]{2,0,1:T(8,128)} %copy.71), kind=kLoop, calls=%fused_computation.95 | loop fusion | flops 24960 | bytes 2446080 | tf_op jit(solution)/shard_map/concatenate | solution.py:25
  41.6 1.9 %collective-permute-start.2 = (f32[48,130]{1,0:T(8,128)S(1)}, f32[48,130]{1,0:T(8,128)S(1)}, u32[]{:S(2)}, u32[]{:S(2)}) collective-permute-start(f32[48,130]{1,0:T(8,128)S(1)} %bitcast.12), channel_id=1, source_target_pairs={{0,16},{16,0},{32,48},{48,32},{64,80},{80,64},{96,112},{112,96},{1... | collective-permute-start | bytes 74888 | tf_op jit(solution)/shard_map/ppermute | solution.py:30
  43.6 0.9 slice_multiply_fusion.2
  44.7 1.9 %collective-permute-start.3 = (f32[48,130]{1,0:T(8,128)S(1)}, f32[48,130]{1,0:T(8,128)}, u32[]{:S(2)}, u32[]{:S(2)}) collective-permute-start(f32[48,130]{1,0:T(8,128)S(1)} %collective-permute-done.2), channel_id=1, source_target_pairs={{0,32},{16,48},{32,0},{48,16},{64,96},{80,112},{96,64},{112,80},{1... | collective-permute-start | bytes 74888 | tf_op jit(solution)/shard_map/ppermute | solution.py:30
  46.7 1.0 copy_convert_fusion.1
  47.7 3.2 %collective-permute-done.3 = f32[48,130]{1,0:T(8,128)} collective-permute-done((f32[48,130]{1,0:T(8,128)S(1)}, f32[48,130]{1,0:T(8,128)}, u32[]{:S(2)}, u32[]{:S(2)}) %collective-permute-start.3) | collective-permute-done | bytes 24992 | tf_op jit(solution)/shard_map/ppermute | solution.py:30
  50.8 1.9 %collective-permute-start.4 = (f32[48,130]{1,0:T(8,128)}, f32[48,130]{1,0:T(8,128)}, u32[]{:S(2)}, u32[]{:S(2)}) collective-permute-start(f32[48,130]{1,0:T(8,128)} %collective-permute-done.3), channel_id=1, source_target_pairs={{0,64},{16,80},{32,96},{48,112},{64,0},{80,16},{96,32},{112,48},{1... | collective-permute-start | bytes 74888 | tf_op jit(solution)/shard_map/ppermute | solution.py:30
  53.3 4.7 %collective-permute-done.4 = f32[48,130]{1,0:T(8,128)} collective-permute-done((f32[48,130]{1,0:T(8,128)}, f32[48,130]{1,0:T(8,128)}, u32[]{:S(2)}, u32[]{:S(2)}) %collective-permute-start.4) | collective-permute-done | bytes 24992 | tf_op jit(solution)/shard_map/ppermute | solution.py:30
  58.0 7.1 %collective-permute-start.5 = (f32[48,130]{1,0:T(8,128)}, f32[48,130]{1,0:T(8,128)}, u32[]{:S(2)}, u32[]{:S(2)}) collective-permute-start(f32[48,130]{1,0:T(8,128)} %collective-permute-done.4), channel_id=1, source_target_pairs={{0,128},{16,144},{32,160},{48,176},{64,192},{80,208},{96,224},{112... | collective-permute-start | bytes 74888 | tf_op jit(solution)/shard_map/ppermute | solution.py:30
  65.8 5.2 %collective-permute-start.7 = (f32[48,1,130]{2,0,1:T(8,128)}, f32[48,1,130]{2,0,1:T(8,128)}, u32[]{:S(2)}, u32[]{:S(2)}) collective-permute-start(f32[48,1,130]{2,0,1:T(8,128)} %get-tuple-element.20), channel_id=1, source_target_pairs={{1,0},{2,1},{3,2},{4,3},{5,4},{6,5},{7,6},{8,7},{9,8},{10,9},{11,1... | collective-permute-start | bytes 74888 | tf_op jit(solution)/shard_map/ppermute | solution.py:24
  71.0 5.1 %collective-permute-start.6 = (f32[48,130]{1,0:T(8,128)}, f32[48,130]{1,0:T(8,128)}, u32[]{:S(2)}, u32[]{:S(2)}) collective-permute-start(f32[48,130]{1,0:T(8,128)} %collective-permute-done.5), channel_id=1, source_target_pairs={{0,256},{16,272},{32,288},{48,304},{64,320},{80,336},{96,352},{112... | collective-permute-start | bytes 74888 | tf_op jit(solution)/shard_map/ppermute | solution.py:30
  76.6 0.7 broadcast_in_dim.4
  78.0 3.3 %collective-permute-start.8 = (f32[48,1,130]{2,0,1:T(8,128)}, f32[48,1,130]{2,0,1:T(8,128)}, u32[]{:S(2)}, u32[]{:S(2)}) collective-permute-start(f32[48,1,130]{2,0,1:T(8,128)} %copy-done.35), channel_id=1, source_target_pairs={{0,1},{1,2},{2,3},{3,4},{4,5},{5,6},{6,7},{7,8},{8,9},{9,10},{10,1... | collective-permute-start | bytes 74888 | tf_op jit(solution)/shard_map/ppermute | solution.py:23
  81.3 1.5 %reverse = f32[48,256]{1,0:T(8,128)} reverse(f32[48,256]{1,0:T(8,128)} %bitcast.9), dimensions={1} | reverse | bytes 98304
  82.8 0.9 fusion.50
  83.8 3.2 %collective-permute-done.8 = f32[48,1,130]{2,0,1:T(8,128)} collective-permute-done((f32[48,1,130]{2,0,1:T(8,128)}, f32[48,1,130]{2,0,1:T(8,128)}, u32[]{:S(2)}, u32[]{:S(2)}) %collective-permute-start.8) | collective-permute-done | bytes 24992 | tf_op jit(solution)/shard_map/ppermute | solution.py:23
  87.0 3.1 %subtract_multiply_fusion.1 = f32[8,98,130]{2,0,1:T(8,128)} fusion(f32[48,1,130]{2,0,1:T(8,128)S(1)} %fusion.50, f32[48,96,1]{2,0,1:T(8,128)} %copy.67, f32[48,96,128]{2,0,1:T(8,128)S(1)} %constant_dynamic-update-slice_fusion, f32[48,96,1]{2,0,1:T(8,128)} %copy.71, f32[48,1,130]{2,0,1:T(8,128)} %collective-permute-done.8, f32[8]{0:T(128)S(1)} %fusion.52, ...), kind=kLoop, calls=%fused_computation.7 | loop fusion | flops 2548000 | bytes 2853856 | tf_op jit(solution)/shard_map/mul | solution.py:144
  90.0 2.7 %reduce_window_sum.23 = f32[8,98,130]{2,0,1:T(8,128)} reduce-window(f32[8,98,130]{2,0,1:T(8,128)} %subtract_multiply_fusion.1, f32[]{:T(128)} %constant.34.clone.1), window={size=8x1x1 pad=7_0x0_0x0_0}, to_apply=%region_1.2 | reduce-window | flops 713440 | bytes 815364 | tf_op jit(solution)/shard_map/jit(cumsum)/reduce_window_sum | solution.py:145
  92.8 2.6 %subtract_multiply_fusion = f32[8,98,130]{2,0,1:T(8,128)S(1)} fusion(f32[8,98,130]{2,0,1:T(8,128)} %reduce_window_sum.23, f32[8]{0:T(128)S(1)} %fusion.52, f32[8]{0:T(128)S(1)} %get-tuple-element.41, f32[48,1,130]{2,0,1:T(8,128)} %copy-done.16, f32[48,96,1]{2,0,1:T(8,128)} %copy.67, f32[48,96,128]{2,0,1:T(8,128)S(1)} %constant_dynamic-update-slice_fusion, ...), kind=kLoop, calls=%fused_computation.6 | loop fusion | flops 2853760 | bytes 3261536 | tf_op jit(solution)/shard_map/mul | solution.py:145
  96.1 2.5 %fusion.26 = (f32[8,96,128]{2,0,1:T(8,128)}, f32[8,96,128]{2,0,1:T(8,128)S(1)}) fusion(f32[48,1,130]{2,0,1:T(8,128)} %collective-permute-done.8, f32[48,96,1]{2,0,1:T(8,128)S(1)} %copy-done.2, f32[48,96,128]{2,0,1:T(8,128)S(1)} %constant_dynamic-update-slice_fusion, f32[48,96,1]{2,0,1:T(8,128)S(1)} %copy-done, f32[8,96,128]{2,0,1:T(8,128)S(1)} %copy-done.6, ...), kind=kLoop, calls=%fused_computation.47 | loop fusion | flops 2359296 | bytes 5616416 | tf_op jit(solution)/shard_map/mul | solution.py:195
  98.6 0.7 copy-done.10
  99.4 1.7 %fusion.36 = f32[8,96,128]{2,0,1:T(8,128)} fusion(f32[48,1,130]{2,0,1:T(8,128)} %collective-permute-done.8, f32[8,96,128]{2,0,1:T(8,128)S(1)} %get-tuple-element.13, f32[8,96,128]{2,0,1:T(8,128)S(1)} %copy-done.6, f32[8,96,128]{2,0,1:T(8,128)S(1)} %get-tuple-element.19, f32[48,96,128]{2,0,1:T(8,128)S(1)} %constant_dynamic-update-slice_fusion, ...), kind=kLoop, calls=%fused_computation.69 | loop fusion | flops 688128 | bytes 3975552 | tf_op jit(solution)/shard_map/sub | solution.py:150
  101.0 1.8 %rev.10 = f32[8,96,128]{2,0,1:T(8,128)} reverse(f32[8,96,128]{2,0,1:T(8,128)} %fusion.36), dimensions={0} | reverse | bytes 786432 | tf_op jit(solution)/shard_map/rev | solution.py:151
  102.8 2.1 %reduce_window_sum.22 = f32[8,96,128]{2,0,1:T(8,128)} reduce-window(f32[8,96,128]{2,0,1:T(8,128)} %rev.10, f32[]{:T(128)} %constant.34.clone.1), window={size=8x1x1 pad=7_0x0_0x0_0}, to_apply=%region_0.1 | reduce-window | flops 688128 | bytes 786436 | tf_op jit(solution)/shard_map/jit(cumsum)/reduce_window_sum | solution.py:151
  104.9 1.8 %rev.11 = f32[8,96,128]{2,0,1:T(8,128)} reverse(f32[8,96,128]{2,0,1:T(8,128)} %reduce_window_sum.22), dimensions={0} | reverse | bytes 786432 | tf_op jit(solution)/shard_map/rev | solution.py:151
  106.7 1.1 neg.18
  107.9 2.5 %fusion.33 = (f32[7,96,128]{2,0,1:T(8,128)S(1)}, f32[7,96,128]{2,0,1:T(8,128)S(1)}, f32[7,96,128]{2,0,1:T(8,128)S(1)}) fusion(f32[8,96,128]{2,0,1:T(8,128)} %get-tuple-element.29, f32[8,96,128]{2,0,1:T(8,128)S(1)} %neg.18, s32[96,128]{1,0:T(8,128)} %param.18, f32[7]{0:T(128)S(1)} %slice.300, f32[96,128]{1,0:T(8,128)} %get-tuple-element.36, ...), kind=kLoop, calls=%fused_computation.63 | loop fusion | flops 1978368 | bytes 4227100 | tf_op jit(solution)/shard_map/sub | solution.py:172
  110.5 0.7 copy-done.3
  111.3 1.9 %fusion.14 = f32[8,96,128]{2,0,1:T(8,128)S(1)} fusion(f32[48,1,130]{2,0,1:T(8,128)S(1)} %copy-done.17, f32[48,96,1]{2,0,1:T(8,128)S(1)} %copy-done.3, f32[48,96,128]{2,0,1:T(8,128)S(1)} %constant_dynamic-update-slice_fusion, f32[48,96,1]{2,0,1:T(8,128)S(1)} %copy-done.1, f32[8,98,130]{2,0,1:T(8,128)S(1)} %copy-done.9, ...), kind=kLoop, calls=%fused_computation.27 | loop fusion | flops 2359296 | bytes 5223200 | tf_op jit(solution)/shard_map/mul | solution.py:199
  113.3 0.8 copy.106
  114.3 2.6 %fusion.4 = f32[8,96,128]{2,0,1:T(8,128)S(1)} fusion(f32[8,96,128]{2,0,1:T(8,128)S(1)} %copy-done.11, f32[48,1,130]{2,0,1:T(8,128)} %collective-permute-done.8, f32[7,96,128]{2,0,1:T(8,128)S(1)} %get-tuple-element.24, f32[1,96,128]{2,0,1:T(1,128)S(1)} %get-tuple-element.27, f32[48,96,1]{2,0,1:T(8,128)S(1)} %copy-done.3, ...), kind=kLoop, calls=%fused_computation.13 | loop fusion | flops 5898240 | bytes 6230816 | tf_op jit(solution)/shard_map/mul | solution.py:177
  116.9 0.8 copy.104
  117.8 2.7 %fusion.2 = f32[8,96,128]{2,0,1:T(8,128)S(1)} fusion(f32[8,96,128]{2,0,1:T(8,128)S(1)} %copy-done.11, f32[48,1,130]{2,0,1:T(8,128)} %collective-permute-done.8, f32[7,96,128]{2,0,1:T(8,128)S(1)} %get-tuple-element.25, f32[1,96,128]{2,0,1:T(1,128)S(1)} %get-tuple-element.28, f32[48,96,1]{2,0,1:T(8,128)S(1)} %copy-done.3, ...), kind=kLoop, calls=%fused_computation.11 | loop fusion | flops 5898240 | bytes 6230816 | tf_op jit(solution)/shard_map/mul | solution.py:177
  120.4 0.8 copy.103
  121.3 0.8 copy.105
  (96 shorter events, 4.5 us)
Async XLA Ops:
  0.6 4.1 %copy-start.18 = (f32[96,128]{1,0:T(8,128)S(1)}, f32[96,128]{1,0:T(8,128)}, u32[]{:S(2)}) copy-start(f32[96,128]{1,0:T(8,128)} %param.20) | copy-start | bytes 147460
  0.6 4.1 %copy-start.20 = (f32[96,128]{1,0:T(8,128)S(1)}, f32[96,128]{1,0:T(8,128)}, u32[]{:S(2)}) copy-start(f32[96,128]{1,0:T(8,128)} %param.19) | copy-start | bytes 147460
  0.7 4.9 %copy-start.26 = (f32[8,96,128]{2,1,0:T(8,128)S(1)}, f32[8,96,128]{2,1,0:T(8,128)}, u32[]{:S(2)}) copy-start(f32[8,96,128]{2,1,0:T(8,128)} %param.13) | copy-start | bytes 1179652
  0.7 4.8 %copy-start.5 = (s32[8,96,128]{2,1,0:T(8,128)S(1)}, s32[8,96,128]{2,1,0:T(8,128)}, u32[]{:S(2)}) copy-start(s32[8,96,128]{2,1,0:T(8,128)} %param.16) | copy-start | bytes 1179652
  0.7 6.0 %copy-start.4 = (s32[8,96,128]{2,1,0:T(8,128)S(1)}, s32[8,96,128]{2,1,0:T(8,128)}, u32[]{:S(2)}) copy-start(s32[8,96,128]{2,1,0:T(8,128)} %param.17) | copy-start | bytes 1179652
  0.7 6.0 %copy-start.24 = (f32[8,96,128]{2,1,0:T(8,128)S(1)}, f32[8,96,128]{2,1,0:T(8,128)}, u32[]{:S(2)}) copy-start(f32[8,96,128]{2,1,0:T(8,128)} %param.14) | copy-start | bytes 1179652
  5.5 2.8 %copy-start.29 = (f32[96,128]{1,0:T(8,128)}, f32[96,128]{1,0:T(8,128)S(1)}, u32[]{:S(2)}) copy-start(f32[96,128]{1,0:T(8,128)S(1)} %get-tuple-element.35) | copy-start | bytes 147460
  5.5 2.9 %copy-start.31 = (f32[96,128]{1,0:T(8,128)}, f32[96,128]{1,0:T(8,128)S(1)}, u32[]{:S(2)}) copy-start(f32[96,128]{1,0:T(8,128)S(1)} %get-tuple-element.38) | copy-start | bytes 147460
  14.6 19.4 %collective-permute-start.1 = (f32[48,96,1]{1,0,2:T(8,128)}, f32[48,96,1]{1,0,2:T(8,128)}, u32[]{:S(2)}, u32[]{:S(2)}) collective-permute-start(f32[48,96,1]{1,0,2:T(8,128)} %copy.70), channel_id=1, source_target_pairs={{0,16},{16,32},{32,48},{48,64},{64,80},{80,96},{96,112},{112,128},... | collective-permute-start | bytes 55304 | tf_op jit(solution)/shard_map/ppermute | solution.py:23
  19.6 17.3 %collective-permute-start = (f32[48,96,1]{1,0,2:T(8,128)}, f32[48,96,1]{1,0,2:T(8,128)}, u32[]{:S(2)}, u32[]{:S(2)}) collective-permute-start(f32[48,96,1]{1,0,2:T(8,128)} %copy.66), channel_id=1, source_target_pairs={{16,0},{32,16},{48,32},{64,48},{80,64},{96,80},{112,96},{128,112},... | collective-permute-start | bytes 55304 | tf_op jit(solution)/shard_map/ppermute | solution.py:24
  40.1 3.5 %copy-start.12 = (f32[8,96,128]{2,0,1:T(8,128)S(1)}, f32[8,96,128]{2,0,1:T(8,128)}, u32[]{:S(2)}) copy-start(f32[8,96,128]{2,0,1:T(8,128)} %get-tuple-element.33) | copy-start | bytes 1179652
  40.1 3.5 %copy-start.13 = (f32[8,96,128]{2,0,1:T(8,128)S(1)}, f32[8,96,128]{2,0,1:T(8,128)}, u32[]{:S(2)}) copy-start(f32[8,96,128]{2,0,1:T(8,128)} %copy_convert_fusion.2) | copy-start | bytes 1179652
  41.6 2.8 %copy-start.35 = (f32[48,1,130]{2,0,1:T(8,128)}, f32[48,1,130]{2,0,1:T(8,128)S(1)}, u32[]{:S(2)}) copy-start(f32[48,1,130]{2,0,1:T(8,128)S(1)} %get-tuple-element.21) | copy-start | bytes 74884
  41.6 3.1 %collective-permute-start.2 = (f32[48,130]{1,0:T(8,128)S(1)}, f32[48,130]{1,0:T(8,128)S(1)}, u32[]{:S(2)}, u32[]{:S(2)}) collective-permute-start(f32[48,130]{1,0:T(8,128)S(1)} %bitcast.12), channel_id=1, source_target_pairs={{0,16},{16,0},{32,48},{48,32},{64,80},{80,64},{96,112},{112,96},{1... | collective-permute-start | bytes 74888 | tf_op jit(solution)/shard_map/ppermute | solution.py:30
  44.7 6.1 %collective-permute-start.3 = (f32[48,130]{1,0:T(8,128)S(1)}, f32[48,130]{1,0:T(8,128)}, u32[]{:S(2)}, u32[]{:S(2)}) collective-permute-start(f32[48,130]{1,0:T(8,128)S(1)} %collective-permute-done.2), channel_id=1, source_target_pairs={{0,32},{16,48},{32,0},{48,16},{64,96},{80,112},{96,64},{112,80},{1... | collective-permute-start | bytes 74888 | tf_op jit(solution)/shard_map/ppermute | solution.py:30
  50.8 7.2 %collective-permute-start.4 = (f32[48,130]{1,0:T(8,128)}, f32[48,130]{1,0:T(8,128)}, u32[]{:S(2)}, u32[]{:S(2)}) collective-permute-start(f32[48,130]{1,0:T(8,128)} %collective-permute-done.3), channel_id=1, source_target_pairs={{0,64},{16,80},{32,96},{48,112},{64,0},{80,16},{96,32},{112,48},{1... | collective-permute-start | bytes 74888 | tf_op jit(solution)/shard_map/ppermute | solution.py:30
  58.0 12.9 %collective-permute-start.5 = (f32[48,130]{1,0:T(8,128)}, f32[48,130]{1,0:T(8,128)}, u32[]{:S(2)}, u32[]{:S(2)}) collective-permute-start(f32[48,130]{1,0:T(8,128)} %collective-permute-done.4), channel_id=1, source_target_pairs={{0,128},{16,144},{32,160},{48,176},{64,192},{80,208},{96,224},{112... | collective-permute-start | bytes 74888 | tf_op jit(solution)/shard_map/ppermute | solution.py:30
  65.8 17.1 %collective-permute-start.7 = (f32[48,1,130]{2,0,1:T(8,128)}, f32[48,1,130]{2,0,1:T(8,128)}, u32[]{:S(2)}, u32[]{:S(2)}) collective-permute-start(f32[48,1,130]{2,0,1:T(8,128)} %get-tuple-element.20), channel_id=1, source_target_pairs={{1,0},{2,1},{3,2},{4,3},{5,4},{6,5},{7,6},{8,7},{9,8},{10,9},{11,1... | collective-permute-start | bytes 74888 | tf_op jit(solution)/shard_map/ppermute | solution.py:24
  71.0 10.3 %collective-permute-start.6 = (f32[48,130]{1,0:T(8,128)}, f32[48,130]{1,0:T(8,128)}, u32[]{:S(2)}, u32[]{:S(2)}) collective-permute-start(f32[48,130]{1,0:T(8,128)} %collective-permute-done.5), channel_id=1, source_target_pairs={{0,256},{16,272},{32,288},{48,304},{64,320},{80,336},{96,352},{112... | collective-permute-start | bytes 74888 | tf_op jit(solution)/shard_map/ppermute | solution.py:30
  78.0 9.0 %collective-permute-start.8 = (f32[48,1,130]{2,0,1:T(8,128)}, f32[48,1,130]{2,0,1:T(8,128)}, u32[]{:S(2)}, u32[]{:S(2)}) collective-permute-start(f32[48,1,130]{2,0,1:T(8,128)} %copy-done.35), channel_id=1, source_target_pairs={{0,1},{1,2},{2,3},{3,4},{4,5},{5,6},{6,7},{7,8},{8,9},{9,10},{10,1... | collective-permute-start | bytes 74888 | tf_op jit(solution)/shard_map/ppermute | solution.py:23
  83.7 3.2 %copy-start.16 = (f32[48,1,130]{2,0,1:T(8,128)}, f32[48,1,130]{2,0,1:T(8,128)S(1)}, u32[]{:S(2)}) copy-start(f32[48,1,130]{2,0,1:T(8,128)S(1)} %fusion.50) | copy-start | bytes 74884
  87.0 5.7 %copy-start.36 = (f32[8]{0:T(128)S(1)}, f32[8]{0:T(128)}, u32[]{:S(2)}) copy-start(f32[8]{0:T(128)} %get-tuple-element.42) | copy-start | bytes 100
  92.7 3.1 %copy-start.2 = (f32[48,96,1]{2,0,1:T(8,128)S(1)}, f32[48,96,1]{2,0,1:T(8,128)}, u32[]{:S(2)}) copy-start(f32[48,96,1]{2,0,1:T(8,128)} %copy.67) | copy-start | bytes 55300
  92.7 3.2 %copy-start.6 = (f32[8,96,128]{2,0,1:T(8,128)S(1)}, f32[8,96,128]{2,0,1:T(8,128)}, u32[]{:S(2)}) copy-start(f32[8,96,128]{2,0,1:T(8,128)} %get-tuple-element.17) | copy-start | bytes 1179652
  92.7 3.2 %copy-start.21 = (f32[96,128]{1,0:T(8,128)S(1)}, f32[96,128]{1,0:T(8,128)}, u32[]{:S(2)}) copy-start(f32[96,128]{1,0:T(8,128)} %param.19) | copy-start | bytes 147460
  92.7 3.3 %copy-start.27 = (f32[8,96,128]{2,1,0:T(8,128)S(1)}, f32[8,96,128]{2,1,0:T(8,128)}, u32[]{:S(2)}) copy-start(f32[8,96,128]{2,1,0:T(8,128)} %param.13) | copy-start | bytes 1179652
  92.8 3.4 %copy-start.28 = (f32[7,96,128]{2,0,1:T(8,128)S(1)}, f32[7,96,128]{2,0,1:T(8,128)}, u32[]{:S(2)}) copy-start(f32[7,96,128]{2,0,1:T(8,128)} %slice_multiply_fusion.2) | copy-start | bytes 1032196
  92.8 3.4 %copy-start.34 = (f32[96,128]{1,0:T(8,128)S(1)}, f32[96,128]{1,0:T(8,128)}, u32[]{:S(2)}) copy-start(f32[96,128]{1,0:T(8,128)} %get-tuple-element.39) | copy-start | bytes 147460
  92.8 3.4 %copy-start.38 = (f32[96]{0:T(128)S(1)}, f32[96]{0:T(128)}, u32[]{:S(2)}) copy-start(f32[96]{0:T(128)} %sine_multiply_fusion) | copy-start | bytes 1156
  95.4 3.2 %copy-start.8 = (f32[8,98,130]{2,0,1:T(8,128)}, f32[8,98,130]{2,0,1:T(8,128)S(1)}, u32[]{:S(2)}) copy-start(f32[8,98,130]{2,0,1:T(8,128)S(1)} %subtract_multiply_fusion) | copy-start | bytes 1223044
  106.7 3.6 %copy-start.9 = (f32[8,98,130]{2,0,1:T(8,128)S(1)}, f32[8,98,130]{2,0,1:T(8,128)}, u32[]{:S(2)}) copy-start(f32[8,98,130]{2,0,1:T(8,128)} %copy-done.8) | copy-start | bytes 1223044
  107.8 2.7 %copy-start.1 = (f32[48,96,1]{2,0,1:T(8,128)S(1)}, f32[48,96,1]{2,0,1:T(8,128)}, u32[]{:S(2)}) copy-start(f32[48,96,1]{2,0,1:T(8,128)} %copy.71) | copy-start | bytes 55300
  107.8 3.4 %copy-start.3 = (f32[48,96,1]{2,0,1:T(8,128)S(1)}, f32[48,96,1]{2,0,1:T(8,128)}, u32[]{:S(2)}) copy-start(f32[48,96,1]{2,0,1:T(8,128)} %copy.67) | copy-start | bytes 55300
  107.8 3.4 %copy-start.17 = (f32[48,1,130]{2,0,1:T(8,128)S(1)}, f32[48,1,130]{2,0,1:T(8,128)}, u32[]{:S(2)}) copy-start(f32[48,1,130]{2,0,1:T(8,128)} %copy-done.16) | copy-start | bytes 74884
  107.9 3.4 %copy-start.37 = (f32[96]{0:T(128)S(1)}, f32[96]{0:T(128)}, u32[]{:S(2)}) copy-start(f32[96]{0:T(128)} %fusion.53) | copy-start | bytes 1156
  111.2 2.9 %slice-start = ((f32[8,96,128]{2,1,0:T(8,128)}), f32[1,96,128]{2,1,0:T(8,128)S(1)}, s32[]{:S(2)}) async-start(f32[8,96,128]{2,1,0:T(8,128)} %param.12), calls=%async_computation | async-start | bytes 98304 | tf_op jit(solution)/shard_map/slice | solution.py:175
  111.2 2.9 %slice-start.1 = ((f32[8,96,128]{2,1,0:T(8,128)}), f32[1,96,128]{2,1,0:T(8,128)S(1)}, s32[]{:S(2)}) async-start(f32[8,96,128]{2,1,0:T(8,128)} %param.11), calls=%async_computation.1 | async-start | bytes 98304 | tf_op jit(solution)/shard_map/slice | solution.py:175
  111.2 3.0 %copy-start.7 = (f32[8,96,128]{2,0,1:T(8,128)S(1)}, f32[8,96,128]{2,0,1:T(8,128)}, u32[]{:S(2)}) copy-start(f32[8,96,128]{2,0,1:T(8,128)} %get-tuple-element.17) | copy-start | bytes 1179652
  111.2 3.0 %copy-start.11 = (f32[8,96,128]{2,0,1:T(8,128)S(1)}, f32[8,96,128]{2,0,1:T(8,128)}, u32[]{:S(2)}) copy-start(f32[8,96,128]{2,0,1:T(8,128)} %copy-done.10) | copy-start | bytes 1179652
  111.3 3.0 %copy-start.14 = (f32[8,96,128]{2,1,0:T(8,128)S(1)}, f32[8,96,128]{2,1,0:T(8,128)}, u32[]{:S(2)}) copy-start(f32[8,96,128]{2,1,0:T(8,128)} %param.12) | copy-start | bytes 1179652
  111.3 3.0 %copy-start.19 = (f32[96,128]{1,0:T(8,128)S(1)}, f32[96,128]{1,0:T(8,128)}, u32[]{:S(2)}) copy-start(f32[96,128]{1,0:T(8,128)} %param.20) | copy-start | bytes 147460
  111.3 3.0 %copy-start.22 = (f32[96,128]{1,0:T(8,128)S(1)}, f32[96,128]{1,0:T(8,128)}, u32[]{:S(2)}) copy-start(f32[96,128]{1,0:T(8,128)} %param.19) | copy-start | bytes 147460
  111.3 3.0 %copy-start.23 = (s32[8,96,128]{2,1,0:T(8,128)S(1)}, s32[8,96,128]{2,1,0:T(8,128)}, u32[]{:S(2)}) copy-start(s32[8,96,128]{2,1,0:T(8,128)} %param.15) | copy-start | bytes 1179652
  111.3 3.0 %copy-start.30 = (f32[96,128]{1,0:T(8,128)S(1)}, f32[96,128]{1,0:T(8,128)}, u32[]{:S(2)}) copy-start(f32[96,128]{1,0:T(8,128)} %copy-done.29) | copy-start | bytes 147460
  111.3 3.0 %copy-start.32 = (f32[96,128]{1,0:T(8,128)S(1)}, f32[96,128]{1,0:T(8,128)}, u32[]{:S(2)}) copy-start(f32[96,128]{1,0:T(8,128)} %copy-done.31) | copy-start | bytes 147460
  111.3 3.0 %copy-start.33 = (f32[96,128]{1,0:T(8,128)S(1)}, f32[96,128]{1,0:T(8,128)}, u32[]{:S(2)}) copy-start(f32[96,128]{1,0:T(8,128)} %get-tuple-element.37) | copy-start | bytes 147460
  114.3 3.5 %copy-start.15 = (f32[8,96,128]{2,1,0:T(8,128)S(1)}, f32[8,96,128]{2,1,0:T(8,128)}, u32[]{:S(2)}) copy-start(f32[8,96,128]{2,1,0:T(8,128)} %param.11) | copy-start | bytes 1179652
  117.8 3.5 %copy-start.25 = (f32[8,96,128]{2,0,1:T(8,128)S(1)}, f32[8,96,128]{2,0,1:T(8,128)}, u32[]{:S(2)}) copy-start(f32[8,96,128]{2,0,1:T(8,128)} %get-tuple-element.12) | copy-start | bytes 1179652
  (2 other events, 3.4 us)
where the time goes:
time: 123 us; the launch traced here: 122 us
  starting transfers between devices  41.5 us (34%)
  other arithmetic  36.4 us (30%)
  local copies, waits for them, and re-layouts  31.6 us (26%)
  waiting for transfers between devices  11.4 us (9%)
    ppermute x2, starting transfers between devices, with_halo(): after = lax.ppermute(initial, axis, down)  18.4 us
    ppermute x5, starting transfers between devices, partner_2(): lax.ppermute(array, axis, [(i, i ^ 1 << stride) for i in range(lax.axis_s...  17.9 us
    unnamed x85, local copies, waits for them, and re-layouts  11.4 us
    ppermute x5, waiting for transfers between devices, partner_2(): lax.ppermute(array, axis, [(i, i ^ 1 << stride) for i in range(lax.axis_s...  8.19 us
    slice x2, local copies, waits for them, and re-layouts, with_halo(): last = lax.slice_in_dim(array, length - width, length, axis=dim)  5.98 us
    mul x2, other arithmetic, tracer(): return (field - TIME_STEP * net_flux / (cell_area * thick_col)) * sea_cells  5.3 us
    ppermute x2, starting transfers between devices, with_halo(): before = lax.ppermute(last, axis, up)  5.22 us
    rev x2, local copies, waits for them, and re-layouts, advance(): upward = -jnp.cumsum(converge[::-1], axis=0)[::-1]  3.56 us
  transfers between devices with their start and end apart: 9, of which 4 were waited for; matrix products, arithmetic and copies ran while one was open for 12% of the time, Pallas kernels for 0%

commit v1 on v0

v1 whole, which is shorter than its diff:
```python
import functools
import math

import jax
import jax.numpy as jnp
from jax import lax
from jax.experimental import pallas as pl
from jax.experimental.pallas import tpu as pltpu
from jax.sharding import PartitionSpec as P

GRAVITY = 9.81
REFERENCE_DENSITY = 1026.0
TIME_STEP = 360.0
LATERAL = 300.0
VERTICAL = 0.001
ROTATION = 7.292e-05

LEVELS = 8
LANES = 128
TILE = 8
PACKET = 4 * LEVELS
VMEM = pltpu.MemorySpace.VMEM

THICK = [6.0 + 4.0 * k for k in range(LEVELS)]
DEPTH = [2.0 * k * k + 6.0 * k + 3.0 for k in range(LEVELS)]
SPACING = [4.0 * k + 4.0 for k in range(LEVELS)]


def lane_index(shape):
    return lax.broadcasted_iota(jnp.int32, shape, len(shape) - 1)


def roll_lanes(x, shift):
    return pltpu.roll(x, shift % LANES, x.ndim - 1)


def density(heat, salt, k):
    anom_t = heat - 10.0
    anom_s = salt - 35.0
    by_t = -0.1655 * (1.0 + 0.0001497 * DEPTH[k])
    by_s = 0.76554 * (1.0 - 1.109e-05 * DEPTH[k])
    along_t = by_t + (-0.1655 * 0.5 * 0.05952) * anom_t - 0.0024341 * anom_s
    along_s = by_s - (0.76554 * 0.5 * 0.00054914) * anom_s
    return along_t * anom_t + along_s * anom_s


def row_pack(
    t_low, t_top, s_low, s_top, u_low, u_top, v_top, zf_low, zf_top, mf_top, e1_top, e2_low, e2_top, to_a, to_b
):
    j = lax.axis_index("lat")
    even = j % 2 == 0
    top = j == lax.axis_size("lat") - 1
    last = TILE - 1

    def put(out, fields):
        for number, field in enumerate(fields):
            out[number * LEVELS : (number + 1) * LEVELS, :] = field

    def upward():
        spacing_x, spacing_y = e1_top[last:, :], e2_top[last:, :]
        face = mf_top[:, last, :].astype(jnp.float32)
        return [
            t_top[:, last, :],
            s_top[:, last, :],
            spacing_x * v_top[:, last, :] * face,
            LATERAL * spacing_x / spacing_y * face,
        ]

    def downward():
        flux = e2_low[:1, :] * u_low[:, 0, :] * zf_low[:, 0, :].astype(jnp.float32)
        return [t_low[:, 0, :], s_low[:, 0, :], flux, jnp.zeros_like(flux)]

    @pl.when(even)
    def _():
        put(to_a, upward())
        put(to_b, downward())

    @pl.when(jnp.logical_not(even))
    def _():
        put(to_a, downward())

    @pl.when(jnp.logical_not(even) & jnp.logical_not(top))
    def _():
        put(to_b, upward())

    @pl.when(top)
    def _():
        flux = e2_top[last:, :] * u_top[:, last, :] * zf_top[:, last, :].astype(jnp.float32)
        rows = jnp.concatenate([t_top[:, last, :], s_top[:, last, :], -flux], axis=0)
        shape = (LANES, LANES)
        mirror = lane_index(shape) + lax.broadcasted_iota(jnp.int32, shape, 0) == LANES - 1
        to_b[: 3 * LEVELS, :] = lax.dot(
            rows, mirror.astype(jnp.float32), precision=lax.Precision.HIGHEST, preferred_element_type=jnp.float32
        )
        to_b[3 * LEVELS :, :] = jnp.zeros((LEVELS, LANES), jnp.float32)


def column_pack(t, s, u, v, zf, mf, e1, e2, to_east, to_west, coriolis, packed):
    lines = t.shape[1]
    lane = lane_index((TILE, LANES))
    first_row = lax.axis_index("lat") * lines
    total_rows = lines * lax.axis_size("lat")
    packed[...] = jnp.zeros_like(packed)

    def tile(r, _):
        rows = pl.ds(pl.multiple_of(r * TILE, TILE), TILE)
        spacing_x, spacing_y = e1[rows, :], e2[rows, :]
        ratio = LATERAL * spacing_y / spacing_x
        fields = [jnp.zeros((TILE, LANES), jnp.float32) for _ in range(7)]

        def keep(number, k, x, source):
            target = number * LEVELS + k
            fields[number] = jnp.where(lane == target, roll_lanes(x, target - source), fields[number])

        for k in range(LEVELS):
            heat, salt = t[k, rows, :], s[k, rows, :]
            face = zf[k, rows, :].astype(jnp.float32)
            keep(0, k, heat, LANES - 1)
            keep(1, k, salt, LANES - 1)
            keep(2, k, spacing_y * u[k, rows, :] * face, LANES - 1)
            keep(3, k, ratio * face, LANES - 1)
            keep(4, k, heat, 0)
            keep(5, k, salt, 0)
            keep(6, k, spacing_x * v[k, rows, :] * mf[k, rows, :].astype(jnp.float32), 0)
        total = fields[0]
        for field in fields[1:]:
            total = total + field
        packed[rows, :] = total
        row = (first_row + r * TILE + lax.broadcasted_iota(jnp.int32, (TILE, LANES), 0)).astype(jnp.float32)
        latitude = 10.0 + 78.0 * (row + 0.5) / total_rows
        coriolis[rows, :] = 2.0 * ROTATION * jnp.sin(latitude * (math.pi / 180.0))
        return 0

    lax.fori_loop(0, lines // TILE, tile, 0)
    turned = packed[...].T
    to_east[...] = turned[:PACKET]
    to_west[...] = turned[PACKET : 2 * PACKET]


def corner_pack(from_a, from_b, to_east, to_west, to_a, to_b):
    even_j = lax.axis_index("lat") % 2 == 0
    even_i = lax.axis_index("lon") % 2 == 0
    shape = (PACKET, LANES)
    row = lax.broadcasted_iota(jnp.int32, shape, 0)
    corner = (lane_index(shape) == 96) & (row >= 2 * LEVELS) & (row < 3 * LEVELS)
    first, second = from_a[...], from_b[...]
    north = jnp.where(even_j, first, second)
    south = jnp.where(even_j, second, first)
    east = jnp.where(corner, roll_lanes(north, 96 - (LANES - 1)), to_east[...])
    west = jnp.where(corner, roll_lanes(south, 96), to_west[...])
    to_a[...] = jnp.where(even_i, east, west)
    to_b[...] = jnp.where(even_i, west, east)


def step(
    t, s, u, v, zf, mf, count, e1, e2, coriolis, own_west, lat_a, lat_b, lon_a, lon_b,
    t_out, s_out, u_out, v_out,
    t_ext, s_ext, p_ext, a_ext, b_ext, u_ext, v_ext, ft_ext, fs_ext, turned, sides,
):
    lines = t.shape[1]
    tiles = lines // TILE
    south_row, north_row = TILE - 1, TILE + lines
    even_j = lax.axis_index("lat") % 2 == 0
    even_i = lax.axis_index("lon") % 2 == 0

    def pick(ref_true, ref_false, flag, number):
        rows = slice(number * LEVELS, (number + 1) * LEVELS)
        return jnp.where(flag, ref_true[rows, :], ref_false[rows, :])

    north = [pick(lat_a, lat_b, even_j, n) for n in range(3)]
    south = [pick(lat_b, lat_a, even_j, n) for n in range(4)]
    east = [pick(lon_a, lon_b, even_i, n) for n in range(3)]
    west = [pick(lon_b, lon_a, even_i, n) for n in range(4)]
    lane = lane_index((TILE, LANES))
    at_first, at_last = lane == 0, lane == LANES - 1

    t_ext[:, north_row, :] = north[0]
    s_ext[:, north_row, :] = north[1]
    a_ext[:, north_row, :] = north[2] + jnp.where(at_first, roll_lanes(west[2], -96), roll_lanes(north[2], 1))
    b_ext[:, south_row, :] = south[2] + jnp.where(at_last, roll_lanes(east[2], 127 - 96), roll_lanes(south[2], -1))
    v_ext[:, south_row, :] = south[2]
    here, there = 0.5 * south[2] + south[3], 0.5 * south[2] - south[3]
    ft_ext[:, south_row, :] = here * south[0] + there * t[:, 0, :]
    fs_ext[:, south_row, :] = here * south[1] + there * s[:, 0, :]

    here, there = 0.5 * west[2] + west[3], 0.5 * west[2] - west[3]
    turned[...] = jnp.zeros_like(turned)
    turned[0:8, :] = here * west[0] + there * own_west[0:8, :]
    turned[8:16, :] = here * west[1] + there * own_west[8:16, :]
    turned[16:24, :] = west[2]
    for n in range(3):
        turned[24 + 8 * n : 32 + 8 * n, :] = east[n]
    head = jnp.zeros((1, LANES), jnp.float32)
    for k in range(LEVELS):
        half = (0.5 * THICK[k]) * density(turned[24 + k : 25 + k, :], turned[32 + k : 33 + k, :], k)
        turned[48 + k : 49 + k, :] = head + half
        head = head + 2.0 * half
    sides[...] = turned[...].T

    def extend(r, _):
        source = pl.ds(pl.multiple_of(r * TILE, TILE), TILE)
        target = pl.ds(pl.multiple_of(r * TILE + TILE, TILE), TILE)
        for k in range(LEVELS):
            t_ext[k, target, :] = t[k, source, :]
            s_ext[k, target, :] = s[k, source, :]
        return 0

    lax.fori_loop(0, tiles, extend, 0)

    def heads(r, _):
        rows = pl.ds(pl.multiple_of(r * TILE + TILE, TILE), TILE)
        head = jnp.zeros((TILE, LANES), jnp.float32)
        for k in range(LEVELS):
            half = (0.5 * THICK[k]) * density(t_ext[k, rows, :], s_ext[k, rows, :], k)
            p_ext[k, rows, :] = head + half
            head = head + 2.0 * half
        return 0

    lax.fori_loop(0, tiles + 1, heads, 0)

    def from_west(x, side, number):
        return jnp.where(at_first, roll_lanes(side, -number), roll_lanes(x, 1))

    def from_east(x, side, number):
        return jnp.where(at_last, roll_lanes(side, LANES - 1 - number), roll_lanes(x, -1))

    def faces(r, _):
        source = pl.ds(pl.multiple_of(r * TILE, TILE), TILE)
        rows = pl.ds(pl.multiple_of(r * TILE + TILE, TILE), TILE)
        above = pl.ds(r * TILE + TILE + 1, TILE)
        spacing_x, spacing_y = e1[source, :], e2[source, :]
        ratio = LATERAL * spacing_x / spacing_y
        side = sides[source, :]
        for k in range(LEVELS):
            flux_x = spacing_y * u[k, source, :] * zf[k, source, :].astype(jnp.float32)
            u_ext[k, rows, :] = flux_x
            a_ext[k, rows, :] = flux_x + from_west(flux_x, side, 16 + k)
            face = mf[k, source, :].astype(jnp.float32)
            flux_y = spacing_x * v[k, source, :] * face
            v_ext[k, rows, :] = flux_y
            b_ext[k, rows, :] = flux_y + from_east(flux_y, side, 40 + k)
            here, there = 0.5 * flux_y + ratio * face, 0.5 * flux_y - ratio * face
            ft_ext[k, rows, :] = here * t_ext[k, rows, :] + there * t_ext[k, above, :]
            fs_ext[k, rows, :] = here * s_ext[k, rows, :] + there * s_ext[k, above, :]
        return 0

    lax.fori_loop(0, tiles, faces, 0)

    def update(r, _):
        source = pl.ds(pl.multiple_of(r * TILE, TILE), TILE)
        rows = pl.ds(pl.multiple_of(r * TILE + TILE, TILE), TILE)
        above = pl.ds(r * TILE + TILE + 1, TILE)
        below = pl.ds(r * TILE + TILE - 1, TILE)
        spacing_x, spacing_y = e1[source, :], e2[source, :]
        side = sides[source, :]
        levels = count[source, :]
        inverse_x, inverse_y = 1.0 / spacing_x, 1.0 / spacing_y
        ratio = LATERAL * spacing_y * inverse_x
        area = spacing_x * spacing_y
        per_area = TIME_STEP * inverse_x * inverse_y
        turn = (0.25 * TIME_STEP) * coriolis[source, :]
        turn_x, turn_y = turn * inverse_x, turn * inverse_y
        push = -TIME_STEP * GRAVITY / REFERENCE_DENSITY
        push_x, push_y = push * inverse_x, push * inverse_y
        zero = jnp.zeros((TILE, LANES), jnp.float32)
        upward, t_below, s_below, u_below, v_below = zero, zero, zero, zero, zero
        for k in reversed(range(LEVELS)):
            heat, salt = t[k, source, :], s[k, source, :]
            flux_x, flux_y = u_ext[k, rows, :], v_ext[k, rows, :]
            face_x, face_y = zf[k, source, :].astype(jnp.float32), mf[k, source, :].astype(jnp.float32)
            both_x, both_y = a_ext[k, rows, :], b_ext[k, rows, :]
            wet = levels > k
            spread = ratio * face_x
            here, there = 0.5 * flux_x + spread, 0.5 * flux_x - spread
            t_east = here * heat + there * from_east(heat, side, 24 + k)
            s_east = here * salt + there * from_east(salt, side, 32 + k)
            t_net = t_east - from_west(t_east, side, k) + ft_ext[k, rows, :] - ft_ext[k, below, :]
            s_net = s_east - from_west(s_east, side, 8 + k) + fs_ext[k, rows, :] - fs_ext[k, below, :]
            converge = 2.0 * flux_x - both_x + flux_y - v_ext[k, below, :]
            upward = upward - THICK[k] * converge
            if k > 0:
                mix = jnp.where(wet, (VERTICAL / SPACING[k]) * area, 0.0)
                upper, lower = 0.5 * upward - mix, 0.5 * upward + mix
                t_above = upper * t[k - 1, source, :] + lower * heat
                s_above = upper * s[k - 1, source, :] + lower * salt
            else:
                t_above, s_above = upward * heat, upward * salt
            t_net = t_net + (t_above - t_below) * (1.0 / THICK[k])
            s_net = s_net + (s_above - s_below) * (1.0 / THICK[k])
            t_below, s_below = t_above, s_above
            t_out[k, source, :] = jnp.where(wet, heat - per_area * t_net, 0.0)
            s_out[k, source, :] = jnp.where(wet, salt - per_area * s_net, 0.0)
            zonal, meridional = u[k, source, :], v[k, source, :]
            if k > 0:
                scale = VERTICAL / SPACING[k]
                u_above = scale * (u[k - 1, source, :] - zonal) * (face_x * zf[k - 1, source, :].astype(jnp.float32))
                v_above = scale * (v[k - 1, source, :] - meridional) * (face_y * mf[k - 1, source, :].astype(jnp.float32))
            else:
                u_above, v_above = zero, zero
            head = p_ext[k, rows, :]
            slope_x = from_east(head, side, 48 + k) - head
            slope_y = p_ext[k, above, :] - head
            share = TIME_STEP / THICK[k]
            u_out[k, source, :] = (
                zonal + push_x * slope_x + turn_x * (both_y + b_ext[k, below, :]) + share * (u_above - u_below)
            ) * face_x
            v_out[k, source, :] = (
                meridional + push_y * slope_y - turn_y * (both_x + a_ext[k, above, :]) + share * (v_above - v_below)
            ) * face_y
            u_below, v_below = u_above, v_above
        return 0

    lax.fori_loop(0, tiles, update, 0)


def whole(n):
    return [pl.BlockSpec(memory_space=VMEM)] * n


def per_device(
    potential_warmth_degrees,
    dissolved_salt_content,
    zonal_edge_current,
    meridional_edge_current,
    wet_grid_flag,
    zonal_wet_edge_flag,
    meridional_wet_edge_flag,
    bottom_tier_count,
    zonal_grid_spacing,
    meridional_grid_spacing,
):
    t, s, u, v = potential_warmth_degrees, dissolved_salt_content, zonal_edge_current, meridional_edge_current
    zf, mf, e1, e2 = zonal_wet_edge_flag, meridional_wet_edge_flag, zonal_grid_spacing, meridional_grid_spacing
    lines = t.shape[1]
    lons, lats = lax.axis_size("lon"), lax.axis_size("lat")
    f32 = jnp.float32
    params = pltpu.CompilerParams(vmem_limit_bytes=24 * 1024 * 1024)
    packet = jax.ShapeDtypeStruct((PACKET, LANES), f32)
    field = jax.ShapeDtypeStruct(t.shape, f32)

    low3 = pl.BlockSpec((LEVELS, TILE, LANES), lambda g: (0, 0, 0))
    top3 = pl.BlockSpec((LEVELS, TILE, LANES), lambda g: (0, lines // TILE - 1, 0))
    low2 = pl.BlockSpec((TILE, LANES), lambda g: (0, 0))
    top2 = pl.BlockSpec((TILE, LANES), lambda g: (lines // TILE - 1, 0))
    out2 = pl.BlockSpec((PACKET, LANES), lambda g: (0, 0))
    lat_to_a, lat_to_b = pl.pallas_call(
        row_pack,
        grid=(1,),
        in_specs=[low3, top3, low3, top3, low3, top3, top3, low3, top3, top3, top2, low2, top2],
        out_specs=[out2, out2],
        out_shape=[packet, packet],
        compiler_params=params,
        name="row_pack",
    )(t, t, s, s, u, u, v, zf, zf, mf, e1, e2, e2)

    pairs_a = [(j, j ^ 1) for j in range(lats)]
    pairs_b = []
    for i in range(lons):
        for j in range(1, lats):
            other = (lons - 1 - i) * lats + j if j == lats - 1 else i * lats + (j + 1 if j % 2 else j - 1)
            pairs_b.append((i * lats + j, other))
    lat_a = lax.ppermute(lat_to_a, "lat", pairs_a)
    lat_b = lax.ppermute(lat_to_b, ("lon", "lat"), pairs_b)

    to_east, to_west, coriolis = pl.pallas_call(
        column_pack,
        in_specs=whole(8),
        out_specs=whole(3),
        out_shape=[packet, packet, jax.ShapeDtypeStruct(e1.shape, f32)],
        scratch_shapes=[VMEM((LANES, LANES), f32)],
        compiler_params=params,
        name="column_pack",
    )(t, s, u, v, zf, mf, e1, e2)

    lon_to_a, lon_to_b = pl.pallas_call(
        corner_pack,
        in_specs=whole(4),
        out_specs=whole(2),
        out_shape=[packet, packet],
        compiler_params=params,
        name="corner_pack",
    )(lat_a, lat_b, to_east, to_west)
    lon_b = lax.ppermute(lon_to_b, "lon", [(i, (i + 1 if i % 2 else i - 1) % lons) for i in range(lons)])
    lon_a = lax.ppermute(lon_to_a, "lon", [(i, i ^ 1) for i in range(lons)])

    extended = VMEM((LEVELS, lines + 2 * TILE, LANES), f32)
    square = VMEM((LANES, LANES), f32)
    return pl.pallas_call(
        step,
        in_specs=whole(15),
        out_specs=whole(4),
        out_shape=[field] * 4,
        scratch_shapes=[extended] * 9 + [square] * 2,
        compiler_params=params,
        name="step",
    )(t, s, u, v, zf, mf, bottom_tier_count, e1, e2, coriolis, to_west, lat_a, lat_b, lon_a, lon_b)


def solution(mesh):
    deep, flat = P(None, "lat", "lon"), P("lat", "lon")
    return jax.shard_map(
        per_device,
        mesh=mesh,
        in_specs=(deep,) * 7 + (flat,) * 3,
        out_specs=(deep,) * 4,
        check_vma=False,
    )
```

time: 123 us -> 43.4 us (0.35)
  other arithmetic: 36.4 us -> 0 us
  local copies, waits for them, and re-layouts: 31.6 us -> 7.59 us
  starting transfers between devices: 41.5 us -> 25.2 us
  waiting for transfers between devices: 11.4 us -> 2.26 us
  Pallas kernels: 0 us -> 7.07 us
    mul x11 -> x0, other arithmetic: 18.2 us -> none  [the longest x2 5.3 us: tracer(): return (field - TIME_STEP * net_flux / (cell_area * thick_col)) * sea_cells]
    ppermute x9 -> x4, starting transfers between devices: 41.5 us -> 25.2 us  [the longest x1 13 us: per_device(): lax.ppermute(lon_to_b, 'lon', [(i, (i + 1 if i % 2 else i - 1) % lons) fo...]
    slice x8 -> x0, local copies, waits for them, and re-layouts: 9.17 us -> none  [the longest x2 5.98 us: with_halo(): last = lax.slice_in_dim(array, length - width, length, axis=dim)]
    ppermute x9 -> x4, waiting for transfers between devices: 11.4 us -> 2.26 us  [the longest x1 1.41 us: per_device(): lax.ppermute(lon_to_b, 'lon', [(i, (i + 1 if i % 2 else i - 1) % lons) fo...]
    pallas_call x0 -> x4, Pallas kernels: none -> 7.07 us  [the longest x1 5.31 us: per_device(): pl.pallas_call(step, in_specs=whole(15), out_specs=whole(4), out_shape=[f...]
    ppermute x2 -> x0, local copies, waits for them, and re-layouts: 6.08 us -> none  [the longest x1 3.08 us: with_halo(): after = lax.ppermute(initial, axis, down)]
    another operation x2 -> x0, other arithmetic: 4.79 us -> none  [the longest x1 2.68 us: advance(): jnp.cumsum(weighted, axis=0) - 0.5 * weighted]
    sub x2 -> x0, other arithmetic: 4.15 us -> none  [the longest x1 2.45 us: tracer(): upward[1:] * (field[:-1] + field[1:]) * 0.5]
  transfers between devices with their start and end apart: 9 -> 4, of which waited for: 4 -> 2; matrix products, arithmetic and copies ran while one was open for 12% -> 0% of each run, Pallas kernels for 0% -> 4%
where the time goes in v1:
time: 43.4 us; the launch traced here: 42.8 us
  starting transfers between devices  25.2 us (58%)
  local copies, waits for them, and re-layouts  7.59 us (17%)
  Pallas kernels  7.07 us (16%)
  waiting for transfers between devices  2.26 us (5%)
  between operations  0.72 us (2%)
    ppermute x1, starting transfers between devices, per_device(): lax.ppermute(lon_to_b, 'lon', [(i, (i + 1 if i % 2 else i - 1) % lons) fo...  13 us
    unnamed x20, local copies, waits for them, and re-layouts  7.59 us
    ppermute x1, starting transfers between devices, per_device(): lat_b = lax.ppermute(lat_to_b, ('lon', 'lat'), pairs_b)  5.93 us
    pallas_call x1, Pallas kernels, per_device(): pl.pallas_call(step, in_specs=whole(15), out_specs=whole(4), out_shape=[f...  5.31 us
    ppermute x1, starting transfers between devices, per_device(): lat_a = lax.ppermute(lat_to_a, 'lat', pairs_a)  4.28 us
    ppermute x1, starting transfers between devices, per_device(): lon_a = lax.ppermute(lon_to_a, 'lon', [(i, i ^ 1) for i in range(lons)])  1.91 us
    pallas_call x1, Pallas kernels, per_device(): pl.pallas_call(column_pack, in_specs=whole(8), out_specs=whole(3), out_sh...  1.63 us
    ppermute x1, waiting for transfers between devices, per_device(): lax.ppermute(lon_to_b, 'lon', [(i, (i + 1 if i % 2 else i - 1) % lons) fo...  1.41 us
  transfers between devices with their start and end apart: 4, of which 2 were waited for; matrix products, arithmetic and copies ran while one was open for 0% of the time, Pallas kernels for 4%

profile of v1, /device:TPU:6, one launch (start us, length us, event | category | flops | bytes accessed | tf_op | source)
XLA Modules:
  0.0 42.8 jit_solution(3365298327595265699)
XLA Ops:
  0.6 0.0 copy-start
  0.6 1.0 %copy-done = f32[8,96,128]{2,1,0:T(8,128)S(1)} copy-done((f32[8,96,128]{2,1,0:T(8,128)S(1)}, f32[8,96,128]{2,1,0:T(8,128)}, u32[]{:S(2)}) %copy-start) | copy-done | bytes 393240
  1.6 0.0 copy-start.2
  1.6 1.0 %copy-done.2 = f32[8,96,128]{2,1,0:T(8,128)S(1)} copy-done((f32[8,96,128]{2,1,0:T(8,128)S(1)}, f32[8,96,128]{2,1,0:T(8,128)}, u32[]{:S(2)}) %copy-start.2) | copy-done | bytes 393240
  2.6 0.0 copy-start.3
  2.6 1.0 %copy-done.3 = f32[8,96,128]{2,1,0:T(8,128)S(1)} copy-done((f32[8,96,128]{2,1,0:T(8,128)S(1)}, f32[8,96,128]{2,1,0:T(8,128)}, u32[]{:S(2)}) %copy-start.3) | copy-done | bytes 393240
  3.6 0.0 copy-start.4
  3.6 1.0 %copy-done.4 = s32[8,96,128]{2,1,0:T(8,128)S(1)} copy-done((s32[8,96,128]{2,1,0:T(8,128)S(1)}, s32[8,96,128]{2,1,0:T(8,128)}, u32[]{:S(2)}) %copy-start.4) | copy-done | bytes 393240
  4.6 0.0 copy-start.5
  4.6 1.0 %copy-done.5 = f32[8,96,128]{2,1,0:T(8,128)S(1)} copy-done((f32[8,96,128]{2,1,0:T(8,128)S(1)}, f32[8,96,128]{2,1,0:T(8,128)}, u32[]{:S(2)}) %copy-start.5) | copy-done | bytes 393240
  5.6 0.0 copy-start.6
  5.6 1.0 %copy-done.6 = s32[8,96,128]{2,1,0:T(8,128)S(1)} copy-done((s32[8,96,128]{2,1,0:T(8,128)S(1)}, s32[8,96,128]{2,1,0:T(8,128)}, u32[]{:S(2)}) %copy-start.6) | copy-done | bytes 393240
  6.6 0.0 copy-start.7
  6.6 0.8 %copy-done.7 = f32[96,128]{1,0:T(8,128)S(1)} copy-done((f32[96,128]{1,0:T(8,128)S(1)}, f32[96,128]{1,0:T(8,128)}, u32[]{:S(2)}) %copy-start.7) | copy-done | bytes 49176
  7.4 0.0 copy-start.8
  7.4 0.8 %copy-done.8 = f32[96,128]{1,0:T(8,128)S(1)} copy-done((f32[96,128]{1,0:T(8,128)S(1)}, f32[96,128]{1,0:T(8,128)}, u32[]{:S(2)}) %copy-start.8) | copy-done | bytes 49176
  8.2 0.1 row_pack.1
  8.3 4.3 %collective-permute-start = (f32[32,128]{1,0:T(8,128)S(1)}, f32[32,128]{1,0:T(8,128)S(1)}, u32[]{:S(2)}, u32[]{:S(2)}) collective-permute-start(f32[32,128]{1,0:T(8,128)S(1)} %get-tuple-element.13), channel_id=1, source_target_pairs={{0,1},{1,0},{2,3},{3,2},{4,5},{5,4},{6,7},{7,6},{8,9},{9,8},{10,11... | collective-permute-start | bytes 49160 | tf_op jit(solution)/shard_map/ppermute | solution.py:362
  12.6 0.0 copy-start.1
  12.6 5.9 %collective-permute-start.1 = (f32[32,128]{1,0:T(8,128)S(1)}, f32[32,128]{1,0:T(8,128)S(1)}, u32[]{:S(2)}, u32[]{:S(2)}) collective-permute-start(f32[32,128]{1,0:T(8,128)S(1)} %get-tuple-element.14), channel_id=1, source_target_pairs={{1,2},{2,1},{3,4},{4,3},{5,6},{6,5},{7,8},{8,7},{9,10},{10,9},{11,... | collective-permute-start | bytes 49160 | tf_op jit(solution)/shard_map/ppermute | solution.py:363
  18.5 1.6 %column_pack.1 = (f32[32,128]{1,0:T(8,128)S(1)}, f32[32,128]{1,0:T(8,128)S(1)}, f32[96,128]{1,0:T(8,128)S(1)}) custom-call(f32[8,96,128]{2,1,0:T(8,128)S(1)} %copy-done, f32[8,96,128]{2,1,0:T(8,128)S(1)} %copy-done.2, f32[8,96,128]{2,1,0:T(8,128)S(1)} %copy-done.3, f32[8,96,128]{2,1,0:T(8,128)S(1)} %copy-done.5, s32[8,96,128]{2,1,0:T(8,128)S(1)} %copy-done.4, ...), custom_call_target="tpu_custom_call" | custom-call | tf_op jit(solution)/shard_map/column_pack/pallas_call | solution.py:365
  20.2 0.0 copy-start.9
  20.2 0.0 collective-permute-done.from_a.lat_a
  20.2 0.8 %collective-permute-done.1.from_b.lat_b = f32[32,128]{1,0:T(8,128)S(1)} collective-permute-done((f32[32,128]{1,0:T(8,128)S(1)}, f32[32,128]{1,0:T(8,128)S(1)}, u32[]{:S(2)}, u32[]{:S(2)}) %collective-permute-start.1) | collective-permute-done | bytes 16416 | tf_op jit(solution)/shard_map/ppermute | solution.py:363
  21.0 0.1 corner_pack.1
  21.1 1.9 %collective-permute-start.2 = (f32[32,128]{1,0:T(8,128)S(1)}, f32[32,128]{1,0:T(8,128)S(1)}, u32[]{:S(2)}, u32[]{:S(2)}) collective-permute-start(f32[32,128]{1,0:T(8,128)S(1)} %get-tuple-element.16), channel_id=1, source_target_pairs={{0,16},{16,0},{32,48},{48,32},{64,80},{80,64},{96,112},{112,96},{1... | collective-permute-start | bytes 49160 | tf_op jit(solution)/shard_map/ppermute | solution.py:384
  23.0 13.0 %collective-permute-start.3 = (f32[32,128]{1,0:T(8,128)S(1)}, f32[32,128]{1,0:T(8,128)S(1)}, u32[]{:S(2)}, u32[]{:S(2)}) collective-permute-start(f32[32,128]{1,0:T(8,128)S(1)} %get-tuple-element.17), channel_id=1, source_target_pairs={{0,496},{16,32},{32,16},{48,64},{64,48},{80,96},{96,80},{112,128},... | collective-permute-start | bytes 49160 | tf_op jit(solution)/shard_map/ppermute | solution.py:383
  36.1 0.0 collective-permute-done.2.lon_a
  36.1 1.4 %collective-permute-done.3.lon_b = f32[32,128]{1,0:T(8,128)S(1)} collective-permute-done((f32[32,128]{1,0:T(8,128)S(1)}, f32[32,128]{1,0:T(8,128)S(1)}, u32[]{:S(2)}, u32[]{:S(2)}) %collective-permute-start.3) | collective-permute-done | bytes 16416 | tf_op jit(solution)/shard_map/ppermute | solution.py:383
  37.5 0.0 copy-done.1
  37.5 0.0 copy-done.9
  37.5 5.3 %step.1 = (f32[8,96,128]{2,1,0:T(8,128)}, f32[8,96,128]{2,1,0:T(8,128)}, f32[8,96,128]{2,1,0:T(8,128)}, f32[8,96,128]{2,1,0:T(8,128)}) custom-call(f32[8,96,128]{2,1,0:T(8,128)S(1)} %copy-done.1, f32[8,96,128]{2,1,0:T(8,128)S(1)} %copy-done.2, f32[8,96,128]{2,1,0:T(8,128)S(1)} %copy-done.3, f32[8,96,128]{2,1,0:T(8,128)S(1)} %copy-done.5, ...), custom_call_target="tpu_custom_call" | custom-call | tf_op jit(solution)/shard_map/step/pallas_call | solution.py:388
Async XLA Ops:
  0.6 1.0 %copy-start = (f32[8,96,128]{2,1,0:T(8,128)S(1)}, f32[8,96,128]{2,1,0:T(8,128)}, u32[]{:S(2)}) copy-start(f32[8,96,128]{2,1,0:T(8,128)} %t.3) | copy-start | bytes 1179652
  1.6 1.0 %copy-start.2 = (f32[8,96,128]{2,1,0:T(8,128)S(1)}, f32[8,96,128]{2,1,0:T(8,128)}, u32[]{:S(2)}) copy-start(f32[8,96,128]{2,1,0:T(8,128)} %s.3) | copy-start | bytes 1179652
  2.6 1.0 %copy-start.3 = (f32[8,96,128]{2,1,0:T(8,128)S(1)}, f32[8,96,128]{2,1,0:T(8,128)}, u32[]{:S(2)}) copy-start(f32[8,96,128]{2,1,0:T(8,128)} %u.3) | copy-start | bytes 1179652
  3.6 1.0 %copy-start.4 = (s32[8,96,128]{2,1,0:T(8,128)S(1)}, s32[8,96,128]{2,1,0:T(8,128)}, u32[]{:S(2)}) copy-start(s32[8,96,128]{2,1,0:T(8,128)} %zf.3) | copy-start | bytes 1179652
  4.6 1.0 %copy-start.5 = (f32[8,96,128]{2,1,0:T(8,128)S(1)}, f32[8,96,128]{2,1,0:T(8,128)}, u32[]{:S(2)}) copy-start(f32[8,96,128]{2,1,0:T(8,128)} %v.3) | copy-start | bytes 1179652
  5.6 1.0 %copy-start.6 = (s32[8,96,128]{2,1,0:T(8,128)S(1)}, s32[8,96,128]{2,1,0:T(8,128)}, u32[]{:S(2)}) copy-start(s32[8,96,128]{2,1,0:T(8,128)} %mf.3) | copy-start | bytes 1179652
  6.6 0.8 %copy-start.7 = (f32[96,128]{1,0:T(8,128)S(1)}, f32[96,128]{1,0:T(8,128)}, u32[]{:S(2)}) copy-start(f32[96,128]{1,0:T(8,128)} %e2.3) | copy-start | bytes 147460
  7.4 0.8 %copy-start.8 = (f32[96,128]{1,0:T(8,128)S(1)}, f32[96,128]{1,0:T(8,128)}, u32[]{:S(2)}) copy-start(f32[96,128]{1,0:T(8,128)} %e1.3) | copy-start | bytes 147460
  8.3 11.9 %collective-permute-start = (f32[32,128]{1,0:T(8,128)S(1)}, f32[32,128]{1,0:T(8,128)S(1)}, u32[]{:S(2)}, u32[]{:S(2)}) collective-permute-start(f32[32,128]{1,0:T(8,128)S(1)} %get-tuple-element.13), channel_id=1, source_target_pairs={{0,1},{1,0},{2,3},{3,2},{4,5},{5,4},{6,7},{7,6},{8,9},{9,8},{10,11... | collective-permute-start | bytes 49160 | tf_op jit(solution)/shard_map/ppermute | solution.py:362
  12.6 24.9 %copy-start.1 = (f32[8,96,128]{2,1,0:T(8,128)S(1)}, f32[8,96,128]{2,1,0:T(8,128)}, u32[]{:S(2)}) copy-start(f32[8,96,128]{2,1,0:T(8,128)} %t.3) | copy-start | bytes 1179652
  12.6 8.5 %collective-permute-start.1 = (f32[32,128]{1,0:T(8,128)S(1)}, f32[32,128]{1,0:T(8,128)S(1)}, u32[]{:S(2)}, u32[]{:S(2)}) collective-permute-start(f32[32,128]{1,0:T(8,128)S(1)} %get-tuple-element.14), channel_id=1, source_target_pairs={{1,2},{2,1},{3,4},{4,3},{5,6},{6,5},{7,8},{8,7},{9,10},{10,9},{11,... | collective-permute-start | bytes 49160 | tf_op jit(solution)/shard_map/ppermute | solution.py:363
  20.2 17.3 %copy-start.9 = (s32[96,128]{1,0:T(8,128)S(1)}, s32[96,128]{1,0:T(8,128)}, u32[]{:S(2)}) copy-start(s32[96,128]{1,0:T(8,128)} %count.1) | copy-start | bytes 147460
  21.1 15.0 %collective-permute-start.2 = (f32[32,128]{1,0:T(8,128)S(1)}, f32[32,128]{1,0:T(8,128)S(1)}, u32[]{:S(2)}, u32[]{:S(2)}) collective-permute-start(f32[32,128]{1,0:T(8,128)S(1)} %get-tuple-element.16), channel_id=1, source_target_pairs={{0,16},{16,0},{32,48},{48,32},{64,80},{80,64},{96,112},{112,96},{1... | collective-permute-start | bytes 49160 | tf_op jit(solution)/shard_map/ppermute | solution.py:384
  23.0 14.5 %collective-permute-start.3 = (f32[32,128]{1,0:T(8,128)S(1)}, f32[32,128]{1,0:T(8,128)S(1)}, u32[]{:S(2)}, u32[]{:S(2)}) collective-permute-start(f32[32,128]{1,0:T(8,128)S(1)} %get-tuple-element.17), channel_id=1, source_target_pairs={{0,496},{16,32},{32,16},{48,64},{64,48},{80,96},{96,80},{112,128},... | collective-permute-start | bytes 49160 | tf_op jit(solution)/shard_map/ppermute | solution.py:383

commit v2 on v1

--- a/solution.py
+++ b/solution.py
@@ -44,31 +44,40 @@
     return along_t * anom_t + along_s * anom_s
 
 
-def row_pack(
-    t_low, t_top, s_low, s_top, u_low, u_top, v_top, zf_low, zf_top, mf_top, e1_top, e2_low, e2_top, to_a, to_b
-):
+def row_pack(t, s, u, v, zf, mf, e1, e2, to_a, to_b, deep, flags, flat, arrived):
     j = lax.axis_index("lat")
     even = j % 2 == 0
     top = j == lax.axis_size("lat") - 1
     last = TILE - 1
+    low, high = pl.ds(0, TILE), pl.ds(t.shape[1] - TILE, TILE)
+    wanted = [(t, low), (t, high), (s, low), (s, high), (u, low), (u, high), (v, high)]
+    marks = [(zf, low), (zf, high), (mf, high)]
+    sizes = [(e1, high), (e2, high), (e2, low)]
+    copies = [pltpu.make_async_copy(ref.at[:, rows, :], deep.at[n], arrived.at[n]) for n, (ref, rows) in enumerate(wanted)]
+    copies += [pltpu.make_async_copy(ref.at[:, rows, :], flags.at[n], arrived.at[7 + n]) for n, (ref, rows) in enumerate(marks)]
+    copies += [pltpu.make_async_copy(ref.at[rows, :], flat.at[n], arrived.at[10 + n]) for n, (ref, rows) in enumerate(sizes)]
+    for copy in copies:
+        copy.start()
+    for copy in copies:
+        copy.wait()
 
     def put(out, fields):
         for number, field in enumerate(fields):
             out[number * LEVELS : (number + 1) * LEVELS, :] = field
 
     def upward():
-        spacing_x, spacing_y = e1_top[last:, :], e2_top[last:, :]
-        face = mf_top[:, last, :].astype(jnp.float32)
+        spacing_x, spacing_y = flat[0, last:, :], flat[1, last:, :]
+        face = flags[2, :, last, :].astype(jnp.float32)
         return [
-            t_top[:, last, :],
-            s_top[:, last, :],
-            spacing_x * v_top[:, last, :] * face,
+            deep[1, :, last, :],
+            deep[3, :, last, :],
+            spacing_x * deep[6, :, last, :] * face,
             LATERAL * spacing_x / spacing_y * face,
         ]
 
     def downward():
-        flux = e2_low[:1, :] * u_low[:, 0, :] * zf_low[:, 0, :].astype(jnp.float32)
-        return [t_low[:, 0, :], s_low[:, 0, :], flux, jnp.zeros_like(flux)]
+        flux = flat[2, :1, :] * deep[4, :, 0, :] * flags[0, :, 0, :].astype(jnp.float32)
+        return [deep[0, :, 0, :], deep[2, :, 0, :], flux, jnp.zeros_like(flux)]
 
     @pl.when(even)
     def _():
@@ -85,8 +94,8 @@
 
     @pl.when(top)
     def _():
-        flux = e2_top[last:, :] * u_top[:, last, :] * zf_top[:, last, :].astype(jnp.float32)
-        rows = jnp.concatenate([t_top[:, last, :], s_top[:, last, :], -flux], axis=0)
+        flux = flat[1, last:, :] * deep[5, :, last, :] * flags[1, :, last, :].astype(jnp.float32)
+        rows = jnp.concatenate([deep[1, :, last, :], deep[3, :, last, :], -flux], axis=0)
         shape = (LANES, LANES)
         mirror = lane_index(shape) + lax.broadcasted_iota(jnp.int32, shape, 0) == LANES - 1
         to_b[: 3 * LEVELS, :] = lax.dot(
@@ -338,20 +347,19 @@
     packet = jax.ShapeDtypeStruct((PACKET, LANES), f32)
     field = jax.ShapeDtypeStruct(t.shape, f32)
 
-    low3 = pl.BlockSpec((LEVELS, TILE, LANES), lambda g: (0, 0, 0))
-    top3 = pl.BlockSpec((LEVELS, TILE, LANES), lambda g: (0, lines // TILE - 1, 0))
-    low2 = pl.BlockSpec((TILE, LANES), lambda g: (0, 0))
-    top2 = pl.BlockSpec((TILE, LANES), lambda g: (lines // TILE - 1, 0))
-    out2 = pl.BlockSpec((PACKET, LANES), lambda g: (0, 0))
     lat_to_a, lat_to_b = pl.pallas_call(
         row_pack,
-        grid=(1,),
-        in_specs=[low3, top3, low3, top3, low3, top3, top3, low3, top3, top3, top2, low2, top2],
-        out_specs=[out2, out2],
+        in_specs=[pl.BlockSpec(memory_space=pl.ANY)] * 8,
+        out_specs=whole(2),
         out_shape=[packet, packet],
-        compiler_params=params,
+        scratch_shapes=[
+            VMEM((7, LEVELS, TILE, LANES), f32),
+            VMEM((3, LEVELS, TILE, LANES), jnp.int32),
+            VMEM((3, TILE, LANES), f32),
+            pltpu.SemaphoreType.DMA((13,)),
+        ],
         name="row_pack",
-    )(t, t, s, s, u, u, v, zf, zf, mf, e1, e2, e2)
+    )(t, s, u, v, zf, mf, e1, e2)
 
     pairs_a = [(j, j ^ 1) for j in range(lats)]
     pairs_b = []

time: 43.4 us -> 37.4 us (0.86)
  local copies, waits for them, and re-layouts: 7.59 us -> 0.06 us
  Pallas kernels: 7.07 us -> 8.83 us
    unnamed x20 -> x18, local copies, waits for them, and re-layouts: 7.59 us -> 0.06 us
    pallas_call x1, Pallas kernels: 0.06 us -> 1.82 us  [per_device(): pl.pallas_call(row_pack, in_specs=[pl.BlockSpec(memory_space=pl.ANY)] * 8...]
where the time goes in v2:
time: 37.4 us; the launch traced here: 37.1 us
  starting transfers between devices  25 us (67%)
  Pallas kernels  8.83 us (24%)
  waiting for transfers between devices  2.39 us (6%)
  between operations  0.83 us (2%)
    ppermute x1, starting transfers between devices, per_device(): lax.ppermute(lon_to_b, 'lon', [(i, (i + 1 if i % 2 else i - 1) % lons) fo...  13 us
    ppermute x1, starting transfers between devices, per_device(): lat_b = lax.ppermute(lat_to_b, ('lon', 'lat'), pairs_b)  5.8 us
    pallas_call x1, Pallas kernels, per_device(): pl.pallas_call(step, in_specs=whole(15), out_specs=whole(4), out_shape=[f...  5.31 us
    ppermute x1, starting transfers between devices, per_device(): lat_a = lax.ppermute(lat_to_a, 'lat', pairs_a)  4.28 us
    ppermute x1, starting transfers between devices, per_device(): lon_a = lax.ppermute(lon_to_a, 'lon', [(i, i ^ 1) for i in range(lons)])  1.91 us
    pallas_call x1, Pallas kernels, per_device(): pl.pallas_call(row_pack, in_specs=[pl.BlockSpec(memory_space=pl.ANY)] * 8...  1.82 us
    pallas_call x1, Pallas kernels, per_device(): pl.pallas_call(column_pack, in_specs=whole(8), out_specs=whole(3), out_sh...  1.63 us
    ppermute x1, waiting for transfers between devices, per_device(): lax.ppermute(lon_to_b, 'lon', [(i, (i + 1 if i % 2 else i - 1) % lons) fo...  1.41 us
  transfers between devices with their start and end apart: 4, of which 2 were waited for; matrix products, arithmetic and copies ran while one was open for 0% of the time, Pallas kernels for 4%

profile of v2, /device:TPU:6, one launch (start us, length us, event | category | flops | bytes accessed | tf_op | source)
XLA Modules:
  0.0 37.1 jit_solution(13218256089676651845)
XLA Ops:
  0.6 0.0 copy-start.7
  0.6 0.0 copy-start.6
  0.7 0.0 copy-start.5
  0.7 0.0 copy-start.4
  0.7 0.0 copy-start.3
  0.7 0.0 copy-start.2
  0.7 0.0 copy-start.1
  0.7 0.0 copy-start
  0.7 1.8 %row_pack.1 = (f32[32,128]{1,0:T(8,128)}, f32[32,128]{1,0:T(8,128)}) custom-call(f32[8,96,128]{2,1,0:T(8,128)} %t.5, f32[8,96,128]{2,1,0:T(8,128)} %s.5, f32[8,96,128]{2,1,0:T(8,128)} %u.5, f32[8,96,128]{2,1,0:T(8,128)} %v.5, s32[8,96,128]{2,1,0:T(8,128)} %zf.5, s32[8,96,128]{2,1,0:T(8,128)} %mf.5, f32[96,128]{1,0:T(8,128)} %e1.5, f32[96,128]{1,0:T(8,128)} %e2.5), custom_call_target="tpu_custom_call" | custom-call | tf_op jit(solution)/shard_map/row_pack/pallas_call | solution.py:350
  2.5 4.3 %collective-permute-start = (f32[32,128]{1,0:T(8,128)}, f32[32,128]{1,0:T(8,128)S(1)}, u32[]{:S(2)}, u32[]{:S(2)}) collective-permute-start(f32[32,128]{1,0:T(8,128)} %get-tuple-element.13), channel_id=1, source_target_pairs={{0,1},{1,0},{2,3},{3,2},{4,5},{5,4},{6,7},{7,6},{8,9},{9,8},{10,11... | collective-permute-start | bytes 49160 | tf_op jit(solution)/shard_map/ppermute | solution.py:370
  6.8 5.8 %collective-permute-start.1 = (f32[32,128]{1,0:T(8,128)}, f32[32,128]{1,0:T(8,128)S(1)}, u32[]{:S(2)}, u32[]{:S(2)}) collective-permute-start(f32[32,128]{1,0:T(8,128)} %get-tuple-element.14), channel_id=1, source_target_pairs={{1,2},{2,1},{3,4},{4,3},{5,6},{6,5},{7,8},{8,7},{9,10},{10,9},{11,... | collective-permute-start | bytes 49160 | tf_op jit(solution)/shard_map/ppermute | solution.py:371
  12.6 0.0 copy-done.7
  12.6 0.0 copy-done.6
  12.7 0.0 copy-done.5
  12.7 0.0 copy-done.4
  12.7 0.0 copy-done.3
  12.7 0.0 copy-done.2
  12.7 0.0 copy-done.1
  12.7 0.0 copy-done
  12.7 1.6 %column_pack.1 = (f32[32,128]{1,0:T(8,128)S(1)}, f32[32,128]{1,0:T(8,128)S(1)}, f32[96,128]{1,0:T(8,128)S(1)}) custom-call(f32[8,96,128]{2,1,0:T(8,128)S(1)} %copy-done, f32[8,96,128]{2,1,0:T(8,128)S(1)} %copy-done.1, f32[8,96,128]{2,1,0:T(8,128)S(1)} %copy-done.2, f32[8,96,128]{2,1,0:T(8,128)S(1)} %copy-done.3, s32[8,96,128]{2,1,0:T(8,128)S(1)} %copy-done.4, ...), custom_call_target="tpu_custom_call" | custom-call | tf_op jit(solution)/shard_map/column_pack/pallas_call | solution.py:373
  14.4 0.0 copy-start.8
  14.4 0.0 collective-permute-done.from_a.lat_a
  14.4 1.0 %collective-permute-done.1.from_b.lat_b = f32[32,128]{1,0:T(8,128)S(1)} collective-permute-done((f32[32,128]{1,0:T(8,128)}, f32[32,128]{1,0:T(8,128)S(1)}, u32[]{:S(2)}, u32[]{:S(2)}) %collective-permute-start.1) | collective-permute-done | bytes 16416 | tf_op jit(solution)/shard_map/ppermute | solution.py:371
  15.4 0.1 corner_pack.1
  15.4 1.9 %collective-permute-start.2 = (f32[32,128]{1,0:T(8,128)S(1)}, f32[32,128]{1,0:T(8,128)S(1)}, u32[]{:S(2)}, u32[]{:S(2)}) collective-permute-start(f32[32,128]{1,0:T(8,128)S(1)} %get-tuple-element.16), channel_id=1, source_target_pairs={{0,16},{16,0},{32,48},{48,32},{64,80},{80,64},{96,112},{112,96},{1... | collective-permute-start | bytes 49160 | tf_op jit(solution)/shard_map/ppermute | solution.py:392
  17.4 13.0 %collective-permute-start.3 = (f32[32,128]{1,0:T(8,128)S(1)}, f32[32,128]{1,0:T(8,128)S(1)}, u32[]{:S(2)}, u32[]{:S(2)}) collective-permute-start(f32[32,128]{1,0:T(8,128)S(1)} %get-tuple-element.17), channel_id=1, source_target_pairs={{0,496},{16,32},{32,16},{48,64},{64,48},{80,96},{96,80},{112,128},... | collective-permute-start | bytes 49160 | tf_op jit(solution)/shard_map/ppermute | solution.py:391
  30.4 0.0 collective-permute-done.2.lon_a
  30.4 1.4 %collective-permute-done.3.lon_b = f32[32,128]{1,0:T(8,128)S(1)} collective-permute-done((f32[32,128]{1,0:T(8,128)S(1)}, f32[32,128]{1,0:T(8,128)S(1)}, u32[]{:S(2)}, u32[]{:S(2)}) %collective-permute-start.3) | collective-permute-done | bytes 16416 | tf_op jit(solution)/shard_map/ppermute | solution.py:391
  31.8 0.0 copy-done.8
  31.8 5.3 %step.1 = (f32[8,96,128]{2,1,0:T(8,128)}, f32[8,96,128]{2,1,0:T(8,128)}, f32[8,96,128]{2,1,0:T(8,128)}, f32[8,96,128]{2,1,0:T(8,128)}) custom-call(f32[8,96,128]{2,1,0:T(8,128)S(1)} %copy-done, f32[8,96,128]{2,1,0:T(8,128)S(1)} %copy-done.1, f32[8,96,128]{2,1,0:T(8,128)S(1)} %copy-done.2, f32[8,96,128]{2,1,0:T(8,128)S(1)} %copy-done.3, ...), custom_call_target="tpu_custom_call" | custom-call | tf_op jit(solution)/shard_map/step/pallas_call | solution.py:396
Async XLA Ops:
  0.6 12.0 %copy-start.7 = (f32[96,128]{1,0:T(8,128)S(1)}, f32[96,128]{1,0:T(8,128)}, u32[]{:S(2)}) copy-start(f32[96,128]{1,0:T(8,128)} %e2.5) | copy-start | bytes 147460
  0.6 12.0 %copy-start.6 = (f32[96,128]{1,0:T(8,128)S(1)}, f32[96,128]{1,0:T(8,128)}, u32[]{:S(2)}) copy-start(f32[96,128]{1,0:T(8,128)} %e1.5) | copy-start | bytes 147460
  0.7 12.0 %copy-start.5 = (s32[8,96,128]{2,1,0:T(8,128)S(1)}, s32[8,96,128]{2,1,0:T(8,128)}, u32[]{:S(2)}) copy-start(s32[8,96,128]{2,1,0:T(8,128)} %mf.5) | copy-start | bytes 1179652
  0.7 12.0 %copy-start.4 = (s32[8,96,128]{2,1,0:T(8,128)S(1)}, s32[8,96,128]{2,1,0:T(8,128)}, u32[]{:S(2)}) copy-start(s32[8,96,128]{2,1,0:T(8,128)} %zf.5) | copy-start | bytes 1179652
  0.7 12.0 %copy-start.3 = (f32[8,96,128]{2,1,0:T(8,128)S(1)}, f32[8,96,128]{2,1,0:T(8,128)}, u32[]{:S(2)}) copy-start(f32[8,96,128]{2,1,0:T(8,128)} %v.5) | copy-start | bytes 1179652
  0.7 12.0 %copy-start.2 = (f32[8,96,128]{2,1,0:T(8,128)S(1)}, f32[8,96,128]{2,1,0:T(8,128)}, u32[]{:S(2)}) copy-start(f32[8,96,128]{2,1,0:T(8,128)} %u.5) | copy-start | bytes 1179652
  0.7 12.0 %copy-start.1 = (f32[8,96,128]{2,1,0:T(8,128)S(1)}, f32[8,96,128]{2,1,0:T(8,128)}, u32[]{:S(2)}) copy-start(f32[8,96,128]{2,1,0:T(8,128)} %s.5) | copy-start | bytes 1179652
  0.7 12.0 %copy-start = (f32[8,96,128]{2,1,0:T(8,128)S(1)}, f32[8,96,128]{2,1,0:T(8,128)}, u32[]{:S(2)}) copy-start(f32[8,96,128]{2,1,0:T(8,128)} %t.5) | copy-start | bytes 1179652
  2.5 11.8 %collective-permute-start = (f32[32,128]{1,0:T(8,128)}, f32[32,128]{1,0:T(8,128)S(1)}, u32[]{:S(2)}, u32[]{:S(2)}) collective-permute-start(f32[32,128]{1,0:T(8,128)} %get-tuple-element.13), channel_id=1, source_target_pairs={{0,1},{1,0},{2,3},{3,2},{4,5},{5,4},{6,7},{7,6},{8,9},{9,8},{10,11... | collective-permute-start | bytes 49160 | tf_op jit(solution)/shard_map/ppermute | solution.py:370
  6.8 8.5 %collective-permute-start.1 = (f32[32,128]{1,0:T(8,128)}, f32[32,128]{1,0:T(8,128)S(1)}, u32[]{:S(2)}, u32[]{:S(2)}) collective-permute-start(f32[32,128]{1,0:T(8,128)} %get-tuple-element.14), channel_id=1, source_target_pairs={{1,2},{2,1},{3,4},{4,3},{5,6},{6,5},{7,8},{8,7},{9,10},{10,9},{11,... | collective-permute-start | bytes 49160 | tf_op jit(solution)/shard_map/ppermute | solution.py:371
  14.4 17.5 %copy-start.8 = (s32[96,128]{1,0:T(8,128)S(1)}, s32[96,128]{1,0:T(8,128)}, u32[]{:S(2)}) copy-start(s32[96,128]{1,0:T(8,128)} %count.1) | copy-start | bytes 147460
  15.4 15.0 %collective-permute-start.2 = (f32[32,128]{1,0:T(8,128)S(1)}, f32[32,128]{1,0:T(8,128)S(1)}, u32[]{:S(2)}, u32[]{:S(2)}) collective-permute-start(f32[32,128]{1,0:T(8,128)S(1)} %get-tuple-element.16), channel_id=1, source_target_pairs={{0,16},{16,0},{32,48},{48,32},{64,80},{80,64},{96,112},{112,96},{1... | collective-permute-start | bytes 49160 | tf_op jit(solution)/shard_map/ppermute | solution.py:392
  17.4 14.5 %collective-permute-start.3 = (f32[32,128]{1,0:T(8,128)S(1)}, f32[32,128]{1,0:T(8,128)S(1)}, u32[]{:S(2)}, u32[]{:S(2)}) collective-permute-start(f32[32,128]{1,0:T(8,128)S(1)} %get-tuple-element.17), channel_id=1, source_target_pairs={{0,496},{16,32},{32,16},{48,64},{64,48},{80,96},{96,80},{112,128},... | collective-permute-start | bytes 49160 | tf_op jit(solution)/shard_map/ppermute | solution.py:391

commit v3 on v2

v3 whole, which is shorter than its diff:
```python
import functools
import math

import jax
import jax.numpy as jnp
from jax import lax
from jax.experimental import pallas as pl
from jax.experimental.pallas import tpu as pltpu
from jax.sharding import PartitionSpec as P

GRAVITY = 9.81
REFERENCE_DENSITY = 1026.0
TIME_STEP = 360.0
LATERAL = 300.0
VERTICAL = 0.001
ROTATION = 7.292e-05

LEVELS = 8
LANES = 128
TILE = 8
PACKET = 4 * LEVELS
CHUNKS = 3
VMEM = pltpu.MemorySpace.VMEM

THICK = [6.0 + 4.0 * k for k in range(LEVELS)]
DEPTH = [2.0 * k * k + 6.0 * k + 3.0 for k in range(LEVELS)]
SPACING = [4.0 * k + 4.0 for k in range(LEVELS)]


def lane_index(shape):
    return lax.broadcasted_iota(jnp.int32, shape, len(shape) - 1)


def roll_lanes(x, shift):
    return pltpu.roll(x, shift % LANES, x.ndim - 1)


def density(heat, salt, k):
    anom_t = heat - 10.0
    anom_s = salt - 35.0
    by_t = -0.1655 * (1.0 + 0.0001497 * DEPTH[k])
    by_s = 0.76554 * (1.0 - 1.109e-05 * DEPTH[k])
    along_t = by_t + (-0.1655 * 0.5 * 0.05952) * anom_t - 0.0024341 * anom_s
    along_s = by_s - (0.76554 * 0.5 * 0.00054914) * anom_s
    return along_t * anom_t + along_s * anom_s


def row_pack(t, s, u, v, zf, mf, e1, e2, to_a, to_b, deep, flags, flat, arrived):
    j = lax.axis_index("lat")
    even = j % 2 == 0
    top = j == lax.axis_size("lat") - 1
    last = TILE - 1
    low, high = pl.ds(0, TILE), pl.ds(t.shape[1] - TILE, TILE)
    wanted = [(t, low), (t, high), (s, low), (s, high), (u, low), (u, high), (v, high)]
    marks = [(zf, low), (zf, high), (mf, high)]
    sizes = [(e1, high), (e2, high), (e2, low)]
    copies = [pltpu.make_async_copy(ref.at[:, rows, :], deep.at[n], arrived.at[n]) for n, (ref, rows) in enumerate(wanted)]
    copies += [pltpu.make_async_copy(ref.at[:, rows, :], flags.at[n], arrived.at[7 + n]) for n, (ref, rows) in enumerate(marks)]
    copies += [pltpu.make_async_copy(ref.at[rows, :], flat.at[n], arrived.at[10 + n]) for n, (ref, rows) in enumerate(sizes)]
    for copy in copies:
        copy.start()
    for copy in copies:
        copy.wait()

    def put(out, fields):
        for number, field in enumerate(fields):
            out[number * LEVELS : (number + 1) * LEVELS, :] = field

    def upward():
        spacing_x, spacing_y = flat[0, last:, :], flat[1, last:, :]
        face = flags[2, :, last, :].astype(jnp.float32)
        return [
            deep[1, :, last, :],
            deep[3, :, last, :],
            spacing_x * deep[6, :, last, :] * face,
            LATERAL * spacing_x / spacing_y * face,
        ]

    def downward():
        flux = flat[2, :1, :] * deep[4, :, 0, :] * flags[0, :, 0, :].astype(jnp.float32)
        return [deep[0, :, 0, :], deep[2, :, 0, :], flux, jnp.zeros_like(flux)]

    @pl.when(even)
    def _():
        put(to_a, upward())
        put(to_b, downward())

    @pl.when(jnp.logical_not(even))
    def _():
        put(to_a, downward())

    @pl.when(jnp.logical_not(even) & jnp.logical_not(top))
    def _():
        put(to_b, upward())

    @pl.when(top)
    def _():
        flux = flat[1, last:, :] * deep[5, :, last, :] * flags[1, :, last, :].astype(jnp.float32)
        rows = jnp.concatenate([deep[1, :, last, :], deep[3, :, last, :], -flux], axis=0)
        shape = (LANES, LANES)
        mirror = lane_index(shape) + lax.broadcasted_iota(jnp.int32, shape, 0) == LANES - 1
        to_b[: 3 * LEVELS, :] = lax.dot(
            rows, mirror.astype(jnp.float32), precision=lax.Precision.HIGHEST, preferred_element_type=jnp.float32
        )
        to_b[3 * LEVELS :, :] = jnp.zeros((LEVELS, LANES), jnp.float32)


def from_west(x):
    return jnp.where(lane_index(x.shape) == 0, 0.0, roll_lanes(x, 1))


def from_east(x):
    return jnp.where(lane_index(x.shape) == LANES - 1, 0.0, roll_lanes(x, -1))


def front(
    t, s, u, v, zf, mf, count, e1, e2,
    to_east, to_west, own, coriolis, p_ext, a_ext, b_ext, u_ext, v_ext, ft_ext, fs_ext, packed,
):
    lines = t.shape[1]
    tiles = lines // TILE
    lane = lane_index((TILE, LANES))
    first_row = lax.axis_index("lat") * lines
    total_rows = lines * lax.axis_size("lat")
    packed[pl.ds(lines, LANES - lines), :] = jnp.zeros((LANES - lines, LANES), jnp.float32)

    def pack(r, _):
        rows = pl.ds(pl.multiple_of(r * TILE, TILE), TILE)
        spacing_x, spacing_y = e1[rows, :], e2[rows, :]
        ratio = LATERAL * spacing_y / spacing_x
        levels = count[rows, :].astype(jnp.float32)
        row = (first_row + r * TILE + lax.broadcasted_iota(jnp.int32, (TILE, LANES), 0)).astype(jnp.float32)
        latitude = 10.0 + 78.0 * (row + 0.5) / total_rows
        turn = 2.0 * ROTATION * jnp.sin(latitude * (math.pi / 180.0))
        coriolis[rows, :] = turn
        fields = [jnp.zeros((TILE, LANES), jnp.float32) for _ in range(8)]

        def keep(number, k, x, source):
            target = number * LEVELS + k
            fields[number] = jnp.where(lane == target, roll_lanes(x, target - source), fields[number])

        for k in range(LEVELS):
            heat, salt = t[k, rows, :], s[k, rows, :]
            face_x, face_y = zf[k, rows, :].astype(jnp.float32), mf[k, rows, :].astype(jnp.float32)
            keep(0, k, heat, LANES - 1)
            keep(1, k, salt, LANES - 1)
            keep(2, k, spacing_y * u[k, rows, :] * face_x, LANES - 1)
            keep(3, k, ratio * face_x, LANES - 1)
            keep(4, k, heat, 0)
            keep(5, k, salt, 0)
            keep(6, k, spacing_x * v[k, rows, :] * face_y, 0)
            keep(7, k, face_y, 0)
        total = jnp.where(lane == 70, turn, 0.0)
        for n, (x, source) in enumerate(
            [(spacing_x, LANES - 1), (spacing_y, LANES - 1), (levels, LANES - 1), (spacing_x, 0), (spacing_y, 0), (levels, 0)]
        ):
            total = jnp.where(lane == 64 + n, roll_lanes(x, 64 + n - source), total)
        for field in fields:
            total = total + field
        packed[rows, :] = total
        return 0

    lax.fori_loop(0, tiles, pack, 0, unroll=4)
    turned = packed[...].T
    to_east[...] = turned[:PACKET]
    to_west[...] = turned[PACKET : 2 * PACKET]
    own[...] = turned[: own.shape[0]]

    def heads(r, _):
        source = pl.ds(pl.multiple_of(r * TILE, TILE), TILE)
        rows = pl.ds(pl.multiple_of(r * TILE + TILE, TILE), TILE)
        head = jnp.zeros((TILE, LANES), jnp.float32)
        for k in range(LEVELS):
            half = (0.5 * THICK[k]) * density(t[k, source, :], s[k, source, :], k)
            p_ext[k, rows, :] = head + half
            head = head + 2.0 * half
        return 0

    lax.fori_loop(0, tiles, heads, 0, unroll=2)

    def faces(r, _, last=False):
        source = pl.ds(pl.multiple_of(r * TILE, TILE), TILE)
        rows = pl.ds(pl.multiple_of(r * TILE + TILE, TILE), TILE)
        above = pl.ds(r * TILE + 1, TILE)
        spacing_x, spacing_y = e1[source, :], e2[source, :]
        ratio = LATERAL * spacing_x / spacing_y
        for k in range(LEVELS):
            flux_x = spacing_y * u[k, source, :] * zf[k, source, :].astype(jnp.float32)
            u_ext[k, rows, :] = flux_x
            a_ext[k, rows, :] = flux_x + from_west(flux_x)
            face = mf[k, source, :].astype(jnp.float32)
            flux_y = spacing_x * v[k, source, :] * face
            v_ext[k, rows, :] = flux_y
            b_ext[k, rows, :] = flux_y + from_east(flux_y)
            if not last:
                here, there = 0.5 * flux_y + ratio * face, 0.5 * flux_y - ratio * face
                ft_ext[k, rows, :] = here * t[k, source, :] + there * t[k, above, :]
                fs_ext[k, rows, :] = here * s[k, source, :] + there * s[k, above, :]
        return 0

    lax.fori_loop(0, tiles - 1, faces, 0)
    faces(tiles - 1, 0, last=True)


def corner_pack(from_a, from_b, to_east, to_west, to_a, to_b):
    even_j = lax.axis_index("lat") % 2 == 0
    even_i = lax.axis_index("lon") % 2 == 0
    shape = (PACKET, LANES)
    row = lax.broadcasted_iota(jnp.int32, shape, 0)
    corner = (lane_index(shape) == 96) & (row >= 2 * LEVELS) & (row < 3 * LEVELS)
    first, second = from_a[...], from_b[...]
    north = jnp.where(even_j, first, second)
    south = jnp.where(even_j, second, first)
    east = jnp.where(corner, roll_lanes(north, 96 - (LANES - 1)), to_east[...])
    west = jnp.where(corner, roll_lanes(south, 96), to_west[...])
    to_a[...] = jnp.where(even_i, east, west)
    to_b[...] = jnp.where(even_i, west, east)


def middle(
    t, s, u, v, zf, mf, count, e1, e2, coriolis, p_ext, a_ext, b_ext, u_ext, v_ext, ft_ext, fs_ext, lat_a, lat_b,
    t_out, s_out, u_out, v_out, beyond,
):
    lines = t.shape[1]
    tiles = lines // TILE
    even_j = lax.axis_index("lat") % 2 == 0

    def pick(ref_true, ref_false, flag, number):
        rows = slice(number * LEVELS, (number + 1) * LEVELS)
        return jnp.where(flag, ref_true[rows, :], ref_false[rows, :])

    north = [pick(lat_a, lat_b, even_j, n) for n in range(3)]
    south = [pick(lat_b, lat_a, even_j, n) for n in range(4)]
    here, there = 0.5 * south[2] + south[3], 0.5 * south[2] - south[3]
    beyond[0] = north[0]
    beyond[1] = north[1]
    beyond[2] = north[2] + from_west(north[2])
    beyond[4] = south[2] + from_east(south[2])
    beyond[5] = south[2]
    beyond[6] = here * south[0] + there * t[:, 0, :]
    beyond[7] = here * south[1] + there * s[:, 0, :]
    head = jnp.zeros((1, LANES), jnp.float32)
    for k in range(LEVELS):
        half = (0.5 * THICK[k]) * density(beyond[0, k : k + 1, :], beyond[1, k : k + 1, :], k)
        beyond[3, k : k + 1, :] = head + half
        head = head + 2.0 * half

    row = lax.broadcasted_iota(jnp.int32, (TILE, LANES), 0)

    def update(r, _, first=False, last=False):
        source = pl.ds(pl.multiple_of(r * TILE, TILE), TILE)
        rows = pl.ds(pl.multiple_of(r * TILE + TILE, TILE), TILE)
        spacing_x, spacing_y = e1[source, :], e2[source, :]
        levels = count[source, :]
        inverse_x, inverse_y = 1.0 / spacing_x, 1.0 / spacing_y
        ratio_x, ratio_y = LATERAL * spacing_y * inverse_x, LATERAL * spacing_x * inverse_y
        area = spacing_x * spacing_y
        per_area = TIME_STEP * inverse_x * inverse_y
        turn = (0.25 * TIME_STEP) * coriolis[source, :]
        turn_x, turn_y = turn * inverse_x, turn * inverse_y
        push = -TIME_STEP * GRAVITY / REFERENCE_DENSITY
        push_x, push_y = push * inverse_x, push * inverse_y
        zero = jnp.zeros((TILE, LANES), jnp.float32)

        def above(ref, k, number, offset=TILE):
            if last:
                return jnp.where(row == TILE - 1, beyond[number, k : k + 1, :], pltpu.roll(ref[k, pl.ds(r * TILE + offset, TILE), :], TILE - 1, 0))
            return ref[k, pl.ds(r * TILE + offset + 1, TILE), :]

        def below(ref, k, number):
            if first:
                return jnp.where(row == 0, beyond[number, k : k + 1, :], pltpu.roll(ref[k, rows, :], 1, 0))
            return ref[k, pl.ds(r * TILE + TILE - 1, TILE), :]

        upward, t_below, s_below, u_below, v_below = zero, zero, zero, zero, zero
        for k in reversed(range(LEVELS)):
            heat, salt = t[k, source, :], s[k, source, :]
            flux_x, flux_y = u_ext[k, rows, :], v_ext[k, rows, :]
            face_x, face_y = zf[k, source, :].astype(jnp.float32), mf[k, source, :].astype(jnp.float32)
            both_x, both_y = a_ext[k, rows, :], b_ext[k, rows, :]
            wet = levels > k
            spread = ratio_x * face_x
            here, there = 0.5 * flux_x + spread, 0.5 * flux_x - spread
            t_east = here * heat + there * from_east(heat)
            s_east = here * salt + there * from_east(salt)
            if last:
                here, there = 0.5 * flux_y + ratio_y * face_y, 0.5 * flux_y - ratio_y * face_y
                t_north, s_north = here * heat + there * above(t, k, 0, 0), here * salt + there * above(s, k, 1, 0)
                under = pl.ds(r * TILE + TILE - 1, 1)
                t_south = jnp.where(row == 0, ft_ext[k, under, :], pltpu.roll(t_north, 1, 0))
                s_south = jnp.where(row == 0, fs_ext[k, under, :], pltpu.roll(s_north, 1, 0))
            else:
                t_north, s_north = ft_ext[k, rows, :], fs_ext[k, rows, :]
                t_south, s_south = below(ft_ext, k, 6), below(fs_ext, k, 7)
            t_net = t_east - from_west(t_east) + t_north - t_south
            s_net = s_east - from_west(s_east) + s_north - s_south
            converge = 2.0 * flux_x - both_x + flux_y - below(v_ext, k, 5)
            upward = upward - THICK[k] * converge
            if k > 0:
                mix = jnp.where(wet, (VERTICAL / SPACING[k]) * area, 0.0)
                upper, lower = 0.5 * upward - mix, 0.5 * upward + mix
                t_above = upper * t[k - 1, source, :] + lower * heat
                s_above = upper * s[k - 1, source, :] + lower * salt
            else:
                t_above, s_above = upward * heat, upward * salt
            t_net = t_net + (t_above - t_below) * (1.0 / THICK[k])
            s_net = s_net + (s_above - s_below) * (1.0 / THICK[k])
            t_below, s_below = t_above, s_above
            t_out[k, source, :] = jnp.where(wet, heat - per_area * t_net, 0.0)
            s_out[k, source, :] = jnp.where(wet, salt - per_area * s_net, 0.0)
            zonal, meridional = u[k, source, :], v[k, source, :]
            if k > 0:
                u_above = (VERTICAL / SPACING[k]) * (u[k - 1, source, :] - zonal) * face_x
                v_above = (VERTICAL / SPACING[k]) * (v[k - 1, source, :] - meridional) * face_y
            else:
                u_above, v_above = zero, zero
            head = p_ext[k, rows, :]
            slope_x = from_east(head) - head
            slope_y = above(p_ext, k, 3) - head
            share = TIME_STEP / THICK[k]
            u_out[k, source, :] = (
                zonal + push_x * slope_x + turn_x * (both_y + below(b_ext, k, 4)) + share * (u_above - u_below)
            ) * face_x
            v_out[k, source, :] = (
                meridional + push_y * slope_y - turn_y * (both_x + above(a_ext, k, 2)) + share * (v_above - v_below)
            ) * face_y
            u_below, v_below = u_above, v_above
        return 0

    update(0, 0, first=True)
    lax.fori_loop(1, tiles - 1, update, 0)
    update(tiles - 1, 0, last=True)


def running_sum(x, level, upward):
    for step in (1, 2, 4):
        if upward:
            x = x + jnp.where(level < LEVELS - step, pltpu.roll(x, LEVELS - step, 0), 0.0)
        else:
            x = x + jnp.where(level >= step, pltpu.roll(x, step, 0), 0.0)
    return x


def finish(t_part, s_part, u_part, v_part, own, lon_a, lon_b, t_out, s_out, u_out, v_out, turned, sides, *buffers_and_done):
    buffers, done = buffers_and_done[:4], buffers_and_done[4]
    lines = t_part.shape[1]
    even_i = lax.axis_index("lon") % 2 == 0

    def pick(ref_true, ref_false, flag, number):
        rows = slice(number * LEVELS, (number + 1) * LEVELS)
        return jnp.where(flag, ref_true[rows, :], ref_false[rows, :])

    t_east, s_east, v_east = [pick(lon_a, lon_b, even_i, n) for n in range(3)]
    t_west, s_west, u_west, g_west = [pick(lon_b, lon_a, even_i, n) for n in range(4)]
    shape = (LEVELS, LANES)
    level, lane = lax.broadcasted_iota(jnp.int32, shape, 0), lane_index(shape)
    depth_index = level.astype(jnp.float32)
    thick = 6.0 + 4.0 * depth_index
    depth = 2.0 * depth_index * depth_index + 6.0 * depth_index + 3.0

    def mine(number):
        return own[number * LEVELS : (number + 1) * LEVELS, :]

    def single(number):
        return own[64 + number : 65 + number, :]

    u_last, g_last, t_first, s_first, face_first = mine(2), mine(3), mine(4), mine(5), mine(7)
    turn = (0.25 * TIME_STEP) * single(6)
    push = -TIME_STEP * GRAVITY / REFERENCE_DENSITY
    inverse_x, inverse_y = 1.0 / single(0), 1.0 / single(1)
    wet = depth_index < single(2)
    back = jnp.where(wet, -(TIME_STEP * inverse_x * inverse_y) * (0.5 * u_last - g_last), 0.0)
    anom_t, anom_s = t_east - 10.0, s_east - 35.0
    weight = 0.5 * thick * (
        (-0.1655 * (1.0 + 0.0001497 * depth) + (-0.1655 * 0.5 * 0.05952) * anom_t - 0.0024341 * anom_s) * anom_t
        + (0.76554 * (1.0 - 1.109e-05 * depth) - (0.76554 * 0.5 * 0.00054914) * anom_s) * anom_s
    )
    head = 2.0 * running_sum(weight, level, False) - weight
    v_south_east = jnp.where(lane == 0, roll_lanes(v_east, -lines), roll_lanes(v_east, 1))
    u_add = jnp.where(g_last > 0.0, (push * inverse_x) * head + (turn * inverse_x) * (v_east + v_south_east), 0.0)
    turned[...] = jnp.zeros_like(turned)
    turned[pl.ds(0, LEVELS, 2), :] = back * t_east
    turned[pl.ds(16, LEVELS, 2), :] = back * s_east
    turned[pl.ds(32, LEVELS, 2), :] = u_add
    inverse_x, inverse_y = 1.0 / single(3), 1.0 / single(4)
    wet = depth_index < single(5)
    scale = jnp.where(wet, -(TIME_STEP * inverse_x * inverse_y), 0.0)
    here, there = 0.5 * u_west + g_west, 0.5 * u_west - g_west
    upward = running_sum(0.5 * thick * u_west, level, True)

    def first_column(q_west, q):
        flux = upward * (q + jnp.where(level == 0, q, pltpu.roll(q, 1, 0)))
        under = jnp.where(level == LEVELS - 1, 0.0, pltpu.roll(flux, LEVELS - 1, 0))
        return scale * ((flux - under) / thick - (here * q_west + there * q))

    turned[pl.ds(1, LEVELS, 2), :] = first_column(t_west, t_first)
    turned[pl.ds(17, LEVELS, 2), :] = first_column(s_west, s_first)
    turned[pl.ds(33, LEVELS, 2), :] = -(turn * inverse_y) * (u_west + roll_lanes(u_west, -1)) * face_first
    sides[...] = turned[...].T

    at_first, at_last = lane == 0, lane == LANES - 1
    at_side = at_first | at_last
    parts, outs = (t_part, s_part, u_part, v_part), (t_out, s_out, u_out, v_out)
    chunk = lines // CHUNKS
    copies = []
    for c in range(CHUNKS):

        def tile(r, _):
            rows = pl.ds(pl.multiple_of(r * TILE, TILE), TILE)
            side = sides[rows, :]
            for k in range(LEVELS):
                both = roll_lanes(side, -(2 * k + 33))
                adds = (
                    jnp.where(at_side, roll_lanes(side, -(2 * k + 1)), 0.0),
                    jnp.where(at_side, roll_lanes(side, -(2 * k + 17)), 0.0),
                    jnp.where(at_last, both, 0.0),
                    jnp.where(at_first, both, 0.0),
                )
                for part, add, buffer in zip(parts, adds, buffers):
                    buffer[k, rows, :] = part[k, rows, :] + add
            return 0

        lax.fori_loop(c * chunk // TILE, (c + 1) * chunk // TILE, tile, 0)
        rows = pl.ds(c * chunk, chunk)
        for n in range(4):
            copy = pltpu.make_async_copy(buffers[n].at[:, rows, :], outs[n].at[:, rows, :], done.at[c * 4 + n])
            copy.start()
            copies.append(copy)
    for copy in copies:
        copy.wait()


def whole(n):
    return [pl.BlockSpec(memory_space=VMEM)] * n


def per_device(
    potential_warmth_degrees,
    dissolved_salt_content,
    zonal_edge_current,
    meridional_edge_current,
    wet_grid_flag,
    zonal_wet_edge_flag,
    meridional_wet_edge_flag,
    bottom_tier_count,
    zonal_grid_spacing,
    meridional_grid_spacing,
):
    t, s, u, v = potential_warmth_degrees, dissolved_salt_content, zonal_edge_current, meridional_edge_current
    zf, mf, e1, e2 = zonal_wet_edge_flag, meridional_wet_edge_flag, zonal_grid_spacing, meridional_grid_spacing
    lines = t.shape[1]
    lons, lats = lax.axis_size("lon"), lax.axis_size("lat")
    f32 = jnp.float32
    params = pltpu.CompilerParams(vmem_limit_bytes=24 * 1024 * 1024)
    packet = jax.ShapeDtypeStruct((PACKET, LANES), f32)
    field = jax.ShapeDtypeStruct(t.shape, f32)

    lat_to_a, lat_to_b = pl.pallas_call(
        row_pack,
        in_specs=[pl.BlockSpec(memory_space=pl.ANY)] * 8,
        out_specs=whole(2),
        out_shape=[packet, packet],
        scratch_shapes=[
            VMEM((7, LEVELS, TILE, LANES), f32),
            VMEM((3, LEVELS, TILE, LANES), jnp.int32),
            VMEM((3, TILE, LANES), f32),
            pltpu.SemaphoreType.DMA((13,)),
        ],
        name="row_pack",
    )(t, s, u, v, zf, mf, e1, e2)

    pairs_a = [(j, j ^ 1) for j in range(lats)]
    pairs_b = []
    for i in range(lons):
        for j in range(1, lats):
            other = (lons - 1 - i) * lats + j if j == lats - 1 else i * lats + (j + 1 if j % 2 else j - 1)
            pairs_b.append((i * lats + j, other))
    lat_a = lax.ppermute(lat_to_a, "lat", pairs_a)
    lat_b = lax.ppermute(lat_to_b, ("lon", "lat"), pairs_b)

    extended = jax.ShapeDtypeStruct((LEVELS, lines + 2 * TILE, LANES), f32)
    square = VMEM((LANES, LANES), f32)
    to_east, to_west, own, coriolis, *parts = pl.pallas_call(
        front,
        in_specs=whole(9),
        out_specs=whole(11),
        out_shape=[packet, packet, jax.ShapeDtypeStruct((72, LANES), f32), jax.ShapeDtypeStruct(e1.shape, f32)] + [extended] * 7,
        scratch_shapes=[square],
        compiler_params=params,
        name="front",
    )(t, s, u, v, zf, mf, bottom_tier_count, e1, e2)

    lon_to_a, lon_to_b = pl.pallas_call(
        corner_pack,
        in_specs=whole(4),
        out_specs=whole(2),
        out_shape=[packet, packet],
        compiler_params=params,
        name="corner_pack",
    )(lat_a, lat_b, to_east, to_west)
    lon_b = lax.ppermute(lon_to_b, "lon", [(i, (i + 1 if i % 2 else i - 1) % lons) for i in range(lons)])
    lon_a = lax.ppermute(lon_to_a, "lon", [(i, i ^ 1) for i in range(lons)])

    parts = pl.pallas_call(
        middle,
        in_specs=whole(19),
        out_specs=whole(4),
        out_shape=[field] * 4,
        scratch_shapes=[VMEM((8, LEVELS, LANES), f32)],
        compiler_params=params,
        name="middle",
    )(t, s, u, v, zf, mf, bottom_tier_count, e1, e2, coriolis, *parts, lat_a, lat_b)

    return pl.pallas_call(
        finish,
        in_specs=whole(7),
        out_specs=[pl.BlockSpec(memory_space=pltpu.MemorySpace.HBM)] * 4,
        out_shape=[field] * 4,
        scratch_shapes=[square] * 2 + [VMEM(t.shape, f32)] * 4 + [pltpu.SemaphoreType.DMA((4 * CHUNKS,))],
        compiler_params=params,
        name="finish",
    )(*parts, own, lon_a, lon_b)


def solution(mesh):
    deep, flat = P(None, "lat", "lon"), P("lat", "lon")
    return jax.shard_map(
        per_device,
        mesh=mesh,
        in_specs=(deep,) * 7 + (flat,) * 3,
        out_specs=(deep,) * 4,
        check_vma=False,
    )
```

time: 37.4 us -> 35.5 us (0.949)
  the two profiles are of different devices: /device:TPU:6 before, /device:TPU:198 now
where the time goes in v3:
time: 35.5 us; the launch traced here: 35.2 us
  starting transfers between devices  23.1 us (65%)
  Pallas kernels  9.06 us (26%)
  waiting for transfers between devices  1.32 us (4%)
  between operations  0.86 us (2%)
  local copies, waits for them, and re-layouts  0.83 us (2%)
    ppermute x1, starting transfers between devices, per_device(): lat_b = lax.ppermute(lat_to_b, ('lon', 'lat'), pairs_b)  10.7 us
    ppermute x1, starting transfers between devices, per_device(): lax.ppermute(lon_to_b, 'lon', [(i, (i + 1 if i % 2 else i - 1) % lons) fo...  7.64 us
    ppermute x1, starting transfers between devices, per_device(): lon_a = lax.ppermute(lon_to_a, 'lon', [(i, i ^ 1) for i in range(lons)])  2.85 us
    pallas_call x1, Pallas kernels, per_device(): pl.pallas_call(front, in_specs=whole(9), out_specs=whole(11), out_shape=[...  2.7 us
    pallas_call x1, Pallas kernels, per_device(): pl.pallas_call(finish, in_specs=whole(7), out_specs=[pl.BlockSpec(memory_...  2.21 us
    pallas_call x1, Pallas kernels, per_device(): pl.pallas_call(middle, in_specs=whole(19), out_specs=whole(4), out_shape=...  2.09 us
    pallas_call x1, Pallas kernels, per_device(): pl.pallas_call(row_pack, in_specs=[pl.BlockSpec(memory_space=pl.ANY)] * 8...  1.98 us
    ppermute x1, starting transfers between devices, per_device(): lat_a = lax.ppermute(lat_to_a, 'lat', pairs_a)  1.92 us
  transfers between devices with their start and end apart: 4, of which 1 were waited for; matrix products, arithmetic and copies ran while one was open for 0% of the time, Pallas kernels for 14%

profile of v3, /device:TPU:198, one launch (start us, length us, event | category | flops | bytes accessed | tf_op | source)
XLA Modules:
  0.0 35.2 jit_solution(2862517399422595608)
XLA Ops:
  0.6 0.0 copy-start.7
  0.6 0.0 copy-start.6
  0.7 0.0 copy-start.5
  0.7 0.0 copy-start.4
  0.7 0.0 copy-start.3
  0.7 0.0 copy-start.2
  0.7 0.0 copy-start.1
  0.7 0.0 copy-start
  0.7 2.0 %row_pack.1 = (f32[32,128]{1,0:T(8,128)}, f32[32,128]{1,0:T(8,128)}) custom-call(f32[8,96,128]{2,1,0:T(8,128)} %t.5, f32[8,96,128]{2,1,0:T(8,128)} %s.5, f32[8,96,128]{2,1,0:T(8,128)} %u.5, f32[8,96,128]{2,1,0:T(8,128)} %v.5, s32[8,96,128]{2,1,0:T(8,128)} %zf.5, s32[8,96,128]{2,1,0:T(8,128)} %mf.5, f32[96,128]{1,0:T(8,128)} %e1.5, f32[96,128]{1,0:T(8,128)} %e2.5), custom_call_target="tpu_custom_call" | custom-call | tf_op jit(solution)/shard_map/row_pack/pallas_call | solution.py:458
  2.7 1.9 %collective-permute-start = (f32[32,128]{1,0:T(8,128)}, f32[32,128]{1,0:T(8,128)S(1)}, u32[]{:S(2)}, u32[]{:S(2)}) collective-permute-start(f32[32,128]{1,0:T(8,128)} %get-tuple-element.31), channel_id=1, source_target_pairs={{0,1},{1,0},{2,3},{3,2},{4,5},{5,4},{6,7},{7,6},{8,9},{9,8},{10,11... | collective-permute-start | bytes 49160 | tf_op jit(solution)/shard_map/ppermute | solution.py:478
  4.6 10.7 %collective-permute-start.1 = (f32[32,128]{1,0:T(8,128)}, f32[32,128]{1,0:T(8,128)S(1)}, u32[]{:S(2)}, u32[]{:S(2)}) collective-permute-start(f32[32,128]{1,0:T(8,128)} %get-tuple-element.32), channel_id=1, source_target_pairs={{1,2},{2,1},{3,4},{4,3},{5,6},{6,5},{7,8},{8,7},{9,10},{10,9},{11,... | collective-permute-start | bytes 49160 | tf_op jit(solution)/shard_map/ppermute | solution.py:479
  15.3 0.0 copy-done.7
  15.3 0.0 copy-done.6
  15.3 0.0 copy-done.5
  15.3 0.0 copy-done.4
  15.3 0.0 copy-done.3
  15.3 0.0 copy-done.2
  15.4 0.0 copy-done.1
  15.4 0.0 copy-done
  15.4 0.0 copy-start.8
  15.4 0.8 %copy-done.8 = s32[96,128]{1,0:T(8,128)S(1)} copy-done((s32[96,128]{1,0:T(8,128)S(1)}, s32[96,128]{1,0:T(8,128)}, u32[]{:S(2)}) %copy-start.8) | copy-done | bytes 49176
  16.2 2.7 %front.1 = (f32[32,128]{1,0:T(8,128)S(1)}, f32[32,128]{1,0:T(8,128)S(1)}, f32[72,128]{1,0:T(8,128)S(1)}, f32[96,128]{1,0:T(8,128)S(1)}, f32[8,112,128]{2,1,0:T(8...) custom-call(f32[8,96,128]{2,1,0:T(8,128)S(1)} %copy-done, ...), custom_call_target="tpu_custom_call" | custom-call | tf_op jit(solution)/shard_map/front/pallas_call | solution.py:483
  18.9 0.0 copy-start.9
  18.9 0.0 collective-permute-done.lat_a.from_a
  18.9 0.0 collective-permute-done.1.lat_b.from_b
  18.9 0.1 corner_pack.1
  19.0 2.9 %collective-permute-start.2 = (f32[32,128]{1,0:T(8,128)S(1)}, f32[32,128]{1,0:T(8,128)S(1)}, u32[]{:S(2)}, u32[]{:S(2)}) collective-permute-start(f32[32,128]{1,0:T(8,128)S(1)} %get-tuple-element.40), channel_id=1, source_target_pairs={{0,16},{16,0},{32,48},{48,32},{64,80},{80,64},{96,112},{112,96},{1... | collective-permute-start | bytes 49160 | tf_op jit(solution)/shard_map/ppermute | solution.py:502
  21.9 7.6 %collective-permute-start.3 = (f32[32,128]{1,0:T(8,128)S(1)}, f32[32,128]{1,0:T(8,128)S(1)}, u32[]{:S(2)}, u32[]{:S(2)}) collective-permute-start(f32[32,128]{1,0:T(8,128)S(1)} %get-tuple-element.41), channel_id=1, source_target_pairs={{0,496},{16,32},{32,16},{48,64},{64,48},{80,96},{96,80},{112,128},... | collective-permute-start | bytes 49160 | tf_op jit(solution)/shard_map/ppermute | solution.py:501
  29.5 0.0 copy-done.9
  29.5 2.1 %middle.1 = (f32[8,96,128]{2,1,0:T(8,128)S(1)}, f32[8,96,128]{2,1,0:T(8,128)S(1)}, f32[8,96,128]{2,1,0:T(8,128)S(1)}, f32[8,96,128]{2,1,0:T(8,128)S(1)}) custom-call(f32[8,96,128]{2,1,0:T(8,128)S(1)} %copy-done, f32[8,96,128]{2,1,0:T(8,128)S(1)} %copy-done.1, f32[8,96,128]{2,1,0:T(8,128)S(1)} %copy-done.2, f32[8,96,128]{2,1,0:T(8,128)S(1)} %copy-done.3, ...), custom_call_target="tpu_custom_call" | custom-call | tf_op jit(solution)/shard_map/middle/pallas_call | solution.py:504
  31.6 0.0 collective-permute-done.2.lon_a
  31.6 1.3 %collective-permute-done.3.lon_b = f32[32,128]{1,0:T(8,128)S(1)} collective-permute-done((f32[32,128]{1,0:T(8,128)S(1)}, f32[32,128]{1,0:T(8,128)S(1)}, u32[]{:S(2)}, u32[]{:S(2)}) %collective-permute-start.3) | collective-permute-done | bytes 16416 | tf_op jit(solution)/shard_map/ppermute | solution.py:501
  32.9 2.2 %finish.1 = (f32[8,96,128]{2,1,0:T(8,128)}, f32[8,96,128]{2,1,0:T(8,128)}, f32[8,96,128]{2,1,0:T(8,128)}, f32[8,96,128]{2,1,0:T(8,128)}) custom-call(f32[8,96,128]{2,1,0:T(8,128)S(1)} %get-tuple-element.33.t_part, f32[8,96,128]{2,1,0:T(8,128)S(1)} %get-tuple-element.34.s_part, f32[8,96,128]{2,1,0:T(8,128)S(1)} %get-tuple-element.35.u_part, ...), custom_call_target="tpu_custom_call" | custom-call | tf_op jit(solution)/shard_map/finish/pallas_call | solution.py:514
Async XLA Ops:
  0.6 14.7 %copy-start.7 = (f32[96,128]{1,0:T(8,128)S(1)}, f32[96,128]{1,0:T(8,128)}, u32[]{:S(2)}) copy-start(f32[96,128]{1,0:T(8,128)} %e2.5) | copy-start | bytes 147460
  0.6 14.7 %copy-start.6 = (f32[96,128]{1,0:T(8,128)S(1)}, f32[96,128]{1,0:T(8,128)}, u32[]{:S(2)}) copy-start(f32[96,128]{1,0:T(8,128)} %e1.5) | copy-start | bytes 147460
  0.7 14.7 %copy-start.5 = (s32[8,96,128]{2,1,0:T(8,128)S(1)}, s32[8,96,128]{2,1,0:T(8,128)}, u32[]{:S(2)}) copy-start(s32[8,96,128]{2,1,0:T(8,128)} %mf.5) | copy-start | bytes 1179652
  0.7 14.7 %copy-start.4 = (s32[8,96,128]{2,1,0:T(8,128)S(1)}, s32[8,96,128]{2,1,0:T(8,128)}, u32[]{:S(2)}) copy-start(s32[8,96,128]{2,1,0:T(8,128)} %zf.5) | copy-start | bytes 1179652
  0.7 14.7 %copy-start.3 = (f32[8,96,128]{2,1,0:T(8,128)S(1)}, f32[8,96,128]{2,1,0:T(8,128)}, u32[]{:S(2)}) copy-start(f32[8,96,128]{2,1,0:T(8,128)} %v.5) | copy-start | bytes 1179652
  0.7 14.7 %copy-start.2 = (f32[8,96,128]{2,1,0:T(8,128)S(1)}, f32[8,96,128]{2,1,0:T(8,128)}, u32[]{:S(2)}) copy-start(f32[8,96,128]{2,1,0:T(8,128)} %u.5) | copy-start | bytes 1179652
  0.7 14.7 %copy-start.1 = (f32[8,96,128]{2,1,0:T(8,128)S(1)}, f32[8,96,128]{2,1,0:T(8,128)}, u32[]{:S(2)}) copy-start(f32[8,96,128]{2,1,0:T(8,128)} %s.5) | copy-start | bytes 1179652
  0.7 14.7 %copy-start = (f32[8,96,128]{2,1,0:T(8,128)S(1)}, f32[8,96,128]{2,1,0:T(8,128)}, u32[]{:S(2)}) copy-start(f32[8,96,128]{2,1,0:T(8,128)} %t.5) | copy-start | bytes 1179652
  2.7 16.2 %collective-permute-start = (f32[32,128]{1,0:T(8,128)}, f32[32,128]{1,0:T(8,128)S(1)}, u32[]{:S(2)}, u32[]{:S(2)}) collective-permute-start(f32[32,128]{1,0:T(8,128)} %get-tuple-element.31), channel_id=1, source_target_pairs={{0,1},{1,0},{2,3},{3,2},{4,5},{5,4},{6,7},{7,6},{8,9},{9,8},{10,11... | collective-permute-start | bytes 49160 | tf_op jit(solution)/shard_map/ppermute | solution.py:478
  4.6 14.3 %collective-permute-start.1 = (f32[32,128]{1,0:T(8,128)}, f32[32,128]{1,0:T(8,128)S(1)}, u32[]{:S(2)}, u32[]{:S(2)}) collective-permute-start(f32[32,128]{1,0:T(8,128)} %get-tuple-element.32), channel_id=1, source_target_pairs={{1,2},{2,1},{3,4},{4,3},{5,6},{6,5},{7,8},{8,7},{9,10},{10,9},{11,... | collective-permute-start | bytes 49160 | tf_op jit(solution)/shard_map/ppermute | solution.py:479
  15.4 0.8 %copy-start.8 = (s32[96,128]{1,0:T(8,128)S(1)}, s32[96,128]{1,0:T(8,128)}, u32[]{:S(2)}) copy-start(s32[96,128]{1,0:T(8,128)} %count.3) | copy-start | bytes 147460
  18.9 10.6 %copy-start.9 = (s32[96,128]{1,0:T(8,128)S(1)}, s32[96,128]{1,0:T(8,128)}, u32[]{:S(2)}) copy-start(s32[96,128]{1,0:T(8,128)} %count.3) | copy-start | bytes 147460
  19.0 12.6 %collective-permute-start.2 = (f32[32,128]{1,0:T(8,128)S(1)}, f32[32,128]{1,0:T(8,128)S(1)}, u32[]{:S(2)}, u32[]{:S(2)}) collective-permute-start(f32[32,128]{1,0:T(8,128)S(1)} %get-tuple-element.40), channel_id=1, source_target_pairs={{0,16},{16,0},{32,48},{48,32},{64,80},{80,64},{96,112},{112,96},{1... | collective-permute-start | bytes 49160 | tf_op jit(solution)/shard_map/ppermute | solution.py:502
  21.9 11.1 %collective-permute-start.3 = (f32[32,128]{1,0:T(8,128)S(1)}, f32[32,128]{1,0:T(8,128)S(1)}, u32[]{:S(2)}, u32[]{:S(2)}) collective-permute-start(f32[32,128]{1,0:T(8,128)S(1)} %get-tuple-element.41), channel_id=1, source_target_pairs={{0,496},{16,32},{32,16},{48,64},{64,48},{80,96},{96,80},{112,128},... | collective-permute-start | bytes 49160 | tf_op jit(solution)/shard_map/ppermute | solution.py:501

commit v4 on v3

--- a/solution.py
+++ b/solution.py
@@ -114,7 +114,7 @@
 
 
 def front(
-    t, s, u, v, zf, mf, count, e1, e2,
+    t, s, u, v, zf, mf, e1, e2,
     to_east, to_west, own, coriolis, p_ext, a_ext, b_ext, u_ext, v_ext, ft_ext, fs_ext, packed,
 ):
     lines = t.shape[1]
@@ -128,7 +128,6 @@
         rows = pl.ds(pl.multiple_of(r * TILE, TILE), TILE)
         spacing_x, spacing_y = e1[rows, :], e2[rows, :]
         ratio = LATERAL * spacing_y / spacing_x
-        levels = count[rows, :].astype(jnp.float32)
         row = (first_row + r * TILE + lax.broadcasted_iota(jnp.int32, (TILE, LANES), 0)).astype(jnp.float32)
         latitude = 10.0 + 78.0 * (row + 0.5) / total_rows
         turn = 2.0 * ROTATION * jnp.sin(latitude * (math.pi / 180.0))
@@ -150,10 +149,8 @@
             keep(5, k, salt, 0)
             keep(6, k, spacing_x * v[k, rows, :] * face_y, 0)
             keep(7, k, face_y, 0)
-        total = jnp.where(lane == 70, turn, 0.0)
-        for n, (x, source) in enumerate(
-            [(spacing_x, LANES - 1), (spacing_y, LANES - 1), (levels, LANES - 1), (spacing_x, 0), (spacing_y, 0), (levels, 0)]
-        ):
+        total = jnp.where(lane == 68, turn, 0.0)
+        for n, (x, source) in enumerate([(spacing_x, LANES - 1), (spacing_y, LANES - 1), (spacing_x, 0), (spacing_y, 0)]):
             total = jnp.where(lane == 64 + n, roll_lanes(x, 64 + n - source), total)
         for field in fields:
             total = total + field
@@ -198,7 +195,7 @@
                 fs_ext[k, rows, :] = here * s[k, source, :] + there * s[k, above, :]
         return 0
 
-    lax.fori_loop(0, tiles - 1, faces, 0)
+    lax.fori_loop(0, tiles - 1, faces, 0, unroll=3)
     faces(tiles - 1, 0, last=True)
 
 
@@ -328,7 +325,7 @@
         return 0
 
     update(0, 0, first=True)
-    lax.fori_loop(1, tiles - 1, update, 0)
+    lax.fori_loop(1, tiles - 1, update, 0, unroll=2)
     update(tiles - 1, 0, last=True)
 
 
@@ -341,7 +338,7 @@
     return x
 
 
-def finish(t_part, s_part, u_part, v_part, own, lon_a, lon_b, t_out, s_out, u_out, v_out, turned, sides, *buffers_and_done):
+def finish(t_part, s_part, u_part, v_part, count, own, lon_a, lon_b, t_out, s_out, u_out, v_out, turned, sides, *buffers_and_done):
     buffers, done = buffers_and_done[:4], buffers_and_done[4]
     lines = t_part.shape[1]
     even_i = lax.axis_index("lon") % 2 == 0
@@ -365,11 +362,10 @@
         return own[64 + number : 65 + number, :]
 
     u_last, g_last, t_first, s_first, face_first = mine(2), mine(3), mine(4), mine(5), mine(7)
-    turn = (0.25 * TIME_STEP) * single(6)
+    turn = (0.25 * TIME_STEP) * single(4)
     push = -TIME_STEP * GRAVITY / REFERENCE_DENSITY
     inverse_x, inverse_y = 1.0 / single(0), 1.0 / single(1)
-    wet = depth_index < single(2)
-    back = jnp.where(wet, -(TIME_STEP * inverse_x * inverse_y) * (0.5 * u_last - g_last), 0.0)
+    back = -(TIME_STEP * inverse_x * inverse_y) * (0.5 * u_last - g_last)
     anom_t, anom_s = t_east - 10.0, s_east - 35.0
     weight = 0.5 * thick * (
         (-0.1655 * (1.0 + 0.0001497 * depth) + (-0.1655 * 0.5 * 0.05952) * anom_t - 0.0024341 * anom_s) * anom_t
@@ -382,9 +378,8 @@
     turned[pl.ds(0, LEVELS, 2), :] = back * t_east
     turned[pl.ds(16, LEVELS, 2), :] = back * s_east
     turned[pl.ds(32, LEVELS, 2), :] = u_add
-    inverse_x, inverse_y = 1.0 / single(3), 1.0 / single(4)
-    wet = depth_index < single(5)
-    scale = jnp.where(wet, -(TIME_STEP * inverse_x * inverse_y), 0.0)
+    inverse_x, inverse_y = 1.0 / single(2), 1.0 / single(3)
+    scale = -(TIME_STEP * inverse_x * inverse_y)
     here, there = 0.5 * u_west + g_west, 0.5 * u_west - g_west
     upward = running_sum(0.5 * thick * u_west, level, True)
 
@@ -408,11 +403,13 @@
         def tile(r, _):
             rows = pl.ds(pl.multiple_of(r * TILE, TILE), TILE)
             side = sides[rows, :]
+            levels = jnp.where(at_side, count[rows, :], 0)
             for k in range(LEVELS):
+                wet = levels > k
                 both = roll_lanes(side, -(2 * k + 33))
                 adds = (
-                    jnp.where(at_side, roll_lanes(side, -(2 * k + 1)), 0.0),
-                    jnp.where(at_side, roll_lanes(side, -(2 * k + 17)), 0.0),
+                    jnp.where(wet, roll_lanes(side, -(2 * k + 1)), 0.0),
+                    jnp.where(wet, roll_lanes(side, -(2 * k + 17)), 0.0),
                     jnp.where(at_last, both, 0.0),
                     jnp.where(at_first, both, 0.0),
                 )
@@ -420,7 +417,7 @@
                     buffer[k, rows, :] = part[k, rows, :] + add
             return 0
 
-        lax.fori_loop(c * chunk // TILE, (c + 1) * chunk // TILE, tile, 0)
+        lax.fori_loop(c * chunk // TILE, (c + 1) * chunk // TILE, tile, 0, unroll=True)
         rows = pl.ds(c * chunk, chunk)
         for n in range(4):
             copy = pltpu.make_async_copy(buffers[n].at[:, rows, :], outs[n].at[:, rows, :], done.at[c * 4 + n])
@@ -482,13 +479,13 @@
     square = VMEM((LANES, LANES), f32)
     to_east, to_west, own, coriolis, *parts = pl.pallas_call(
         front,
-        in_specs=whole(9),
+        in_specs=whole(8),
         out_specs=whole(11),
         out_shape=[packet, packet, jax.ShapeDtypeStruct((72, LANES), f32), jax.ShapeDtypeStruct(e1.shape, f32)] + [extended] * 7,
         scratch_shapes=[square],
         compiler_params=params,
         name="front",
-    )(t, s, u, v, zf, mf, bottom_tier_count, e1, e2)
+    )(t, s, u, v, zf, mf, e1, e2)
 
     lon_to_a, lon_to_b = pl.pallas_call(
         corner_pack,
@@ -513,13 +510,13 @@
 
     return pl.pallas_call(
         finish,
-        in_specs=whole(7),
+        in_specs=whole(8),
         out_specs=[pl.BlockSpec(memory_space=pltpu.MemorySpace.HBM)] * 4,
         out_shape=[field] * 4,
         scratch_shapes=[square] * 2 + [VMEM(t.shape, f32)] * 4 + [pltpu.SemaphoreType.DMA((4 * CHUNKS,))],
         compiler_params=params,
         name="finish",
-    )(*parts, own, lon_a, lon_b)
+    )(*parts, bottom_tier_count, own, lon_a, lon_b)
 
 
 def solution(mesh):

time: 35.5 us -> 33.7 us (0.949)
  the two profiles are of different devices: /device:TPU:198 before, /device:TPU:6 now
where the time goes in v4:
time: 33.7 us; the launch traced here: 33.5 us
  starting transfers between devices  25 us (74%)
  Pallas kernels  7.15 us (21%)
  between operations  0.85 us (3%)
  waiting for transfers between devices  0.43 us (1%)
    ppermute x1, starting transfers between devices, per_device(): lax.ppermute(lon_to_b, 'lon', [(i, (i + 1 if i % 2 else i - 1) % lons) fo...  13 us
    ppermute x1, starting transfers between devices, per_device(): lat_b = lax.ppermute(lat_to_b, ('lon', 'lat'), pairs_b)  5.8 us
    ppermute x1, starting transfers between devices, per_device(): lat_a = lax.ppermute(lat_to_a, 'lat', pairs_a)  4.28 us
    pallas_call x1, Pallas kernels, per_device(): pl.pallas_call(front, in_specs=whole(8), out_specs=whole(11), out_shape=[...  2.2 us
    ppermute x1, starting transfers between devices, per_device(): lon_a = lax.ppermute(lon_to_a, 'lon', [(i, i ^ 1) for i in range(lons)])  1.91 us
    pallas_call x1, Pallas kernels, per_device(): pl.pallas_call(row_pack, in_specs=[pl.BlockSpec(memory_space=pl.ANY)] * 8...  1.82 us
    pallas_call x1, Pallas kernels, per_device(): pl.pallas_call(finish, in_specs=whole(8), out_specs=[pl.BlockSpec(memory_...  1.59 us
    pallas_call x1, Pallas kernels, per_device(): pl.pallas_call(middle, in_specs=whole(19), out_specs=whole(4), out_shape=...  1.47 us
  transfers between devices with their start and end apart: 4, of which 1 were waited for; matrix products, arithmetic and copies ran while one was open for 0% of the time, Pallas kernels for 11%

profile of v4, /device:TPU:6, one launch (start us, length us, event | category | flops | bytes accessed | tf_op | source)
XLA Modules:
  0.0 33.5 jit_solution(9127657189138491272)
XLA Ops:
  0.6 0.0 copy-start.7
  0.6 0.0 copy-start.6
  0.7 0.0 copy-start.5
  0.7 0.0 copy-start.4
  0.7 0.0 copy-start.3
  0.7 0.0 copy-start.2
  0.7 0.0 copy-start.1
  0.7 0.0 copy-start
  0.7 1.8 %row_pack.1 = (f32[32,128]{1,0:T(8,128)}, f32[32,128]{1,0:T(8,128)}) custom-call(f32[8,96,128]{2,1,0:T(8,128)} %t.5, f32[8,96,128]{2,1,0:T(8,128)} %s.5, f32[8,96,128]{2,1,0:T(8,128)} %u.5, f32[8,96,128]{2,1,0:T(8,128)} %v.5, s32[8,96,128]{2,1,0:T(8,128)} %zf.5, s32[8,96,128]{2,1,0:T(8,128)} %mf.5, f32[96,128]{1,0:T(8,128)} %e1.5, f32[96,128]{1,0:T(8,128)} %e2.5), custom_call_target="tpu_custom_call" | custom-call | tf_op jit(solution)/shard_map/row_pack/pallas_call | solution.py:455
  2.5 4.3 %collective-permute-start = (f32[32,128]{1,0:T(8,128)}, f32[32,128]{1,0:T(8,128)S(1)}, u32[]{:S(2)}, u32[]{:S(2)}) collective-permute-start(f32[32,128]{1,0:T(8,128)} %get-tuple-element.31), channel_id=1, source_target_pairs={{0,1},{1,0},{2,3},{3,2},{4,5},{5,4},{6,7},{7,6},{8,9},{9,8},{10,11... | collective-permute-start | bytes 49160 | tf_op jit(solution)/shard_map/ppermute | solution.py:475
  6.8 5.8 %collective-permute-start.1 = (f32[32,128]{1,0:T(8,128)}, f32[32,128]{1,0:T(8,128)S(1)}, u32[]{:S(2)}, u32[]{:S(2)}) collective-permute-start(f32[32,128]{1,0:T(8,128)} %get-tuple-element.32), channel_id=1, source_target_pairs={{1,2},{2,1},{3,4},{4,3},{5,6},{6,5},{7,8},{8,7},{9,10},{10,9},{11,... | collective-permute-start | bytes 49160 | tf_op jit(solution)/shard_map/ppermute | solution.py:476
  12.6 0.0 copy-done.7
  12.6 0.0 copy-done.6
  12.7 0.0 copy-done.5
  12.7 0.0 copy-done.4
  12.7 0.0 copy-done.3
  12.7 0.0 copy-done.2
  12.7 0.0 copy-done.1
  12.7 0.0 copy-done
  12.7 2.2 %front.1 = (f32[32,128]{1,0:T(8,128)S(1)}, f32[32,128]{1,0:T(8,128)S(1)}, f32[72,128]{1,0:T(8,128)S(1)}, f32[96,128]{1,0:T(8,128)S(1)}, f32[8,112,128]{2,1,0:T(8...) custom-call(f32[8,96,128]{2,1,0:T(8,128)S(1)} %copy-done, ...), custom_call_target="tpu_custom_call" | custom-call | tf_op jit(solution)/shard_map/front/pallas_call | solution.py:480
  14.9 0.0 copy-start.8
  14.9 0.0 collective-permute-done.lat_a.from_a
  14.9 0.4 %collective-permute-done.1.lat_b.from_b = f32[32,128]{1,0:T(8,128)S(1)} collective-permute-done((f32[32,128]{1,0:T(8,128)}, f32[32,128]{1,0:T(8,128)S(1)}, u32[]{:S(2)}, u32[]{:S(2)}) %collective-permute-start.1) | collective-permute-done | bytes 16416 | tf_op jit(solution)/shard_map/ppermute | solution.py:476
  15.4 0.1 corner_pack.1
  15.4 1.9 %collective-permute-start.2 = (f32[32,128]{1,0:T(8,128)S(1)}, f32[32,128]{1,0:T(8,128)S(1)}, u32[]{:S(2)}, u32[]{:S(2)}) collective-permute-start(f32[32,128]{1,0:T(8,128)S(1)} %get-tuple-element.40), channel_id=1, source_target_pairs={{0,16},{16,0},{32,48},{48,32},{64,80},{80,64},{96,112},{112,96},{1... | collective-permute-start | bytes 49160 | tf_op jit(solution)/shard_map/ppermute | solution.py:499
  17.4 13.0 %collective-permute-start.3 = (f32[32,128]{1,0:T(8,128)S(1)}, f32[32,128]{1,0:T(8,128)S(1)}, u32[]{:S(2)}, u32[]{:S(2)}) collective-permute-start(f32[32,128]{1,0:T(8,128)S(1)} %get-tuple-element.41), channel_id=1, source_target_pairs={{0,496},{16,32},{32,16},{48,64},{64,48},{80,96},{96,80},{112,128},... | collective-permute-start | bytes 49160 | tf_op jit(solution)/shard_map/ppermute | solution.py:498
  30.4 0.0 copy-done.8
  30.4 1.5 %middle.1 = (f32[8,96,128]{2,1,0:T(8,128)S(1)}, f32[8,96,128]{2,1,0:T(8,128)S(1)}, f32[8,96,128]{2,1,0:T(8,128)S(1)}, f32[8,96,128]{2,1,0:T(8,128)S(1)}) custom-call(f32[8,96,128]{2,1,0:T(8,128)S(1)} %copy-done, f32[8,96,128]{2,1,0:T(8,128)S(1)} %copy-done.1, f32[8,96,128]{2,1,0:T(8,128)S(1)} %copy-done.2, f32[8,96,128]{2,1,0:T(8,128)S(1)} %copy-done.3, ...), custom_call_target="tpu_custom_call" | custom-call | tf_op jit(solution)/shard_map/middle/pallas_call | solution.py:501
  31.9 0.0 collective-permute-done.2.lon_a
  31.9 0.0 collective-permute-done.3.lon_b
  31.9 1.6 %finish.1 = (f32[8,96,128]{2,1,0:T(8,128)}, f32[8,96,128]{2,1,0:T(8,128)}, f32[8,96,128]{2,1,0:T(8,128)}, f32[8,96,128]{2,1,0:T(8,128)}) custom-call(f32[8,96,128]{2,1,0:T(8,128)S(1)} %get-tuple-element.33.t_part, f32[8,96,128]{2,1,0:T(8,128)S(1)} %get-tuple-element.34.s_part, f32[8,96,128]{2,1,0:T(8,128)S(1)} %get-tuple-element.35.u_part, ...), custom_call_target="tpu_custom_call" | custom-call | tf_op jit(solution)/shard_map/finish/pallas_call | solution.py:511
Async XLA Ops:
  0.6 12.0 %copy-start.7 = (f32[96,128]{1,0:T(8,128)S(1)}, f32[96,128]{1,0:T(8,128)}, u32[]{:S(2)}) copy-start(f32[96,128]{1,0:T(8,128)} %e2.5) | copy-start | bytes 147460
  0.6 12.0 %copy-start.6 = (f32[96,128]{1,0:T(8,128)S(1)}, f32[96,128]{1,0:T(8,128)}, u32[]{:S(2)}) copy-start(f32[96,128]{1,0:T(8,128)} %e1.5) | copy-start | bytes 147460
  0.7 12.0 %copy-start.5 = (s32[8,96,128]{2,1,0:T(8,128)S(1)}, s32[8,96,128]{2,1,0:T(8,128)}, u32[]{:S(2)}) copy-start(s32[8,96,128]{2,1,0:T(8,128)} %mf.5) | copy-start | bytes 1179652
  0.7 12.0 %copy-start.4 = (s32[8,96,128]{2,1,0:T(8,128)S(1)}, s32[8,96,128]{2,1,0:T(8,128)}, u32[]{:S(2)}) copy-start(s32[8,96,128]{2,1,0:T(8,128)} %zf.5) | copy-start | bytes 1179652
  0.7 12.0 %copy-start.3 = (f32[8,96,128]{2,1,0:T(8,128)S(1)}, f32[8,96,128]{2,1,0:T(8,128)}, u32[]{:S(2)}) copy-start(f32[8,96,128]{2,1,0:T(8,128)} %v.5) | copy-start | bytes 1179652
  0.7 12.0 %copy-start.2 = (f32[8,96,128]{2,1,0:T(8,128)S(1)}, f32[8,96,128]{2,1,0:T(8,128)}, u32[]{:S(2)}) copy-start(f32[8,96,128]{2,1,0:T(8,128)} %u.5) | copy-start | bytes 1179652
  0.7 12.0 %copy-start.1 = (f32[8,96,128]{2,1,0:T(8,128)S(1)}, f32[8,96,128]{2,1,0:T(8,128)}, u32[]{:S(2)}) copy-start(f32[8,96,128]{2,1,0:T(8,128)} %s.5) | copy-start | bytes 1179652
  0.7 12.0 %copy-start = (f32[8,96,128]{2,1,0:T(8,128)S(1)}, f32[8,96,128]{2,1,0:T(8,128)}, u32[]{:S(2)}) copy-start(f32[8,96,128]{2,1,0:T(8,128)} %t.5) | copy-start | bytes 1179652
  2.5 12.4 %collective-permute-start = (f32[32,128]{1,0:T(8,128)}, f32[32,128]{1,0:T(8,128)S(1)}, u32[]{:S(2)}, u32[]{:S(2)}) collective-permute-start(f32[32,128]{1,0:T(8,128)} %get-tuple-element.31), channel_id=1, source_target_pairs={{0,1},{1,0},{2,3},{3,2},{4,5},{5,4},{6,7},{7,6},{8,9},{9,8},{10,11... | collective-permute-start | bytes 49160 | tf_op jit(solution)/shard_map/ppermute | solution.py:475
  6.8 8.5 %collective-permute-start.1 = (f32[32,128]{1,0:T(8,128)}, f32[32,128]{1,0:T(8,128)S(1)}, u32[]{:S(2)}, u32[]{:S(2)}) collective-permute-start(f32[32,128]{1,0:T(8,128)} %get-tuple-element.32), channel_id=1, source_target_pairs={{1,2},{2,1},{3,4},{4,3},{5,6},{6,5},{7,8},{8,7},{9,10},{10,9},{11,... | collective-permute-start | bytes 49160 | tf_op jit(solution)/shard_map/ppermute | solution.py:476
  14.9 15.5 %copy-start.8 = (s32[96,128]{1,0:T(8,128)S(1)}, s32[96,128]{1,0:T(8,128)}, u32[]{:S(2)}) copy-start(s32[96,128]{1,0:T(8,128)} %count.3) | copy-start | bytes 147460
  15.4 16.4 %collective-permute-start.2 = (f32[32,128]{1,0:T(8,128)S(1)}, f32[32,128]{1,0:T(8,128)S(1)}, u32[]{:S(2)}, u32[]{:S(2)}) collective-permute-start(f32[32,128]{1,0:T(8,128)S(1)} %get-tuple-element.40), channel_id=1, source_target_pairs={{0,16},{16,0},{32,48},{48,32},{64,80},{80,64},{96,112},{112,96},{1... | collective-permute-start | bytes 49160 | tf_op jit(solution)/shard_map/ppermute | solution.py:499
  17.4 14.5 %collective-permute-start.3 = (f32[32,128]{1,0:T(8,128)S(1)}, f32[32,128]{1,0:T(8,128)S(1)}, u32[]{:S(2)}, u32[]{:S(2)}) collective-permute-start(f32[32,128]{1,0:T(8,128)S(1)} %get-tuple-element.41), channel_id=1, source_target_pairs={{0,496},{16,32},{32,16},{48,64},{64,48},{80,96},{96,80},{112,128},... | collective-permute-start | bytes 49160 | tf_op jit(solution)/shard_map/ppermute | solution.py:498

commit v5 on v4

--- a/solution.py
+++ b/solution.py
@@ -96,13 +96,7 @@
     @pl.when(top)
     def _():
         flux = flat[1, last:, :] * deep[5, :, last, :] * flags[1, :, last, :].astype(jnp.float32)
-        rows = jnp.concatenate([deep[1, :, last, :], deep[3, :, last, :], -flux], axis=0)
-        shape = (LANES, LANES)
-        mirror = lane_index(shape) + lax.broadcasted_iota(jnp.int32, shape, 0) == LANES - 1
-        to_b[: 3 * LEVELS, :] = lax.dot(
-            rows, mirror.astype(jnp.float32), precision=lax.Precision.HIGHEST, preferred_element_type=jnp.float32
-        )
-        to_b[3 * LEVELS :, :] = jnp.zeros((LEVELS, LANES), jnp.float32)
+        put(to_b, [deep[1, :, last, :], deep[3, :, last, :], -flux, jnp.zeros_like(flux)])
 
 
 def from_west(x):
@@ -208,7 +202,9 @@
     first, second = from_a[...], from_b[...]
     north = jnp.where(even_j, first, second)
     south = jnp.where(even_j, second, first)
-    east = jnp.where(corner, roll_lanes(north, 96 - (LANES - 1)), to_east[...])
+    top = lax.axis_index("lat") == lax.axis_size("lat") - 1
+    last_north = jnp.where(top, roll_lanes(north, 96), roll_lanes(north, 96 - (LANES - 1)))
+    east = jnp.where(corner, last_north, to_east[...])
     west = jnp.where(corner, roll_lanes(south, 96), to_west[...])
     to_a[...] = jnp.where(even_i, east, west)
     to_b[...] = jnp.where(even_i, west, east)
@@ -216,7 +212,7 @@
 
 def middle(
     t, s, u, v, zf, mf, count, e1, e2, coriolis, p_ext, a_ext, b_ext, u_ext, v_ext, ft_ext, fs_ext, lat_a, lat_b,
-    t_out, s_out, u_out, v_out, beyond,
+    t_out, s_out, u_out, v_out, beyond, beyond_north,
 ):
     lines = t.shape[1]
     tiles = lines // TILE
@@ -226,7 +222,17 @@
         rows = slice(number * LEVELS, (number + 1) * LEVELS)
         return jnp.where(flag, ref_true[rows, :], ref_false[rows, :])
 
-    north = [pick(lat_a, lat_b, even_j, n) for n in range(3)]
+    beyond_north[...] = jnp.where(even_j, lat_a[: 3 * LEVELS, :], lat_b[: 3 * LEVELS, :])
+
+    @pl.when(lax.axis_index("lat") == lax.axis_size("lat") - 1)
+    def _():
+        shape = (LANES, LANES)
+        mirror = lane_index(shape) + lax.broadcasted_iota(jnp.int32, shape, 0) == LANES - 1
+        beyond_north[...] = lax.dot(
+            beyond_north[...], mirror.astype(jnp.float32), precision=lax.Precision.HIGHEST, preferred_element_type=jnp.float32
+        )
+
+    north = [beyond_north[n * LEVELS : (n + 1) * LEVELS, :] for n in range(3)]
     south = [pick(lat_b, lat_a, even_j, n) for n in range(4)]
     here, there = 0.5 * south[2] + south[3], 0.5 * south[2] - south[3]
     beyond[0] = north[0]
@@ -338,7 +344,7 @@
     return x
 
 
-def finish(t_part, s_part, u_part, v_part, count, own, lon_a, lon_b, t_out, s_out, u_out, v_out, turned, sides, *buffers_and_done):
+def finish(t_part, s_part, u_part, v_part, count, own, lon_b, lon_a, t_out, s_out, u_out, v_out, turned, sides, *buffers_and_done):
     buffers, done = buffers_and_done[:4], buffers_and_done[4]
     lines = t_part.shape[1]
     even_i = lax.axis_index("lon") % 2 == 0
@@ -503,7 +509,7 @@
         in_specs=whole(19),
         out_specs=whole(4),
         out_shape=[field] * 4,
-        scratch_shapes=[VMEM((8, LEVELS, LANES), f32)],
+        scratch_shapes=[VMEM((8, LEVELS, LANES), f32), VMEM((3 * LEVELS, LANES), f32)],
         compiler_params=params,
         name="middle",
     )(t, s, u, v, zf, mf, bottom_tier_count, e1, e2, coriolis, *parts, lat_a, lat_b)
@@ -516,7 +522,7 @@
         scratch_shapes=[square] * 2 + [VMEM(t.shape, f32)] * 4 + [pltpu.SemaphoreType.DMA((4 * CHUNKS,))],
         compiler_params=params,
         name="finish",
-    )(*parts, bottom_tier_count, own, lon_a, lon_b)
+    )(*parts, bottom_tier_count, own, lon_b, lon_a)
 
 
 def solution(mesh):

time: 33.7 us -> 32.8 us (0.973)
  the two profiles are of different devices: /device:TPU:6 before, /device:TPU:199 now
where the time goes in v5:
time: 32.8 us; the launch traced here: 32.5 us
  starting transfers between devices  24.3 us (74%)
  Pallas kernels  7.34 us (22%)
  between operations  0.86 us (3%)
    ppermute x1, starting transfers between devices, per_device(): lat_b = lax.ppermute(lat_to_b, ('lon', 'lat'), pairs_b)  11.9 us
    ppermute x1, starting transfers between devices, per_device(): lon_a = lax.ppermute(lon_to_a, 'lon', [(i, i ^ 1) for i in range(lons)])  7.1 us
    ppermute x1, starting transfers between devices, per_device(): lax.ppermute(lon_to_b, 'lon', [(i, (i + 1 if i % 2 else i - 1) % lons) fo...  3.3 us
    pallas_call x1, Pallas kernels, per_device(): pl.pallas_call(front, in_specs=whole(8), out_specs=whole(11), out_shape=[...  2.2 us
    ppermute x1, starting transfers between devices, per_device(): lat_a = lax.ppermute(lat_to_a, 'lat', pairs_a)  1.92 us
    pallas_call x1, Pallas kernels, per_device(): pl.pallas_call(row_pack, in_specs=[pl.BlockSpec(memory_space=pl.ANY)] * 8...  1.82 us
    pallas_call x1, Pallas kernels, per_device(): pl.pallas_call(middle, in_specs=whole(19), out_specs=whole(4), out_shape=...  1.65 us
    pallas_call x1, Pallas kernels, per_device(): pl.pallas_call(finish, in_specs=whole(8), out_specs=[pl.BlockSpec(memory_...  1.59 us
  transfers between devices with their start and end apart: 4, of which 0 were waited for; matrix products, arithmetic and copies ran while one was open for 0% of the time, Pallas kernels for 12%

profile of v5, /device:TPU:199, one launch (start us, length us, event | category | flops | bytes accessed | tf_op | source)
XLA Modules:
  0.0 32.5 jit_solution(14935549539000549903)
XLA Ops:
  0.6 0.0 copy-start.7
  0.6 0.0 copy-start.6
  0.7 0.0 copy-start.5
  0.7 0.0 copy-start.4
  0.7 0.0 copy-start.3
  0.7 0.0 copy-start.2
  0.7 0.0 copy-start.1
  0.7 0.0 copy-start
  0.7 1.8 %row_pack.1 = (f32[32,128]{1,0:T(8,128)}, f32[32,128]{1,0:T(8,128)}) custom-call(f32[8,96,128]{2,1,0:T(8,128)} %t.5, f32[8,96,128]{2,1,0:T(8,128)} %s.5, f32[8,96,128]{2,1,0:T(8,128)} %u.5, f32[8,96,128]{2,1,0:T(8,128)} %v.5, s32[8,96,128]{2,1,0:T(8,128)} %zf.5, s32[8,96,128]{2,1,0:T(8,128)} %mf.5, f32[96,128]{1,0:T(8,128)} %e1.5, f32[96,128]{1,0:T(8,128)} %e2.5), custom_call_target="tpu_custom_call" | custom-call | tf_op jit(solution)/shard_map/row_pack/pallas_call | solution.py:461
  2.5 1.9 %collective-permute-start = (f32[32,128]{1,0:T(8,128)}, f32[32,128]{1,0:T(8,128)S(1)}, u32[]{:S(2)}, u32[]{:S(2)}) collective-permute-start(f32[32,128]{1,0:T(8,128)} %get-tuple-element.31), channel_id=1, source_target_pairs={{0,1},{1,0},{2,3},{3,2},{4,5},{5,4},{6,7},{7,6},{8,9},{9,8},{10,11... | collective-permute-start | bytes 49160 | tf_op jit(solution)/shard_map/ppermute | solution.py:481
  4.5 11.9 %collective-permute-start.1 = (f32[32,128]{1,0:T(8,128)}, f32[32,128]{1,0:T(8,128)S(1)}, u32[]{:S(2)}, u32[]{:S(2)}) collective-permute-start(f32[32,128]{1,0:T(8,128)} %get-tuple-element.32), channel_id=1, source_target_pairs={{1,2},{2,1},{3,4},{4,3},{5,6},{6,5},{7,8},{8,7},{9,10},{10,9},{11,... | collective-permute-start | bytes 49160 | tf_op jit(solution)/shard_map/ppermute | solution.py:482
  16.4 0.0 copy-done.7
  16.4 0.0 copy-done.6
  16.4 0.0 copy-done.5
  16.5 0.0 copy-done.4
  16.5 0.0 copy-done.3
  16.5 0.0 copy-done.2
  16.5 0.0 copy-done.1
  16.5 0.0 copy-done
  16.5 2.2 %front.1 = (f32[32,128]{1,0:T(8,128)S(1)}, f32[32,128]{1,0:T(8,128)S(1)}, f32[72,128]{1,0:T(8,128)S(1)}, f32[96,128]{1,0:T(8,128)S(1)}, f32[8,112,128]{2,1,0:T(8...) custom-call(f32[8,96,128]{2,1,0:T(8,128)S(1)} %copy-done, ...), custom_call_target="tpu_custom_call" | custom-call | tf_op jit(solution)/shard_map/front/pallas_call | solution.py:486
  18.7 0.0 copy-start.8
  18.7 0.0 collective-permute-done.lat_a.from_a
  18.7 0.0 collective-permute-done.1.lat_b.from_b
  18.7 0.1 corner_pack.1
  18.8 3.3 %collective-permute-start.2 = (f32[32,128]{1,0:T(8,128)S(1)}, f32[32,128]{1,0:T(8,128)S(1)}, u32[]{:S(2)}, u32[]{:S(2)}) collective-permute-start(f32[32,128]{1,0:T(8,128)S(1)} %get-tuple-element.40), channel_id=1, source_target_pairs={{0,496},{16,32},{32,16},{48,64},{64,48},{80,96},{96,80},{112,128},... | collective-permute-start | bytes 49160 | tf_op jit(solution)/shard_map/ppermute | solution.py:504
  22.1 7.1 %collective-permute-start.3 = (f32[32,128]{1,0:T(8,128)S(1)}, f32[32,128]{1,0:T(8,128)S(1)}, u32[]{:S(2)}, u32[]{:S(2)}) collective-permute-start(f32[32,128]{1,0:T(8,128)S(1)} %get-tuple-element.41), channel_id=1, source_target_pairs={{0,16},{16,0},{32,48},{48,32},{64,80},{80,64},{96,112},{112,96},{1... | collective-permute-start | bytes 49160 | tf_op jit(solution)/shard_map/ppermute | solution.py:505
  29.2 0.0 copy-done.8
  29.3 1.7 %middle.1 = (f32[8,96,128]{2,1,0:T(8,128)S(1)}, f32[8,96,128]{2,1,0:T(8,128)S(1)}, f32[8,96,128]{2,1,0:T(8,128)S(1)}, f32[8,96,128]{2,1,0:T(8,128)S(1)}) custom-call(f32[8,96,128]{2,1,0:T(8,128)S(1)} %copy-done, f32[8,96,128]{2,1,0:T(8,128)S(1)} %copy-done.1, f32[8,96,128]{2,1,0:T(8,128)S(1)} %copy-done.2, f32[8,96,128]{2,1,0:T(8,128)S(1)} %copy-done.3, ...), custom_call_target="tpu_custom_call" | custom-call | tf_op jit(solution)/shard_map/middle/pallas_call | solution.py:507
  30.9 0.0 collective-permute-done.2.lon_b
  30.9 0.0 collective-permute-done.3.lon_a
  30.9 1.6 %finish.1 = (f32[8,96,128]{2,1,0:T(8,128)}, f32[8,96,128]{2,1,0:T(8,128)}, f32[8,96,128]{2,1,0:T(8,128)}, f32[8,96,128]{2,1,0:T(8,128)}) custom-call(f32[8,96,128]{2,1,0:T(8,128)S(1)} %get-tuple-element.33.t_part, f32[8,96,128]{2,1,0:T(8,128)S(1)} %get-tuple-element.34.s_part, f32[8,96,128]{2,1,0:T(8,128)S(1)} %get-tuple-element.35.u_part, ...), custom_call_target="tpu_custom_call" | custom-call | tf_op jit(solution)/shard_map/finish/pallas_call | solution.py:517
Async XLA Ops:
  0.6 15.8 %copy-start.7 = (f32[96,128]{1,0:T(8,128)S(1)}, f32[96,128]{1,0:T(8,128)}, u32[]{:S(2)}) copy-start(f32[96,128]{1,0:T(8,128)} %e2.5) | copy-start | bytes 147460
  0.6 15.8 %copy-start.6 = (f32[96,128]{1,0:T(8,128)S(1)}, f32[96,128]{1,0:T(8,128)}, u32[]{:S(2)}) copy-start(f32[96,128]{1,0:T(8,128)} %e1.5) | copy-start | bytes 147460
  0.7 15.8 %copy-start.5 = (s32[8,96,128]{2,1,0:T(8,128)S(1)}, s32[8,96,128]{2,1,0:T(8,128)}, u32[]{:S(2)}) copy-start(s32[8,96,128]{2,1,0:T(8,128)} %mf.5) | copy-start | bytes 1179652
  0.7 15.8 %copy-start.4 = (s32[8,96,128]{2,1,0:T(8,128)S(1)}, s32[8,96,128]{2,1,0:T(8,128)}, u32[]{:S(2)}) copy-start(s32[8,96,128]{2,1,0:T(8,128)} %zf.5) | copy-start | bytes 1179652
  0.7 15.8 %copy-start.3 = (f32[8,96,128]{2,1,0:T(8,128)S(1)}, f32[8,96,128]{2,1,0:T(8,128)}, u32[]{:S(2)}) copy-start(f32[8,96,128]{2,1,0:T(8,128)} %v.5) | copy-start | bytes 1179652
  0.7 15.8 %copy-start.2 = (f32[8,96,128]{2,1,0:T(8,128)S(1)}, f32[8,96,128]{2,1,0:T(8,128)}, u32[]{:S(2)}) copy-start(f32[8,96,128]{2,1,0:T(8,128)} %u.5) | copy-start | bytes 1179652
  0.7 15.8 %copy-start.1 = (f32[8,96,128]{2,1,0:T(8,128)S(1)}, f32[8,96,128]{2,1,0:T(8,128)}, u32[]{:S(2)}) copy-start(f32[8,96,128]{2,1,0:T(8,128)} %s.5) | copy-start | bytes 1179652
  0.7 15.8 %copy-start = (f32[8,96,128]{2,1,0:T(8,128)S(1)}, f32[8,96,128]{2,1,0:T(8,128)}, u32[]{:S(2)}) copy-start(f32[8,96,128]{2,1,0:T(8,128)} %t.5) | copy-start | bytes 1179652
  2.5 16.2 %collective-permute-start = (f32[32,128]{1,0:T(8,128)}, f32[32,128]{1,0:T(8,128)S(1)}, u32[]{:S(2)}, u32[]{:S(2)}) collective-permute-start(f32[32,128]{1,0:T(8,128)} %get-tuple-element.31), channel_id=1, source_target_pairs={{0,1},{1,0},{2,3},{3,2},{4,5},{5,4},{6,7},{7,6},{8,9},{9,8},{10,11... | collective-permute-start | bytes 49160 | tf_op jit(solution)/shard_map/ppermute | solution.py:481
  4.5 14.3 %collective-permute-start.1 = (f32[32,128]{1,0:T(8,128)}, f32[32,128]{1,0:T(8,128)S(1)}, u32[]{:S(2)}, u32[]{:S(2)}) collective-permute-start(f32[32,128]{1,0:T(8,128)} %get-tuple-element.32), channel_id=1, source_target_pairs={{1,2},{2,1},{3,4},{4,3},{5,6},{6,5},{7,8},{8,7},{9,10},{10,9},{11,... | collective-permute-start | bytes 49160 | tf_op jit(solution)/shard_map/ppermute | solution.py:482
  18.7 10.5 %copy-start.8 = (s32[96,128]{1,0:T(8,128)S(1)}, s32[96,128]{1,0:T(8,128)}, u32[]{:S(2)}) copy-start(s32[96,128]{1,0:T(8,128)} %count.3) | copy-start | bytes 147460
  18.8 12.1 %collective-permute-start.2 = (f32[32,128]{1,0:T(8,128)S(1)}, f32[32,128]{1,0:T(8,128)S(1)}, u32[]{:S(2)}, u32[]{:S(2)}) collective-permute-start(f32[32,128]{1,0:T(8,128)S(1)} %get-tuple-element.40), channel_id=1, source_target_pairs={{0,496},{16,32},{32,16},{48,64},{64,48},{80,96},{96,80},{112,128},... | collective-permute-start | bytes 49160 | tf_op jit(solution)/shard_map/ppermute | solution.py:504
  22.1 8.8 %collective-permute-start.3 = (f32[32,128]{1,0:T(8,128)S(1)}, f32[32,128]{1,0:T(8,128)S(1)}, u32[]{:S(2)}, u32[]{:S(2)}) collective-permute-start(f32[32,128]{1,0:T(8,128)S(1)} %get-tuple-element.41), channel_id=1, source_target_pairs={{0,16},{16,0},{32,48},{48,32},{64,80},{80,64},{96,112},{112,96},{1... | collective-permute-start | bytes 49160 | tf_op jit(solution)/shard_map/ppermute | solution.py:505

commit v6 on v4

--- a/solution.py
+++ b/solution.py
@@ -20,6 +20,7 @@
 TILE = 8
 PACKET = 4 * LEVELS
 CHUNKS = 3
+EARLY = 7
 VMEM = pltpu.MemorySpace.VMEM
 
 THICK = [6.0 + 4.0 * k for k in range(LEVELS)]
@@ -45,7 +46,7 @@
     return along_t * anom_t + along_s * anom_s
 
 
-def row_pack(t, s, u, v, zf, mf, e1, e2, to_a, to_b, deep, flags, flat, arrived):
+def row_pack(t, s, u, v, zf, mf, e1, e2, bottom, to_a, to_b, count, deep, flags, flat, arrived):
     j = lax.axis_index("lat")
     even = j % 2 == 0
     top = j == lax.axis_size("lat") - 1
@@ -57,6 +58,7 @@
     copies = [pltpu.make_async_copy(ref.at[:, rows, :], deep.at[n], arrived.at[n]) for n, (ref, rows) in enumerate(wanted)]
     copies += [pltpu.make_async_copy(ref.at[:, rows, :], flags.at[n], arrived.at[7 + n]) for n, (ref, rows) in enumerate(marks)]
     copies += [pltpu.make_async_copy(ref.at[rows, :], flat.at[n], arrived.at[10 + n]) for n, (ref, rows) in enumerate(sizes)]
+    copies.append(pltpu.make_async_copy(bottom, count, arrived.at[13]))
     for copy in copies:
         copy.start()
     for copy in copies:
@@ -96,13 +98,7 @@
     @pl.when(top)
     def _():
         flux = flat[1, last:, :] * deep[5, :, last, :] * flags[1, :, last, :].astype(jnp.float32)
-        rows = jnp.concatenate([deep[1, :, last, :], deep[3, :, last, :], -flux], axis=0)
-        shape = (LANES, LANES)
-        mirror = lane_index(shape) + lax.broadcasted_iota(jnp.int32, shape, 0) == LANES - 1
-        to_b[: 3 * LEVELS, :] = lax.dot(
-            rows, mirror.astype(jnp.float32), precision=lax.Precision.HIGHEST, preferred_element_type=jnp.float32
-        )
-        to_b[3 * LEVELS :, :] = jnp.zeros((LEVELS, LANES), jnp.float32)
+        put(to_b, [deep[1, :, last, :], deep[3, :, last, :], -flux, jnp.zeros_like(flux)])
 
 
 def from_west(x):
@@ -113,135 +109,10 @@
     return jnp.where(lane_index(x.shape) == LANES - 1, 0.0, roll_lanes(x, -1))
 
 
-def front(
-    t, s, u, v, zf, mf, e1, e2,
-    to_east, to_west, own, coriolis, p_ext, a_ext, b_ext, u_ext, v_ext, ft_ext, fs_ext, packed,
-):
-    lines = t.shape[1]
-    tiles = lines // TILE
-    lane = lane_index((TILE, LANES))
-    first_row = lax.axis_index("lat") * lines
-    total_rows = lines * lax.axis_size("lat")
-    packed[pl.ds(lines, LANES - lines), :] = jnp.zeros((LANES - lines, LANES), jnp.float32)
-
-    def pack(r, _):
-        rows = pl.ds(pl.multiple_of(r * TILE, TILE), TILE)
-        spacing_x, spacing_y = e1[rows, :], e2[rows, :]
-        ratio = LATERAL * spacing_y / spacing_x
-        row = (first_row + r * TILE + lax.broadcasted_iota(jnp.int32, (TILE, LANES), 0)).astype(jnp.float32)
-        latitude = 10.0 + 78.0 * (row + 0.5) / total_rows
-        turn = 2.0 * ROTATION * jnp.sin(latitude * (math.pi / 180.0))
-        coriolis[rows, :] = turn
-        fields = [jnp.zeros((TILE, LANES), jnp.float32) for _ in range(8)]
-
-        def keep(number, k, x, source):
-            target = number * LEVELS + k
-            fields[number] = jnp.where(lane == target, roll_lanes(x, target - source), fields[number])
-
-        for k in range(LEVELS):
-            heat, salt = t[k, rows, :], s[k, rows, :]
-            face_x, face_y = zf[k, rows, :].astype(jnp.float32), mf[k, rows, :].astype(jnp.float32)
-            keep(0, k, heat, LANES - 1)
-            keep(1, k, salt, LANES - 1)
-            keep(2, k, spacing_y * u[k, rows, :] * face_x, LANES - 1)
-            keep(3, k, ratio * face_x, LANES - 1)
-            keep(4, k, heat, 0)
-            keep(5, k, salt, 0)
-            keep(6, k, spacing_x * v[k, rows, :] * face_y, 0)
-            keep(7, k, face_y, 0)
-        total = jnp.where(lane == 68, turn, 0.0)
-        for n, (x, source) in enumerate([(spacing_x, LANES - 1), (spacing_y, LANES - 1), (spacing_x, 0), (spacing_y, 0)]):
-            total = jnp.where(lane == 64 + n, roll_lanes(x, 64 + n - source), total)
-        for field in fields:
-            total = total + field
-        packed[rows, :] = total
-        return 0
-
-    lax.fori_loop(0, tiles, pack, 0, unroll=4)
-    turned = packed[...].T
-    to_east[...] = turned[:PACKET]
-    to_west[...] = turned[PACKET : 2 * PACKET]
-    own[...] = turned[: own.shape[0]]
-
-    def heads(r, _):
-        source = pl.ds(pl.multiple_of(r * TILE, TILE), TILE)
-        rows = pl.ds(pl.multiple_of(r * TILE + TILE, TILE), TILE)
-        head = jnp.zeros((TILE, LANES), jnp.float32)
-        for k in range(LEVELS):
-            half = (0.5 * THICK[k]) * density(t[k, source, :], s[k, source, :], k)
-            p_ext[k, rows, :] = head + half
-            head = head + 2.0 * half
-        return 0
-
-    lax.fori_loop(0, tiles, heads, 0, unroll=2)
-
-    def faces(r, _, last=False):
-        source = pl.ds(pl.multiple_of(r * TILE, TILE), TILE)
-        rows = pl.ds(pl.multiple_of(r * TILE + TILE, TILE), TILE)
-        above = pl.ds(r * TILE + 1, TILE)
-        spacing_x, spacing_y = e1[source, :], e2[source, :]
-        ratio = LATERAL * spacing_x / spacing_y
-        for k in range(LEVELS):
-            flux_x = spacing_y * u[k, source, :] * zf[k, source, :].astype(jnp.float32)
-            u_ext[k, rows, :] = flux_x
-            a_ext[k, rows, :] = flux_x + from_west(flux_x)
-            face = mf[k, source, :].astype(jnp.float32)
-            flux_y = spacing_x * v[k, source, :] * face
-            v_ext[k, rows, :] = flux_y
-            b_ext[k, rows, :] = flux_y + from_east(flux_y)
-            if not last:
-                here, there = 0.5 * flux_y + ratio * face, 0.5 * flux_y - ratio * face
-                ft_ext[k, rows, :] = here * t[k, source, :] + there * t[k, above, :]
-                fs_ext[k, rows, :] = here * s[k, source, :] + there * s[k, above, :]
-        return 0
-
-    lax.fori_loop(0, tiles - 1, faces, 0, unroll=3)
-    faces(tiles - 1, 0, last=True)
-
-
-def corner_pack(from_a, from_b, to_east, to_west, to_a, to_b):
-    even_j = lax.axis_index("lat") % 2 == 0
-    even_i = lax.axis_index("lon") % 2 == 0
-    shape = (PACKET, LANES)
-    row = lax.broadcasted_iota(jnp.int32, shape, 0)
-    corner = (lane_index(shape) == 96) & (row >= 2 * LEVELS) & (row < 3 * LEVELS)
-    first, second = from_a[...], from_b[...]
-    north = jnp.where(even_j, first, second)
-    south = jnp.where(even_j, second, first)
-    east = jnp.where(corner, roll_lanes(north, 96 - (LANES - 1)), to_east[...])
-    west = jnp.where(corner, roll_lanes(south, 96), to_west[...])
-    to_a[...] = jnp.where(even_i, east, west)
-    to_b[...] = jnp.where(even_i, west, east)
-
-
-def middle(
-    t, s, u, v, zf, mf, count, e1, e2, coriolis, p_ext, a_ext, b_ext, u_ext, v_ext, ft_ext, fs_ext, lat_a, lat_b,
+def tile_update(
+    t, s, u, v, zf, mf, count, e1, e2, coriolis, p_ext, a_ext, b_ext, u_ext, v_ext, ft_ext, fs_ext,
     t_out, s_out, u_out, v_out, beyond,
 ):
-    lines = t.shape[1]
-    tiles = lines // TILE
-    even_j = lax.axis_index("lat") % 2 == 0
-
-    def pick(ref_true, ref_false, flag, number):
-        rows = slice(number * LEVELS, (number + 1) * LEVELS)
-        return jnp.where(flag, ref_true[rows, :], ref_false[rows, :])
-
-    north = [pick(lat_a, lat_b, even_j, n) for n in range(3)]
-    south = [pick(lat_b, lat_a, even_j, n) for n in range(4)]
-    here, there = 0.5 * south[2] + south[3], 0.5 * south[2] - south[3]
-    beyond[0] = north[0]
-    beyond[1] = north[1]
-    beyond[2] = north[2] + from_west(north[2])
-    beyond[4] = south[2] + from_east(south[2])
-    beyond[5] = south[2]
-    beyond[6] = here * south[0] + there * t[:, 0, :]
-    beyond[7] = here * south[1] + there * s[:, 0, :]
-    head = jnp.zeros((1, LANES), jnp.float32)
-    for k in range(LEVELS):
-        half = (0.5 * THICK[k]) * density(beyond[0, k : k + 1, :], beyond[1, k : k + 1, :], k)
-        beyond[3, k : k + 1, :] = head + half
-        head = head + 2.0 * half
-
     row = lax.broadcasted_iota(jnp.int32, (TILE, LANES), 0)
 
     def update(r, _, first=False, last=False):
@@ -324,8 +195,162 @@
             u_below, v_below = u_above, v_above
         return 0
 
+    return update
+
+
+def front(
+    t, s, u, v, zf, mf, count, e1, e2,
+    to_east, to_west, own, coriolis, p_ext, a_ext, b_ext, u_ext, v_ext, ft_ext, fs_ext,
+    t_out, s_out, u_out, v_out, packed,
+):
+    lines = t.shape[1]
+    tiles = lines // TILE
+    lane = lane_index((TILE, LANES))
+    first_row = lax.axis_index("lat") * lines
+    total_rows = lines * lax.axis_size("lat")
+    packed[pl.ds(lines, LANES - lines), :] = jnp.zeros((LANES - lines, LANES), jnp.float32)
+
+    def pack(r, _):
+        rows = pl.ds(pl.multiple_of(r * TILE, TILE), TILE)
+        spacing_x, spacing_y = e1[rows, :], e2[rows, :]
+        ratio = LATERAL * spacing_y / spacing_x
+        row = (first_row + r * TILE + lax.broadcasted_iota(jnp.int32, (TILE, LANES), 0)).astype(jnp.float32)
+        latitude = 10.0 + 78.0 * (row + 0.5) / total_rows
+        turn = 2.0 * ROTATION * jnp.sin(latitude * (math.pi / 180.0))
+        coriolis[rows, :] = turn
+        fields = [jnp.zeros((TILE, LANES), jnp.float32) for _ in range(8)]
+
+        def keep(number, k, x, source):
+            target = number * LEVELS + k
+            fields[number] = jnp.where(lane == target, roll_lanes(x, target - source), fields[number])
+
+        for k in range(LEVELS):
+            heat, salt = t[k, rows, :], s[k, rows, :]
+            face_x, face_y = zf[k, rows, :].astype(jnp.float32), mf[k, rows, :].astype(jnp.float32)
+            keep(0, k, heat, LANES - 1)
+            keep(1, k, salt, LANES - 1)
+            keep(2, k, spacing_y * u[k, rows, :] * face_x, LANES - 1)
+            keep(3, k, ratio * face_x, LANES - 1)
+            keep(4, k, heat, 0)
+            keep(5, k, salt, 0)
+            keep(6, k, spacing_x * v[k, rows, :] * face_y, 0)
+            keep(7, k, face_y, 0)
+        total = jnp.where(lane == 68, turn, 0.0)
+        for n, (x, source) in enumerate([(spacing_x, LANES - 1), (spacing_y, LANES - 1), (spacing_x, 0), (spacing_y, 0)]):
+            total = jnp.where(lane == 64 + n, roll_lanes(x, 64 + n - source), total)
+        for field in fields:
+            total = total + field
+        packed[rows, :] = total
+        return 0
+
+    lax.fori_loop(0, tiles, pack, 0, unroll=4)
+    turned = packed[...].T
+    to_east[...] = turned[:PACKET]
+    to_west[...] = turned[PACKET : 2 * PACKET]
+    own[...] = turned[: own.shape[0]]
+
+    def heads(r, _):
+        source = pl.ds(pl.multiple_of(r * TILE, TILE), TILE)
+        rows = pl.ds(pl.multiple_of(r * TILE + TILE, TILE), TILE)
+        head = jnp.zeros((TILE, LANES), jnp.float32)
+        for k in range(LEVELS):
+            half = (0.5 * THICK[k]) * density(t[k, source, :], s[k, source, :], k)
+            p_ext[k, rows, :] = head + half
+            head = head + 2.0 * half
+        return 0
+
+    lax.fori_loop(0, tiles, heads, 0, unroll=2)
+
+    def faces(r, _, last=False):
+        source = pl.ds(pl.multiple_of(r * TILE, TILE), TILE)
+        rows = pl.ds(pl.multiple_of(r * TILE + TILE, TILE), TILE)
+        above = pl.ds(r * TILE + 1, TILE)
+        spacing_x, spacing_y = e1[source, :], e2[source, :]
+        ratio = LATERAL * spacing_x / spacing_y
+        for k in range(LEVELS):
+            flux_x = spacing_y * u[k, source, :] * zf[k, source, :].astype(jnp.float32)
+            u_ext[k, rows, :] = flux_x
+            a_ext[k, rows, :] = flux_x + from_west(flux_x)
+            face = mf[k, source, :].astype(jnp.float32)
+            flux_y = spacing_x * v[k, source, :] * face
+            v_ext[k, rows, :] = flux_y
+            b_ext[k, rows, :] = flux_y + from_east(flux_y)
+            if not last:
+                here, there = 0.5 * flux_y + ratio * face, 0.5 * flux_y - ratio * face
+                ft_ext[k, rows, :] = here * t[k, source, :] + there * t[k, above, :]
+                fs_ext[k, rows, :] = here * s[k, source, :] + there * s[k, above, :]
+        return 0
+
+    lax.fori_loop(0, tiles - 1, faces, 0, unroll=3)
+    faces(tiles - 1, 0, last=True)
+    update = tile_update(
+        t, s, u, v, zf, mf, count, e1, e2, coriolis, p_ext, a_ext, b_ext, u_ext, v_ext, ft_ext, fs_ext,
+        t_out, s_out, u_out, v_out, None,
+    )
+    lax.fori_loop(1, EARLY, update, 0, unroll=2)
+
+
+def corner_pack(from_a, from_b, to_east, to_west, to_a, to_b):
+    even_j = lax.axis_index("lat") % 2 == 0
+    even_i = lax.axis_index("lon") % 2 == 0
+    shape = (PACKET, LANES)
+    row = lax.broadcasted_iota(jnp.int32, shape, 0)
+    corner = (lane_index(shape) == 96) & (row >= 2 * LEVELS) & (row < 3 * LEVELS)
+    first, second = from_a[...], from_b[...]
+    north = jnp.where(even_j, first, second)
+    south = jnp.where(even_j, second, first)
+    top = lax.axis_index("lat") == lax.axis_size("lat") - 1
+    last_north = jnp.where(top, roll_lanes(north, 96), roll_lanes(north, 96 - (LANES - 1)))
+    east = jnp.where(corner, last_north, to_east[...])
+    west = jnp.where(corner, roll_lanes(south, 96), to_west[...])
+    to_a[...] = jnp.where(even_i, east, west)
+    to_b[...] = jnp.where(even_i, west, east)
+
+
+def middle(
+    t, s, u, v, zf, mf, count, e1, e2, coriolis, p_ext, a_ext, b_ext, u_ext, v_ext, ft_ext, fs_ext, lat_a, lat_b,
+    t_out, s_out, u_out, v_out, beyond, beyond_north,
+):
+    lines = t.shape[1]
+    tiles = lines // TILE
+    even_j = lax.axis_index("lat") % 2 == 0
+
+    def pick(ref_true, ref_false, flag, number):
+        rows = slice(number * LEVELS, (number + 1) * LEVELS)
+        return jnp.where(flag, ref_true[rows, :], ref_false[rows, :])
+
+    beyond_north[...] = jnp.where(even_j, lat_a[: 3 * LEVELS, :], lat_b[: 3 * LEVELS, :])
+
+    @pl.when(lax.axis_index("lat") == lax.axis_size("lat") - 1)
+    def _():
+        shape = (LANES, LANES)
+        mirror = lane_index(shape) + lax.broadcasted_iota(jnp.int32, shape, 0) == LANES - 1
+        beyond_north[...] = lax.dot(
+            beyond_north[...], mirror.astype(jnp.float32), precision=lax.Precision.HIGHEST, preferred_element_type=jnp.float32
+        )
+
+    north = [beyond_north[n * LEVELS : (n + 1) * LEVELS, :] for n in range(3)]
+    south = [pick(lat_b, lat_a, even_j, n) for n in range(4)]
+    here, there = 0.5 * south[2] + south[3], 0.5 * south[2] - south[3]
+    beyond[0] = north[0]
+    beyond[1] = north[1]
+    beyond[2] = north[2] + from_west(north[2])
+    beyond[4] = south[2] + from_east(south[2])
+    beyond[5] = south[2]
+    beyond[6] = here * south[0] + there * t[:, 0, :]
+    beyond[7] = here * south[1] + there * s[:, 0, :]
+    head = jnp.zeros((1, LANES), jnp.float32)
+    for k in range(LEVELS):
+        half = (0.5 * THICK[k]) * density(beyond[0, k : k + 1, :], beyond[1, k : k + 1, :], k)
+        beyond[3, k : k + 1, :] = head + half
+        head = head + 2.0 * half
+
+    update = tile_update(
+        t, s, u, v, zf, mf, count, e1, e2, coriolis, p_ext, a_ext, b_ext, u_ext, v_ext, ft_ext, fs_ext,
+        t_out, s_out, u_out, v_out, beyond,
+    )
     update(0, 0, first=True)
-    lax.fori_loop(1, tiles - 1, update, 0, unroll=2)
+    lax.fori_loop(EARLY, tiles - 1, update, 0, unroll=2)
     update(tiles - 1, 0, last=True)
 
 
@@ -338,7 +363,7 @@
     return x
 
 
-def finish(t_part, s_part, u_part, v_part, count, own, lon_a, lon_b, t_out, s_out, u_out, v_out, turned, sides, *buffers_and_done):
+def finish(t_early, s_early, u_early, v_early, t_part, s_part, u_part, v_part, count, own, lon_b, lon_a, t_out, s_out, u_out, v_out, turned, sides, *buffers_and_done):
     buffers, done = buffers_and_done[:4], buffers_and_done[4]
     lines = t_part.shape[1]
     even_i = lax.axis_index("lon") % 2 == 0
@@ -395,13 +420,13 @@
 
     at_first, at_last = lane == 0, lane == LANES - 1
     at_side = at_first | at_last
-    parts, outs = (t_part, s_part, u_part, v_part), (t_out, s_out, u_out, v_out)
+    early, parts, outs = (t_early, s_early, u_early, v_early), (t_part, s_part, u_part, v_part), (t_out, s_out, u_out, v_out)
     chunk = lines // CHUNKS
     copies = []
     for c in range(CHUNKS):
 
-        def tile(r, _):
-            rows = pl.ds(pl.multiple_of(r * TILE, TILE), TILE)
+        for r in range(c * chunk // TILE, (c + 1) * chunk // TILE):
+            rows = pl.ds(r * TILE, TILE)
             side = sides[rows, :]
             levels = jnp.where(at_side, count[rows, :], 0)
             for k in range(LEVELS):
@@ -413,11 +438,8 @@
                     jnp.where(at_last, both, 0.0),
                     jnp.where(at_first, both, 0.0),
                 )
-                for part, add, buffer in zip(parts, adds, buffers):
+                for part, add, buffer in zip(early if 1 <= r < EARLY else parts, adds, buffers):
                     buffer[k, rows, :] = part[k, rows, :] + add
-            return 0
-
-        lax.fori_loop(c * chunk // TILE, (c + 1) * chunk // TILE, tile, 0, unroll=True)
         rows = pl.ds(c * chunk, chunk)
         for n in range(4):
             copy = pltpu.make_async_copy(buffers[n].at[:, rows, :], outs[n].at[:, rows, :], done.at[c * 4 + n])
@@ -452,19 +474,20 @@
     packet = jax.ShapeDtypeStruct((PACKET, LANES), f32)
     field = jax.ShapeDtypeStruct(t.shape, f32)
 
-    lat_to_a, lat_to_b = pl.pallas_call(
+    lat_to_a, lat_to_b, count = pl.pallas_call(
         row_pack,
-        in_specs=[pl.BlockSpec(memory_space=pl.ANY)] * 8,
-        out_specs=whole(2),
-        out_shape=[packet, packet],
+        in_specs=[pl.BlockSpec(memory_space=pl.ANY)] * 9,
+        out_specs=whole(3),
+        out_shape=[packet, packet, jax.ShapeDtypeStruct(e1.shape, jnp.int32)],
         scratch_shapes=[
             VMEM((7, LEVELS, TILE, LANES), f32),
             VMEM((3, LEVELS, TILE, LANES), jnp.int32),
             VMEM((3, TILE, LANES), f32),
-            pltpu.SemaphoreType.DMA((13,)),
+            pltpu.SemaphoreType.DMA((14,)),
         ],
+        compiler_params=pltpu.CompilerParams(vmem_limit_bytes=4 * 1024 * 1024),
         name="row_pack",
-    )(t, s, u, v, zf, mf, e1, e2)
+    )(*[pltpu.with_memory_space_constraint(x, pltpu.HBM) for x in (t, s, u, v, zf, mf, e1, e2, bottom_tier_count)])
 
     pairs_a = [(j, j ^ 1) for j in range(lats)]
     pairs_b = []
@@ -479,13 +502,14 @@
     square = VMEM((LANES, LANES), f32)
     to_east, to_west, own, coriolis, *parts = pl.pallas_call(
         front,
-        in_specs=whole(8),
-        out_specs=whole(11),
-        out_shape=[packet, packet, jax.ShapeDtypeStruct((72, LANES), f32), jax.ShapeDtypeStruct(e1.shape, f32)] + [extended] * 7,
+        in_specs=whole(9),
+        out_specs=whole(15),
+        out_shape=[packet, packet, jax.ShapeDtypeStruct((72, LANES), f32), jax.ShapeDtypeStruct(e1.shape, f32)] + [extended] * 7 + [field] * 4,
         scratch_shapes=[square],
         compiler_params=params,
         name="front",
-    )(t, s, u, v, zf, mf, e1, e2)
+    )(t, s, u, v, zf, mf, count, e1, e2)
+    parts, early = parts[:7], parts[7:]
 
     lon_to_a, lon_to_b = pl.pallas_call(
         corner_pack,
@@ -503,20 +527,20 @@
         in_specs=whole(19),
         out_specs=whole(4),
         out_shape=[field] * 4,
-        scratch_shapes=[VMEM((8, LEVELS, LANES), f32)],
+        scratch_shapes=[VMEM((8, LEVELS, LANES), f32), VMEM((3 * LEVELS, LANES), f32)],
         compiler_params=params,
         name="middle",
-    )(t, s, u, v, zf, mf, bottom_tier_count, e1, e2, coriolis, *parts, lat_a, lat_b)
+    )(t, s, u, v, zf, mf, count, e1, e2, coriolis, *parts, lat_a, lat_b)
 
     return pl.pallas_call(
         finish,
-        in_specs=whole(8),
+        in_specs=whole(12),
         out_specs=[pl.BlockSpec(memory_space=pltpu.MemorySpace.HBM)] * 4,
         out_shape=[field] * 4,
         scratch_shapes=[square] * 2 + [VMEM(t.shape, f32)] * 4 + [pltpu.SemaphoreType.DMA((4 * CHUNKS,))],
         compiler_params=params,
         name="finish",
-    )(*parts, bottom_tier_count, own, lon_a, lon_b)
+    )(*early, *parts, count, own, lon_b, lon_a)
 
 
 def solution(mesh):

time: 33.7 us -> 31.3 us (0.929)
  the two profiles are of different devices: /device:TPU:6 before, /device:TPU:199 now
where the time goes in v6:
time: 31.3 us; the launch traced here: 31.1 us
  starting transfers between devices  23.4 us (75%)
  Pallas kernels  6.83 us (22%)
  between operations  0.84 us (3%)
    ppermute x1, starting transfers between devices, per_device(): lat_b = lax.ppermute(lat_to_b, ('lon', 'lat'), pairs_b)  11.9 us
    ppermute x1, starting transfers between devices, per_device(): lon_a = lax.ppermute(lon_to_a, 'lon', [(i, i ^ 1) for i in range(lons)])  6.2 us
    ppermute x1, starting transfers between devices, per_device(): lax.ppermute(lon_to_b, 'lon', [(i, (i + 1 if i % 2 else i - 1) % lons) fo...  3.3 us
    pallas_call x1, Pallas kernels, per_device(): pl.pallas_call(front, in_specs=whole(9), out_specs=whole(15), out_shape=[...  2.9 us
    ppermute x1, starting transfers between devices, per_device(): lat_a = lax.ppermute(lat_to_a, 'lat', pairs_a)  1.92 us
    pallas_call x1, Pallas kernels, per_device(): pl.pallas_call(finish, in_specs=whole(12), out_specs=[pl.BlockSpec(memory...  1.59 us
    pallas_call x1, Pallas kernels, per_device(): pl.pallas_call(row_pack, in_specs=[pl.BlockSpec(memory_space=pl.ANY)] * 9...  1.28 us
    pallas_call x1, Pallas kernels, per_device(): pl.pallas_call(middle, in_specs=whole(19), out_specs=whole(4), out_shape=...  0.97 us
  transfers between devices with their start and end apart: 4, of which 0 were waited for; matrix products, arithmetic and copies ran while one was open for 0% of the time, Pallas kernels for 12%

profile of v6, /device:TPU:199, one launch (start us, length us, event | category | flops | bytes accessed | tf_op | source)
XLA Modules:
  0.0 31.1 jit_solution(843451810541479189)
XLA Ops:
  0.6 0.0 copy-start.7
  0.6 0.0 copy-start.6
  0.7 0.0 copy-start.5
  0.7 0.0 copy-start.4
  0.7 0.0 copy-start.3
  0.7 0.0 copy-start.2
  0.7 0.0 copy-start.1
  0.7 0.0 copy-start
  0.7 1.3 %row_pack.1 = (f32[32,128]{1,0:T(8,128)S(1)}, f32[32,128]{1,0:T(8,128)S(1)}, s32[96,128]{1,0:T(8,128)S(1)}) custom-call(f32[8,96,128]{2,1,0:T(8,128)} %t.5, f32[8,96,128]{2,1,0:T(8,128)} %s.5, f32[8,96,128]{2,1,0:T(8,128)} %u.5, f32[8,96,128]{2,1,0:T(8,128)} %v.5, s32[8,96,128]{2,1,0:T(8,128)} %zf.5, s32[8,96,128]{2,1,0:T(8,128)} %mf.5, f32[96,128]{1,0:T(8,128)} %e1.5, ...), custom_call_target="tpu_custom_call" | custom-call | tf_op jit(solution)/shard_map/row_pack/pallas_call | solution.py:477
  2.0 1.9 %collective-permute-start = (f32[32,128]{1,0:T(8,128)S(1)}, f32[32,128]{1,0:T(8,128)S(1)}, u32[]{:S(2)}, u32[]{:S(2)}) collective-permute-start(f32[32,128]{1,0:T(8,128)S(1)} %get-tuple-element.41), channel_id=1, source_target_pairs={{0,1},{1,0},{2,3},{3,2},{4,5},{5,4},{6,7},{7,6},{8,9},{9,8},{10,11... | collective-permute-start | bytes 49160 | tf_op jit(solution)/shard_map/ppermute | solution.py:498
  3.9 11.9 %collective-permute-start.1 = (f32[32,128]{1,0:T(8,128)S(1)}, f32[32,128]{1,0:T(8,128)S(1)}, u32[]{:S(2)}, u32[]{:S(2)}) collective-permute-start(f32[32,128]{1,0:T(8,128)S(1)} %get-tuple-element.42), channel_id=1, source_target_pairs={{1,2},{2,1},{3,4},{4,3},{5,6},{6,5},{7,8},{8,7},{9,10},{10,9},{11,... | collective-permute-start | bytes 49160 | tf_op jit(solution)/shard_map/ppermute | solution.py:499
  15.9 0.0 copy-done.7
  15.9 0.0 copy-done.6
  15.9 0.0 copy-done.5
  15.9 0.0 copy-done.4
  15.9 0.0 copy-done.3
  15.9 0.0 copy-done.2
  15.9 0.0 copy-done.1
  16.0 0.0 copy-done
  16.0 2.9 %front.1 = (f32[32,128]{1,0:T(8,128)S(1)}, f32[32,128]{1,0:T(8,128)S(1)}, f32[72,128]{1,0:T(8,128)S(1)}, f32[96,128]{1,0:T(8,128)S(1)}, f32[8,112,128]{2,1,0:T(8...) custom-call(f32[8,96,128]{2,1,0:T(8,128)S(1)} %copy-done, ...), custom_call_target="tpu_custom_call" | custom-call | tf_op jit(solution)/shard_map/front/pallas_call | solution.py:503
  18.9 0.0 collective-permute-done.lat_a.from_a
  18.9 0.0 collective-permute-done.1.lat_b.from_b
  18.9 0.1 corner_pack.1
  19.0 3.3 %collective-permute-start.2 = (f32[32,128]{1,0:T(8,128)S(1)}, f32[32,128]{1,0:T(8,128)S(1)}, u32[]{:S(2)}, u32[]{:S(2)}) collective-permute-start(f32[32,128]{1,0:T(8,128)S(1)} %get-tuple-element.50), channel_id=1, source_target_pairs={{0,496},{16,32},{32,16},{48,64},{64,48},{80,96},{96,80},{112,128},... | collective-permute-start | bytes 49160 | tf_op jit(solution)/shard_map/ppermute | solution.py:522
  22.3 6.2 %collective-permute-start.3 = (f32[32,128]{1,0:T(8,128)S(1)}, f32[32,128]{1,0:T(8,128)S(1)}, u32[]{:S(2)}, u32[]{:S(2)}) collective-permute-start(f32[32,128]{1,0:T(8,128)S(1)} %get-tuple-element.51), channel_id=1, source_target_pairs={{0,16},{16,0},{32,48},{48,32},{64,80},{80,64},{96,112},{112,96},{1... | collective-permute-start | bytes 49160 | tf_op jit(solution)/shard_map/ppermute | solution.py:523
  28.5 1.0 %middle.1 = (f32[8,96,128]{2,1,0:T(8,128)S(1)}, f32[8,96,128]{2,1,0:T(8,128)S(1)}, f32[8,96,128]{2,1,0:T(8,128)S(1)}, f32[8,96,128]{2,1,0:T(8,128)S(1)}) custom-call(f32[8,96,128]{2,1,0:T(8,128)S(1)} %copy-done, f32[8,96,128]{2,1,0:T(8,128)S(1)} %copy-done.1, f32[8,96,128]{2,1,0:T(8,128)S(1)} %copy-done.2, f32[8,96,128]{2,1,0:T(8,128)S(1)} %copy-done.3, ...), custom_call_target="tpu_custom_call" | custom-call | tf_op jit(solution)/shard_map/middle/pallas_call | solution.py:525
  29.5 0.0 collective-permute-done.2.lon_b
  29.5 0.0 collective-permute-done.3.lon_a
  29.5 1.6 %finish.1 = (f32[8,96,128]{2,1,0:T(8,128)}, f32[8,96,128]{2,1,0:T(8,128)}, f32[8,96,128]{2,1,0:T(8,128)}, f32[8,96,128]{2,1,0:T(8,128)}) custom-call(f32[8,96,128]{2,1,0:T(8,128)S(1)} %get-tuple-element.29.t_early, f32[8,96,128]{2,1,0:T(8,128)S(1)} %get-tuple-element.30.s_early, f32[8,96,128]{2,1,0:T(8,128)S(1)} %get-tuple-element.31.u_early, ...), custom_call_target="tpu_custom_call" | custom-call | tf_op jit(solution)/shard_map/finish/pallas_call | solution.py:535
Async XLA Ops:
  0.6 15.3 %copy-start.7 = (f32[96,128]{1,0:T(8,128)S(1)}, f32[96,128]{1,0:T(8,128)}, u32[]{:S(2)}) copy-start(f32[96,128]{1,0:T(8,128)} %e2.5) | copy-start | bytes 147460
  0.6 15.3 %copy-start.6 = (f32[96,128]{1,0:T(8,128)S(1)}, f32[96,128]{1,0:T(8,128)}, u32[]{:S(2)}) copy-start(f32[96,128]{1,0:T(8,128)} %e1.5) | copy-start | bytes 147460
  0.7 15.3 %copy-start.5 = (s32[8,96,128]{2,1,0:T(8,128)S(1)}, s32[8,96,128]{2,1,0:T(8,128)}, u32[]{:S(2)}) copy-start(s32[8,96,128]{2,1,0:T(8,128)} %mf.5) | copy-start | bytes 1179652
  0.7 15.3 %copy-start.4 = (s32[8,96,128]{2,1,0:T(8,128)S(1)}, s32[8,96,128]{2,1,0:T(8,128)}, u32[]{:S(2)}) copy-start(s32[8,96,128]{2,1,0:T(8,128)} %zf.5) | copy-start | bytes 1179652
  0.7 15.3 %copy-start.3 = (f32[8,96,128]{2,1,0:T(8,128)S(1)}, f32[8,96,128]{2,1,0:T(8,128)}, u32[]{:S(2)}) copy-start(f32[8,96,128]{2,1,0:T(8,128)} %v.5) | copy-start | bytes 1179652
  0.7 15.3 %copy-start.2 = (f32[8,96,128]{2,1,0:T(8,128)S(1)}, f32[8,96,128]{2,1,0:T(8,128)}, u32[]{:S(2)}) copy-start(f32[8,96,128]{2,1,0:T(8,128)} %u.5) | copy-start | bytes 1179652
  0.7 15.3 %copy-start.1 = (f32[8,96,128]{2,1,0:T(8,128)S(1)}, f32[8,96,128]{2,1,0:T(8,128)}, u32[]{:S(2)}) copy-start(f32[8,96,128]{2,1,0:T(8,128)} %s.5) | copy-start | bytes 1179652
  0.7 15.3 %copy-start = (f32[8,96,128]{2,1,0:T(8,128)S(1)}, f32[8,96,128]{2,1,0:T(8,128)}, u32[]{:S(2)}) copy-start(f32[8,96,128]{2,1,0:T(8,128)} %t.5) | copy-start | bytes 1179652
  2.0 16.9 %collective-permute-start = (f32[32,128]{1,0:T(8,128)S(1)}, f32[32,128]{1,0:T(8,128)S(1)}, u32[]{:S(2)}, u32[]{:S(2)}) collective-permute-start(f32[32,128]{1,0:T(8,128)S(1)} %get-tuple-element.41), channel_id=1, source_target_pairs={{0,1},{1,0},{2,3},{3,2},{4,5},{5,4},{6,7},{7,6},{8,9},{9,8},{10,11... | collective-permute-start | bytes 49160 | tf_op jit(solution)/shard_map/ppermute | solution.py:498
  3.9 15.0 %collective-permute-start.1 = (f32[32,128]{1,0:T(8,128)S(1)}, f32[32,128]{1,0:T(8,128)S(1)}, u32[]{:S(2)}, u32[]{:S(2)}) collective-permute-start(f32[32,128]{1,0:T(8,128)S(1)} %get-tuple-element.42), channel_id=1, source_target_pairs={{1,2},{2,1},{3,4},{4,3},{5,6},{6,5},{7,8},{8,7},{9,10},{10,9},{11,... | collective-permute-start | bytes 49160 | tf_op jit(solution)/shard_map/ppermute | solution.py:499
  19.0 10.5 %collective-permute-start.2 = (f32[32,128]{1,0:T(8,128)S(1)}, f32[32,128]{1,0:T(8,128)S(1)}, u32[]{:S(2)}, u32[]{:S(2)}) collective-permute-start(f32[32,128]{1,0:T(8,128)S(1)} %get-tuple-element.50), channel_id=1, source_target_pairs={{0,496},{16,32},{32,16},{48,64},{64,48},{80,96},{96,80},{112,128},... | collective-permute-start | bytes 49160 | tf_op jit(solution)/shard_map/ppermute | solution.py:522
  22.3 7.2 %collective-permute-start.3 = (f32[32,128]{1,0:T(8,128)S(1)}, f32[32,128]{1,0:T(8,128)S(1)}, u32[]{:S(2)}, u32[]{:S(2)}) collective-permute-start(f32[32,128]{1,0:T(8,128)S(1)} %get-tuple-element.51), channel_id=1, source_target_pairs={{0,16},{16,0},{32,48},{48,32},{64,80},{80,64},{96,112},{112,96},{1... | collective-permute-start | bytes 49160 | tf_op jit(solution)/shard_map/ppermute | solution.py:523

commit v7 on v6

--- a/solution.py
+++ b/solution.py
@@ -20,7 +20,7 @@
 TILE = 8
 PACKET = 4 * LEVELS
 CHUNKS = 3
-EARLY = 7
+EARLY = 9
 VMEM = pltpu.MemorySpace.VMEM
 
 THICK = [6.0 + 4.0 * k for k in range(LEVELS)]
@@ -309,7 +309,7 @@
 
 def middle(
     t, s, u, v, zf, mf, count, e1, e2, coriolis, p_ext, a_ext, b_ext, u_ext, v_ext, ft_ext, fs_ext, lat_a, lat_b,
-    t_out, s_out, u_out, v_out, beyond, beyond_north,
+    t_out, s_out, u_out, v_out, beyond,
 ):
     lines = t.shape[1]
     tiles = lines // TILE
@@ -319,17 +319,9 @@
         rows = slice(number * LEVELS, (number + 1) * LEVELS)
         return jnp.where(flag, ref_true[rows, :], ref_false[rows, :])
 
-    beyond_north[...] = jnp.where(even_j, lat_a[: 3 * LEVELS, :], lat_b[: 3 * LEVELS, :])
-
-    @pl.when(lax.axis_index("lat") == lax.axis_size("lat") - 1)
-    def _():
-        shape = (LANES, LANES)
-        mirror = lane_index(shape) + lax.broadcasted_iota(jnp.int32, shape, 0) == LANES - 1
-        beyond_north[...] = lax.dot(
-            beyond_north[...], mirror.astype(jnp.float32), precision=lax.Precision.HIGHEST, preferred_element_type=jnp.float32
-        )
-
-    north = [beyond_north[n * LEVELS : (n + 1) * LEVELS, :] for n in range(3)]
+    lane = lane_index((LEVELS, LANES))
+    source = jnp.where(lax.axis_index("lat") == lax.axis_size("lat") - 1, LANES - 1 - lane, lane)
+    north = [jnp.take_along_axis(pick(lat_a, lat_b, even_j, n), source, axis=1) for n in range(3)]
     south = [pick(lat_b, lat_a, even_j, n) for n in range(4)]
     here, there = 0.5 * south[2] + south[3], 0.5 * south[2] - south[3]
     beyond[0] = north[0]
@@ -527,7 +519,7 @@
         in_specs=whole(19),
         out_specs=whole(4),
         out_shape=[field] * 4,
-        scratch_shapes=[VMEM((8, LEVELS, LANES), f32), VMEM((3 * LEVELS, LANES), f32)],
+        scratch_shapes=[VMEM((8, LEVELS, LANES), f32)],
         compiler_params=params,
         name="middle",
     )(t, s, u, v, zf, mf, count, e1, e2, coriolis, *parts, lat_a, lat_b)

time: 31.3 us -> 31.2 us (level)
  the two profiles are of different devices: /device:TPU:199 before, /device:TPU:6 now
where the time goes in v7:
time: 31.2 us; the launch traced here: 30.6 us
  starting transfers between devices  22.5 us (72%)
  Pallas kernels  6.75 us (22%)
  between operations  0.84 us (3%)
  waiting for transfers between devices  0.45 us (1%)
    ppermute x1, starting transfers between devices, per_device(): lax.ppermute(lon_to_b, 'lon', [(i, (i + 1 if i % 2 else i - 1) % lons) fo...  10.5 us
    ppermute x1, starting transfers between devices, per_device(): lat_b = lax.ppermute(lat_to_b, ('lon', 'lat'), pairs_b)  5.8 us
    ppermute x1, starting transfers between devices, per_device(): lat_a = lax.ppermute(lat_to_a, 'lat', pairs_a)  4.28 us
    pallas_call x1, Pallas kernels, per_device(): pl.pallas_call(front, in_specs=whole(9), out_specs=whole(15), out_shape=[...  3.11 us
    ppermute x1, starting transfers between devices, per_device(): lon_a = lax.ppermute(lon_to_a, 'lon', [(i, i ^ 1) for i in range(lons)])  1.92 us
    pallas_call x1, Pallas kernels, per_device(): pl.pallas_call(finish, in_specs=whole(12), out_specs=[pl.BlockSpec(memory...  1.58 us
    pallas_call x1, Pallas kernels, per_device(): pl.pallas_call(row_pack, in_specs=[pl.BlockSpec(memory_space=pl.ANY)] * 9...  1.28 us
    pallas_call x1, Pallas kernels, per_device(): pl.pallas_call(middle, in_specs=whole(19), out_specs=whole(4), out_shape=...  0.69 us
  transfers between devices with their start and end apart: 4, of which 1 were waited for; matrix products, arithmetic and copies ran while one was open for 0% of the time, Pallas kernels for 12%

profile of v7, /device:TPU:6, one launch (start us, length us, event | category | flops | bytes accessed | tf_op | source)
XLA Modules:
  0.0 30.6 jit_solution(14906982873581187555)
XLA Ops:
  0.6 0.0 copy-start.7
  0.6 0.0 copy-start.6
  0.7 0.0 copy-start.5
  0.7 0.0 copy-start.4
  0.7 0.0 copy-start.3
  0.7 0.0 copy-start.2
  0.7 0.0 copy-start.1
  0.7 0.0 copy-start
  0.7 1.3 %row_pack.1 = (f32[32,128]{1,0:T(8,128)S(1)}, f32[32,128]{1,0:T(8,128)S(1)}, s32[96,128]{1,0:T(8,128)S(1)}) custom-call(f32[8,96,128]{2,1,0:T(8,128)} %t.5, f32[8,96,128]{2,1,0:T(8,128)} %s.5, f32[8,96,128]{2,1,0:T(8,128)} %u.5, f32[8,96,128]{2,1,0:T(8,128)} %v.5, s32[8,96,128]{2,1,0:T(8,128)} %zf.5, s32[8,96,128]{2,1,0:T(8,128)} %mf.5, f32[96,128]{1,0:T(8,128)} %e1.5, ...), custom_call_target="tpu_custom_call" | custom-call | tf_op jit(solution)/shard_map/row_pack/pallas_call | solution.py:469
  2.0 4.3 %collective-permute-start = (f32[32,128]{1,0:T(8,128)S(1)}, f32[32,128]{1,0:T(8,128)S(1)}, u32[]{:S(2)}, u32[]{:S(2)}) collective-permute-start(f32[32,128]{1,0:T(8,128)S(1)} %get-tuple-element.41), channel_id=1, source_target_pairs={{0,1},{1,0},{2,3},{3,2},{4,5},{5,4},{6,7},{7,6},{8,9},{9,8},{10,11... | collective-permute-start | bytes 49160 | tf_op jit(solution)/shard_map/ppermute | solution.py:490
  6.3 5.8 %collective-permute-start.1 = (f32[32,128]{1,0:T(8,128)S(1)}, f32[32,128]{1,0:T(8,128)S(1)}, u32[]{:S(2)}, u32[]{:S(2)}) collective-permute-start(f32[32,128]{1,0:T(8,128)S(1)} %get-tuple-element.42), channel_id=1, source_target_pairs={{1,2},{2,1},{3,4},{4,3},{5,6},{6,5},{7,8},{8,7},{9,10},{10,9},{11,... | collective-permute-start | bytes 49160 | tf_op jit(solution)/shard_map/ppermute | solution.py:491
  12.1 0.0 copy-done.7
  12.1 0.0 copy-done.6
  12.1 0.0 copy-done.5
  12.1 0.0 copy-done.4
  12.1 0.0 copy-done.3
  12.2 0.0 copy-done.2
  12.2 0.0 copy-done.1
  12.2 0.0 copy-done
  12.2 3.1 %front.1 = (f32[32,128]{1,0:T(8,128)S(1)}, f32[32,128]{1,0:T(8,128)S(1)}, f32[72,128]{1,0:T(8,128)S(1)}, f32[96,128]{1,0:T(8,128)S(1)}, f32[8,112,128]{2,1,0:T(8...) custom-call(f32[8,96,128]{2,1,0:T(8,128)S(1)} %copy-done, ...), custom_call_target="tpu_custom_call" | custom-call | tf_op jit(solution)/shard_map/front/pallas_call | solution.py:495
  15.3 0.0 collective-permute-done.lat_a.from_a
  15.3 0.0 collective-permute-done.1.lat_b.from_b
  15.3 0.1 corner_pack.1
  15.4 10.5 %collective-permute-start.2 = (f32[32,128]{1,0:T(8,128)S(1)}, f32[32,128]{1,0:T(8,128)S(1)}, u32[]{:S(2)}, u32[]{:S(2)}) collective-permute-start(f32[32,128]{1,0:T(8,128)S(1)} %get-tuple-element.50), channel_id=1, source_target_pairs={{0,496},{16,32},{32,16},{48,64},{64,48},{80,96},{96,80},{112,128},... | collective-permute-start | bytes 49160 | tf_op jit(solution)/shard_map/ppermute | solution.py:514
  25.9 1.9 %collective-permute-start.3 = (f32[32,128]{1,0:T(8,128)S(1)}, f32[32,128]{1,0:T(8,128)S(1)}, u32[]{:S(2)}, u32[]{:S(2)}) collective-permute-start(f32[32,128]{1,0:T(8,128)S(1)} %get-tuple-element.51), channel_id=1, source_target_pairs={{0,16},{16,0},{32,48},{48,32},{64,80},{80,64},{96,112},{112,96},{1... | collective-permute-start | bytes 49160 | tf_op jit(solution)/shard_map/ppermute | solution.py:515
  27.9 0.7 %middle.1 = (f32[8,96,128]{2,1,0:T(8,128)S(1)}, f32[8,96,128]{2,1,0:T(8,128)S(1)}, f32[8,96,128]{2,1,0:T(8,128)S(1)}, f32[8,96,128]{2,1,0:T(8,128)S(1)}) custom-call(f32[8,96,128]{2,1,0:T(8,128)S(1)} %copy-done, f32[8,96,128]{2,1,0:T(8,128)S(1)} %copy-done.1, f32[8,96,128]{2,1,0:T(8,128)S(1)} %copy-done.2, f32[8,96,128]{2,1,0:T(8,128)S(1)} %copy-done.3, ...), custom_call_target="tpu_custom_call" | custom-call | tf_op jit(solution)/shard_map/middle/pallas_call | solution.py:517
  28.6 0.0 collective-permute-done.2.lon_b
  28.6 0.4 %collective-permute-done.3.lon_a = f32[32,128]{1,0:T(8,128)S(1)} collective-permute-done((f32[32,128]{1,0:T(8,128)S(1)}, f32[32,128]{1,0:T(8,128)S(1)}, u32[]{:S(2)}, u32[]{:S(2)}) %collective-permute-start.3) | collective-permute-done | bytes 16416 | tf_op jit(solution)/shard_map/ppermute | solution.py:515
  29.0 1.6 %finish.1 = (f32[8,96,128]{2,1,0:T(8,128)}, f32[8,96,128]{2,1,0:T(8,128)}, f32[8,96,128]{2,1,0:T(8,128)}, f32[8,96,128]{2,1,0:T(8,128)}) custom-call(f32[8,96,128]{2,1,0:T(8,128)S(1)} %get-tuple-element.29.t_early, f32[8,96,128]{2,1,0:T(8,128)S(1)} %get-tuple-element.30.s_early, f32[8,96,128]{2,1,0:T(8,128)S(1)} %get-tuple-element.31.u_early, ...), custom_call_target="tpu_custom_call" | custom-call | tf_op jit(solution)/shard_map/finish/pallas_call | solution.py:527
Async XLA Ops:
  0.6 11.5 %copy-start.7 = (f32[96,128]{1,0:T(8,128)S(1)}, f32[96,128]{1,0:T(8,128)}, u32[]{:S(2)}) copy-start(f32[96,128]{1,0:T(8,128)} %e2.5) | copy-start | bytes 147460
  0.6 11.5 %copy-start.6 = (f32[96,128]{1,0:T(8,128)S(1)}, f32[96,128]{1,0:T(8,128)}, u32[]{:S(2)}) copy-start(f32[96,128]{1,0:T(8,128)} %e1.5) | copy-start | bytes 147460
  0.7 11.5 %copy-start.5 = (s32[8,96,128]{2,1,0:T(8,128)S(1)}, s32[8,96,128]{2,1,0:T(8,128)}, u32[]{:S(2)}) copy-start(s32[8,96,128]{2,1,0:T(8,128)} %mf.5) | copy-start | bytes 1179652
  0.7 11.5 %copy-start.4 = (s32[8,96,128]{2,1,0:T(8,128)S(1)}, s32[8,96,128]{2,1,0:T(8,128)}, u32[]{:S(2)}) copy-start(s32[8,96,128]{2,1,0:T(8,128)} %zf.5) | copy-start | bytes 1179652
  0.7 11.5 %copy-start.3 = (f32[8,96,128]{2,1,0:T(8,128)S(1)}, f32[8,96,128]{2,1,0:T(8,128)}, u32[]{:S(2)}) copy-start(f32[8,96,128]{2,1,0:T(8,128)} %v.5) | copy-start | bytes 1179652
  0.7 11.5 %copy-start.2 = (f32[8,96,128]{2,1,0:T(8,128)S(1)}, f32[8,96,128]{2,1,0:T(8,128)}, u32[]{:S(2)}) copy-start(f32[8,96,128]{2,1,0:T(8,128)} %u.5) | copy-start | bytes 1179652
  0.7 11.5 %copy-start.1 = (f32[8,96,128]{2,1,0:T(8,128)S(1)}, f32[8,96,128]{2,1,0:T(8,128)}, u32[]{:S(2)}) copy-start(f32[8,96,128]{2,1,0:T(8,128)} %s.5) | copy-start | bytes 1179652
  0.7 11.5 %copy-start = (f32[8,96,128]{2,1,0:T(8,128)S(1)}, f32[8,96,128]{2,1,0:T(8,128)}, u32[]{:S(2)}) copy-start(f32[8,96,128]{2,1,0:T(8,128)} %t.5) | copy-start | bytes 1179652
  2.0 13.3 %collective-permute-start = (f32[32,128]{1,0:T(8,128)S(1)}, f32[32,128]{1,0:T(8,128)S(1)}, u32[]{:S(2)}, u32[]{:S(2)}) collective-permute-start(f32[32,128]{1,0:T(8,128)S(1)} %get-tuple-element.41), channel_id=1, source_target_pairs={{0,1},{1,0},{2,3},{3,2},{4,5},{5,4},{6,7},{7,6},{8,9},{9,8},{10,11... | collective-permute-start | bytes 49160 | tf_op jit(solution)/shard_map/ppermute | solution.py:490
  6.3 9.0 %collective-permute-start.1 = (f32[32,128]{1,0:T(8,128)S(1)}, f32[32,128]{1,0:T(8,128)S(1)}, u32[]{:S(2)}, u32[]{:S(2)}) collective-permute-start(f32[32,128]{1,0:T(8,128)S(1)} %get-tuple-element.42), channel_id=1, source_target_pairs={{1,2},{2,1},{3,4},{4,3},{5,6},{6,5},{7,8},{8,7},{9,10},{10,9},{11,... | collective-permute-start | bytes 49160 | tf_op jit(solution)/shard_map/ppermute | solution.py:491
  15.4 13.2 %collective-permute-start.2 = (f32[32,128]{1,0:T(8,128)S(1)}, f32[32,128]{1,0:T(8,128)S(1)}, u32[]{:S(2)}, u32[]{:S(2)}) collective-permute-start(f32[32,128]{1,0:T(8,128)S(1)} %get-tuple-element.50), channel_id=1, source_target_pairs={{0,496},{16,32},{32,16},{48,64},{64,48},{80,96},{96,80},{112,128},... | collective-permute-start | bytes 49160 | tf_op jit(solution)/shard_map/ppermute | solution.py:514
  25.9 3.1 %collective-permute-start.3 = (f32[32,128]{1,0:T(8,128)S(1)}, f32[32,128]{1,0:T(8,128)S(1)}, u32[]{:S(2)}, u32[]{:S(2)}) collective-permute-start(f32[32,128]{1,0:T(8,128)S(1)} %get-tuple-element.51), channel_id=1, source_target_pairs={{0,16},{16,0},{32,48},{48,32},{64,80},{80,64},{96,112},{112,96},{1... | collective-permute-start | bytes 49160 | tf_op jit(solution)/shard_map/ppermute | solution.py:515

commit v8 on v7

--- a/solution.py
+++ b/solution.py
@@ -20,7 +20,7 @@
 TILE = 8
 PACKET = 4 * LEVELS
 CHUNKS = 3
-EARLY = 9
+EARLY = 7
 VMEM = pltpu.MemorySpace.VMEM
 
 THICK = [6.0 + 4.0 * k for k in range(LEVELS)]
@@ -360,12 +360,11 @@
     lines = t_part.shape[1]
     even_i = lax.axis_index("lon") % 2 == 0
 
-    def pick(ref_true, ref_false, flag, number):
-        rows = slice(number * LEVELS, (number + 1) * LEVELS)
-        return jnp.where(flag, ref_true[rows, :], ref_false[rows, :])
-
-    t_east, s_east, v_east = [pick(lon_a, lon_b, even_i, n) for n in range(3)]
-    t_west, s_west, u_west, g_west = [pick(lon_b, lon_a, even_i, n) for n in range(4)]
+    def part(ref, number):
+        return ref[number * LEVELS : (number + 1) * LEVELS, :]
+
+    t_east, s_east, v_east = [jnp.where(even_i, part(lon_a, 4 + n), part(lon_b, n)) for n in range(3)]
+    t_west, s_west, u_west, g_west = [jnp.where(even_i, part(lon_b, n), part(lon_a, n)) for n in range(4)]
     shape = (LEVELS, LANES)
     level, lane = lax.broadcasted_iota(jnp.int32, shape, 0), lane_index(shape)
     depth_index = level.astype(jnp.float32)
@@ -512,7 +511,7 @@
         name="corner_pack",
     )(lat_a, lat_b, to_east, to_west)
     lon_b = lax.ppermute(lon_to_b, "lon", [(i, (i + 1 if i % 2 else i - 1) % lons) for i in range(lons)])
-    lon_a = lax.ppermute(lon_to_a, "lon", [(i, i ^ 1) for i in range(lons)])
+    lon_a = lax.all_gather(lon_to_a, "lon", axis_index_groups=[[i, i + 1] for i in range(0, lons, 2)], tiled=True)
 
     parts = pl.pallas_call(
         middle,

time: 31.2 us -> 30.7 us (0.984)
  the two profiles are of different devices: /device:TPU:6 before, /device:TPU:198 now
where the time goes in v8:
time: 30.7 us; the launch traced here: 30.5 us
  starting transfers between devices  20.8 us (68%)
  Pallas kernels  6.64 us (22%)
  blocking collectives  1.83 us (6%)
  between operations  0.82 us (3%)
  waiting for transfers between devices  0.39 us (1%)
    ppermute x1, starting transfers between devices, per_device(): lat_b = lax.ppermute(lat_to_b, ('lon', 'lat'), pairs_b)  10.8 us
    ppermute x1, starting transfers between devices, per_device(): lax.ppermute(lon_to_b, 'lon', [(i, (i + 1 if i % 2 else i - 1) % lons) fo...  8.04 us
    pallas_call x1, Pallas kernels, per_device(): pl.pallas_call(front, in_specs=whole(9), out_specs=whole(15), out_shape=[...  2.9 us
    ppermute x1, starting transfers between devices, per_device(): lat_a = lax.ppermute(lat_to_a, 'lat', pairs_a)  1.92 us
    all_gather x1, blocking collectives, per_device(): lax.all_gather(lon_to_a, 'lon', axis_index_groups=[[i, i + 1] for i in ra...  1.83 us
    pallas_call x1, Pallas kernels, per_device(): pl.pallas_call(finish, in_specs=whole(12), out_specs=[pl.BlockSpec(memory...  1.58 us
    pallas_call x1, Pallas kernels, per_device(): pl.pallas_call(row_pack, in_specs=[pl.BlockSpec(memory_space=pl.ANY)] * 9...  1.28 us
    pallas_call x1, Pallas kernels, per_device(): pl.pallas_call(middle, in_specs=whole(19), out_specs=whole(4), out_shape=...  0.79 us
  transfers between devices with their start and end apart: 3, of which 1 were waited for; matrix products, arithmetic and copies ran while one was open for 0% of the time, Pallas kernels for 12%

profile of v8, /device:TPU:198, one launch (start us, length us, event | category | flops | bytes accessed | tf_op | source)
XLA Modules:
  0.0 30.5 jit_solution(14943514972145493168)
XLA Ops:
  0.6 0.0 copy-start.7
  0.6 0.0 copy-start.6
  0.7 0.0 copy-start.5
  0.7 0.0 copy-start.4
  0.7 0.0 copy-start.3
  0.7 0.0 copy-start.2
  0.7 0.0 copy-start.1
  0.7 0.0 copy-start
  0.7 1.3 %row_pack.1 = (f32[32,128]{1,0:T(8,128)S(1)}, f32[32,128]{1,0:T(8,128)S(1)}, s32[96,128]{1,0:T(8,128)S(1)}) custom-call(f32[8,96,128]{2,1,0:T(8,128)} %t.5, f32[8,96,128]{2,1,0:T(8,128)} %s.5, f32[8,96,128]{2,1,0:T(8,128)} %u.5, f32[8,96,128]{2,1,0:T(8,128)} %v.5, s32[8,96,128]{2,1,0:T(8,128)} %zf.5, s32[8,96,128]{2,1,0:T(8,128)} %mf.5, f32[96,128]{1,0:T(8,128)} %e1.5, ...), custom_call_target="tpu_custom_call" | custom-call | tf_op jit(solution)/shard_map/row_pack/pallas_call | solution.py:468
  2.0 1.9 %collective-permute-start = (f32[32,128]{1,0:T(8,128)S(1)}, f32[32,128]{1,0:T(8,128)S(1)}, u32[]{:S(2)}, u32[]{:S(2)}) collective-permute-start(f32[32,128]{1,0:T(8,128)S(1)} %get-tuple-element.41), channel_id=1, source_target_pairs={{0,1},{1,0},{2,3},{3,2},{4,5},{5,4},{6,7},{7,6},{8,9},{9,8},{10,11... | collective-permute-start | bytes 49160 | tf_op jit(solution)/shard_map/ppermute | solution.py:489
  3.9 10.8 %collective-permute-start.1 = (f32[32,128]{1,0:T(8,128)S(1)}, f32[32,128]{1,0:T(8,128)S(1)}, u32[]{:S(2)}, u32[]{:S(2)}) collective-permute-start(f32[32,128]{1,0:T(8,128)S(1)} %get-tuple-element.42), channel_id=1, source_target_pairs={{1,2},{2,1},{3,4},{4,3},{5,6},{6,5},{7,8},{8,7},{9,10},{10,9},{11,... | collective-permute-start | bytes 49160 | tf_op jit(solution)/shard_map/ppermute | solution.py:490
  14.8 0.0 copy-done.7
  14.8 0.0 copy-done.6
  14.8 0.0 copy-done.5
  14.8 0.0 copy-done.4
  14.8 0.0 copy-done.3
  14.8 0.0 copy-done.2
  14.8 0.0 copy-done.1
  14.8 0.0 copy-done
  14.8 2.9 %front.1 = (f32[32,128]{1,0:T(8,128)S(1)}, f32[32,128]{1,0:T(8,128)S(1)}, f32[72,128]{1,0:T(8,128)S(1)}, f32[96,128]{1,0:T(8,128)S(1)}, f32[8,112,128]{2,1,0:T(8...) custom-call(f32[8,96,128]{2,1,0:T(8,128)S(1)} %copy-done, ...), custom_call_target="tpu_custom_call" | custom-call | tf_op jit(solution)/shard_map/front/pallas_call | solution.py:494
  17.7 0.0 collective-permute-done.lat_a.from_a
  17.8 0.0 collective-permute-done.1.lat_b.from_b
  17.8 0.1 corner_pack.1
  17.9 8.0 %collective-permute-start.2 = (f32[32,128]{1,0:T(8,128)S(1)}, f32[32,128]{1,0:T(8,128)S(1)}, u32[]{:S(2)}, u32[]{:S(2)}) collective-permute-start(f32[32,128]{1,0:T(8,128)S(1)} %get-tuple-element.50), channel_id=1, source_target_pairs={{0,496},{16,32},{32,16},{48,64},{64,48},{80,96},{96,80},{112,128},... | collective-permute-start | bytes 49160 | tf_op jit(solution)/shard_map/ppermute | solution.py:513
  25.9 0.8 %middle.1 = (f32[8,96,128]{2,1,0:T(8,128)S(1)}, f32[8,96,128]{2,1,0:T(8,128)S(1)}, f32[8,96,128]{2,1,0:T(8,128)S(1)}, f32[8,96,128]{2,1,0:T(8,128)S(1)}) custom-call(f32[8,96,128]{2,1,0:T(8,128)S(1)} %copy-done, f32[8,96,128]{2,1,0:T(8,128)S(1)} %copy-done.1, f32[8,96,128]{2,1,0:T(8,128)S(1)} %copy-done.2, f32[8,96,128]{2,1,0:T(8,128)S(1)} %copy-done.3, ...), custom_call_target="tpu_custom_call" | custom-call | tf_op jit(solution)/shard_map/middle/pallas_call | solution.py:516
  26.7 1.8 %all_gather.3.lon_a = f32[64,128]{1,0:T(8,128)S(1)} all-gather(f32[32,128]{1,0:T(8,128)S(1)} %get-tuple-element.51), channel_id=1, replica_groups={{0,16},{32,48},{64,80},{96,112},{128,144},{160,176},{192,208},{224,240}..., dimensions={0}, use_global_device_ids=true | all-gather | bytes 49152 | tf_op jit(solution)/shard_map/all_gather | solution.py:514
  28.5 0.4 %collective-permute-done.2.lon_b = f32[32,128]{1,0:T(8,128)S(1)} collective-permute-done((f32[32,128]{1,0:T(8,128)S(1)}, f32[32,128]{1,0:T(8,128)S(1)}, u32[]{:S(2)}, u32[]{:S(2)}) %collective-permute-start.2) | collective-permute-done | bytes 16416 | tf_op jit(solution)/shard_map/ppermute | solution.py:513
  28.9 1.6 %finish.1 = (f32[8,96,128]{2,1,0:T(8,128)}, f32[8,96,128]{2,1,0:T(8,128)}, f32[8,96,128]{2,1,0:T(8,128)}, f32[8,96,128]{2,1,0:T(8,128)}) custom-call(f32[8,96,128]{2,1,0:T(8,128)S(1)} %get-tuple-element.29.t_early, f32[8,96,128]{2,1,0:T(8,128)S(1)} %get-tuple-element.30.s_early, f32[8,96,128]{2,1,0:T(8,128)S(1)} %get-tuple-element.31.u_early, ...), custom_call_target="tpu_custom_call" | custom-call | tf_op jit(solution)/shard_map/finish/pallas_call | solution.py:526
Async XLA Ops:
  0.6 14.1 %copy-start.7 = (f32[96,128]{1,0:T(8,128)S(1)}, f32[96,128]{1,0:T(8,128)}, u32[]{:S(2)}) copy-start(f32[96,128]{1,0:T(8,128)} %e2.5) | copy-start | bytes 147460
  0.6 14.1 %copy-start.6 = (f32[96,128]{1,0:T(8,128)S(1)}, f32[96,128]{1,0:T(8,128)}, u32[]{:S(2)}) copy-start(f32[96,128]{1,0:T(8,128)} %e1.5) | copy-start | bytes 147460
  0.7 14.1 %copy-start.5 = (s32[8,96,128]{2,1,0:T(8,128)S(1)}, s32[8,96,128]{2,1,0:T(8,128)}, u32[]{:S(2)}) copy-start(s32[8,96,128]{2,1,0:T(8,128)} %mf.5) | copy-start | bytes 1179652
  0.7 14.1 %copy-start.4 = (s32[8,96,128]{2,1,0:T(8,128)S(1)}, s32[8,96,128]{2,1,0:T(8,128)}, u32[]{:S(2)}) copy-start(s32[8,96,128]{2,1,0:T(8,128)} %zf.5) | copy-start | bytes 1179652
  0.7 14.1 %copy-start.3 = (f32[8,96,128]{2,1,0:T(8,128)S(1)}, f32[8,96,128]{2,1,0:T(8,128)}, u32[]{:S(2)}) copy-start(f32[8,96,128]{2,1,0:T(8,128)} %v.5) | copy-start | bytes 1179652
  0.7 14.1 %copy-start.2 = (f32[8,96,128]{2,1,0:T(8,128)S(1)}, f32[8,96,128]{2,1,0:T(8,128)}, u32[]{:S(2)}) copy-start(f32[8,96,128]{2,1,0:T(8,128)} %u.5) | copy-start | bytes 1179652
  0.7 14.1 %copy-start.1 = (f32[8,96,128]{2,1,0:T(8,128)S(1)}, f32[8,96,128]{2,1,0:T(8,128)}, u32[]{:S(2)}) copy-start(f32[8,96,128]{2,1,0:T(8,128)} %s.5) | copy-start | bytes 1179652
  0.7 14.1 %copy-start = (f32[8,96,128]{2,1,0:T(8,128)S(1)}, f32[8,96,128]{2,1,0:T(8,128)}, u32[]{:S(2)}) copy-start(f32[8,96,128]{2,1,0:T(8,128)} %t.5) | copy-start | bytes 1179652
  2.0 15.8 %collective-permute-start = (f32[32,128]{1,0:T(8,128)S(1)}, f32[32,128]{1,0:T(8,128)S(1)}, u32[]{:S(2)}, u32[]{:S(2)}) collective-permute-start(f32[32,128]{1,0:T(8,128)S(1)} %get-tuple-element.41), channel_id=1, source_target_pairs={{0,1},{1,0},{2,3},{3,2},{4,5},{5,4},{6,7},{7,6},{8,9},{9,8},{10,11... | collective-permute-start | bytes 49160 | tf_op jit(solution)/shard_map/ppermute | solution.py:489
  3.9 13.8 %collective-permute-start.1 = (f32[32,128]{1,0:T(8,128)S(1)}, f32[32,128]{1,0:T(8,128)S(1)}, u32[]{:S(2)}, u32[]{:S(2)}) collective-permute-start(f32[32,128]{1,0:T(8,128)S(1)} %get-tuple-element.42), channel_id=1, source_target_pairs={{1,2},{2,1},{3,4},{4,3},{5,6},{6,5},{7,8},{8,7},{9,10},{10,9},{11,... | collective-permute-start | bytes 49160 | tf_op jit(solution)/shard_map/ppermute | solution.py:490
  17.9 11.1 %collective-permute-start.2 = (f32[32,128]{1,0:T(8,128)S(1)}, f32[32,128]{1,0:T(8,128)S(1)}, u32[]{:S(2)}, u32[]{:S(2)}) collective-permute-start(f32[32,128]{1,0:T(8,128)S(1)} %get-tuple-element.50), channel_id=1, source_target_pairs={{0,496},{16,32},{32,16},{48,64},{64,48},{80,96},{96,80},{112,128},... | collective-permute-start | bytes 49160 | tf_op jit(solution)/shard_map/ppermute | solution.py:513

commit v9 on v8

--- a/solution.py
+++ b/solution.py
@@ -19,7 +19,7 @@
 LANES = 128
 TILE = 8
 PACKET = 4 * LEVELS
-CHUNKS = 3
+CHUNKS = 4
 EARLY = 7
 VMEM = pltpu.MemorySpace.VMEM
 
@@ -243,7 +243,7 @@
         packed[rows, :] = total
         return 0
 
-    lax.fori_loop(0, tiles, pack, 0, unroll=4)
+    lax.fori_loop(0, tiles, pack, 0, unroll=True)
     turned = packed[...].T
     to_east[...] = turned[:PACKET]
     to_west[...] = turned[PACKET : 2 * PACKET]
@@ -259,7 +259,7 @@
             head = head + 2.0 * half
         return 0
 
-    lax.fori_loop(0, tiles, heads, 0, unroll=2)
+    lax.fori_loop(0, tiles, heads, 0, unroll=4)
 
     def faces(r, _, last=False):
         source = pl.ds(pl.multiple_of(r * TILE, TILE), TILE)
@@ -287,7 +287,7 @@
         t, s, u, v, zf, mf, count, e1, e2, coriolis, p_ext, a_ext, b_ext, u_ext, v_ext, ft_ext, fs_ext,
         t_out, s_out, u_out, v_out, None,
     )
-    lax.fori_loop(1, EARLY, update, 0, unroll=2)
+    lax.fori_loop(1, EARLY, update, 0, unroll=3)
 
 
 def corner_pack(from_a, from_b, to_east, to_west, to_a, to_b):

time: 30.7 us -> 30.7 us (level)
  the two profiles are of different devices: /device:TPU:198 before, /device:TPU:199 now
where the time goes in v9:
time: 30.7 us; the launch traced here: 30.5 us
  starting transfers between devices  17.2 us (56%)
  Pallas kernels  6.49 us (21%)
  blocking collectives  5.94 us (19%)
  between operations  0.82 us (3%)
    ppermute x1, starting transfers between devices, per_device(): lat_b = lax.ppermute(lat_to_b, ('lon', 'lat'), pairs_b)  11.9 us
    all_gather x1, blocking collectives, per_device(): lax.all_gather(lon_to_a, 'lon', axis_index_groups=[[i, i + 1] for i in ra...  5.94 us
    ppermute x1, starting transfers between devices, per_device(): lax.ppermute(lon_to_b, 'lon', [(i, (i + 1 if i % 2 else i - 1) % lons) fo...  3.3 us
    pallas_call x1, Pallas kernels, per_device(): pl.pallas_call(front, in_specs=whole(9), out_specs=whole(15), out_shape=[...  2.74 us
    ppermute x1, starting transfers between devices, per_device(): lat_a = lax.ppermute(lat_to_a, 'lat', pairs_a)  1.92 us
    pallas_call x1, Pallas kernels, per_device(): pl.pallas_call(finish, in_specs=whole(12), out_specs=[pl.BlockSpec(memory...  1.59 us
    pallas_call x1, Pallas kernels, per_device(): pl.pallas_call(row_pack, in_specs=[pl.BlockSpec(memory_space=pl.ANY)] * 9...  1.28 us
    pallas_call x1, Pallas kernels, per_device(): pl.pallas_call(middle, in_specs=whole(19), out_specs=whole(4), out_shape=...  0.79 us
  transfers between devices with their start and end apart: 3, of which 0 were waited for; matrix products, arithmetic and copies ran while one was open for 0% of the time, Pallas kernels for 12%

profile of v9, /device:TPU:199, one launch (start us, length us, event | category | flops | bytes accessed | tf_op | source)
XLA Modules:
  0.0 30.5 jit_solution(4973694145585096434)
XLA Ops:
  0.6 0.0 copy-start.7
  0.6 0.0 copy-start.6
  0.7 0.0 copy-start.5
  0.7 0.0 copy-start.4
  0.7 0.0 copy-start.3
  0.7 0.0 copy-start.2
  0.7 0.0 copy-start.1
  0.7 0.0 copy-start
  0.7 1.3 %row_pack.1 = (f32[32,128]{1,0:T(8,128)S(1)}, f32[32,128]{1,0:T(8,128)S(1)}, s32[96,128]{1,0:T(8,128)S(1)}) custom-call(f32[8,96,128]{2,1,0:T(8,128)} %t.5, f32[8,96,128]{2,1,0:T(8,128)} %s.5, f32[8,96,128]{2,1,0:T(8,128)} %u.5, f32[8,96,128]{2,1,0:T(8,128)} %v.5, s32[8,96,128]{2,1,0:T(8,128)} %zf.5, s32[8,96,128]{2,1,0:T(8,128)} %mf.5, f32[96,128]{1,0:T(8,128)} %e1.5, ...), custom_call_target="tpu_custom_call" | custom-call | tf_op jit(solution)/shard_map/row_pack/pallas_call | solution.py:468
  2.0 1.9 %collective-permute-start = (f32[32,128]{1,0:T(8,128)S(1)}, f32[32,128]{1,0:T(8,128)S(1)}, u32[]{:S(2)}, u32[]{:S(2)}) collective-permute-start(f32[32,128]{1,0:T(8,128)S(1)} %get-tuple-element.41), channel_id=1, source_target_pairs={{0,1},{1,0},{2,3},{3,2},{4,5},{5,4},{6,7},{7,6},{8,9},{9,8},{10,11... | collective-permute-start | bytes 49160 | tf_op jit(solution)/shard_map/ppermute | solution.py:489
  3.9 11.9 %collective-permute-start.1 = (f32[32,128]{1,0:T(8,128)S(1)}, f32[32,128]{1,0:T(8,128)S(1)}, u32[]{:S(2)}, u32[]{:S(2)}) collective-permute-start(f32[32,128]{1,0:T(8,128)S(1)} %get-tuple-element.42), channel_id=1, source_target_pairs={{1,2},{2,1},{3,4},{4,3},{5,6},{6,5},{7,8},{8,7},{9,10},{10,9},{11,... | collective-permute-start | bytes 49160 | tf_op jit(solution)/shard_map/ppermute | solution.py:490
  15.9 0.0 copy-done.7
  15.9 0.0 copy-done.6
  15.9 0.0 copy-done.5
  15.9 0.0 copy-done.4
  15.9 0.0 copy-done.3
  15.9 0.0 copy-done.2
  15.9 0.0 copy-done.1
  16.0 0.0 copy-done
  16.0 2.7 %front.1 = (f32[32,128]{1,0:T(8,128)S(1)}, f32[32,128]{1,0:T(8,128)S(1)}, f32[72,128]{1,0:T(8,128)S(1)}, f32[96,128]{1,0:T(8,128)S(1)}, f32[8,112,128]{2,1,0:T(8...) custom-call(f32[8,96,128]{2,1,0:T(8,128)S(1)} %copy-done, ...), custom_call_target="tpu_custom_call" | custom-call | tf_op jit(solution)/shard_map/front/pallas_call | solution.py:494
  18.7 0.0 collective-permute-done.lat_a.from_a
  18.7 0.0 collective-permute-done.1.lat_b.from_b
  18.7 0.1 corner_pack.1
  18.8 3.3 %collective-permute-start.2 = (f32[32,128]{1,0:T(8,128)S(1)}, f32[32,128]{1,0:T(8,128)S(1)}, u32[]{:S(2)}, u32[]{:S(2)}) collective-permute-start(f32[32,128]{1,0:T(8,128)S(1)} %get-tuple-element.50), channel_id=1, source_target_pairs={{0,496},{16,32},{32,16},{48,64},{64,48},{80,96},{96,80},{112,128},... | collective-permute-start | bytes 49160 | tf_op jit(solution)/shard_map/ppermute | solution.py:513
  22.1 0.8 %middle.1 = (f32[8,96,128]{2,1,0:T(8,128)S(1)}, f32[8,96,128]{2,1,0:T(8,128)S(1)}, f32[8,96,128]{2,1,0:T(8,128)S(1)}, f32[8,96,128]{2,1,0:T(8,128)S(1)}) custom-call(f32[8,96,128]{2,1,0:T(8,128)S(1)} %copy-done, f32[8,96,128]{2,1,0:T(8,128)S(1)} %copy-done.1, f32[8,96,128]{2,1,0:T(8,128)S(1)} %copy-done.2, f32[8,96,128]{2,1,0:T(8,128)S(1)} %copy-done.3, ...), custom_call_target="tpu_custom_call" | custom-call | tf_op jit(solution)/shard_map/middle/pallas_call | solution.py:516
  22.9 5.9 %all_gather.3.lon_a = f32[64,128]{1,0:T(8,128)S(1)} all-gather(f32[32,128]{1,0:T(8,128)S(1)} %get-tuple-element.51), channel_id=1, replica_groups={{0,16},{32,48},{64,80},{96,112},{128,144},{160,176},{192,208},{224,240}..., dimensions={0}, use_global_device_ids=true | all-gather | bytes 49152 | tf_op jit(solution)/shard_map/all_gather | solution.py:514
  28.9 0.0 collective-permute-done.2.lon_b
  28.9 1.6 %finish.1 = (f32[8,96,128]{2,1,0:T(8,128)}, f32[8,96,128]{2,1,0:T(8,128)}, f32[8,96,128]{2,1,0:T(8,128)}, f32[8,96,128]{2,1,0:T(8,128)}) custom-call(f32[8,96,128]{2,1,0:T(8,128)S(1)} %get-tuple-element.29.t_early, f32[8,96,128]{2,1,0:T(8,128)S(1)} %get-tuple-element.30.s_early, f32[8,96,128]{2,1,0:T(8,128)S(1)} %get-tuple-element.31.u_early, ...), custom_call_target="tpu_custom_call" | custom-call | tf_op jit(solution)/shard_map/finish/pallas_call | solution.py:526
Async XLA Ops:
  0.6 15.3 %copy-start.7 = (f32[96,128]{1,0:T(8,128)S(1)}, f32[96,128]{1,0:T(8,128)}, u32[]{:S(2)}) copy-start(f32[96,128]{1,0:T(8,128)} %e2.5) | copy-start | bytes 147460
  0.6 15.3 %copy-start.6 = (f32[96,128]{1,0:T(8,128)S(1)}, f32[96,128]{1,0:T(8,128)}, u32[]{:S(2)}) copy-start(f32[96,128]{1,0:T(8,128)} %e1.5) | copy-start | bytes 147460
  0.7 15.3 %copy-start.5 = (s32[8,96,128]{2,1,0:T(8,128)S(1)}, s32[8,96,128]{2,1,0:T(8,128)}, u32[]{:S(2)}) copy-start(s32[8,96,128]{2,1,0:T(8,128)} %mf.5) | copy-start | bytes 1179652
  0.7 15.3 %copy-start.4 = (s32[8,96,128]{2,1,0:T(8,128)S(1)}, s32[8,96,128]{2,1,0:T(8,128)}, u32[]{:S(2)}) copy-start(s32[8,96,128]{2,1,0:T(8,128)} %zf.5) | copy-start | bytes 1179652
  0.7 15.3 %copy-start.3 = (f32[8,96,128]{2,1,0:T(8,128)S(1)}, f32[8,96,128]{2,1,0:T(8,128)}, u32[]{:S(2)}) copy-start(f32[8,96,128]{2,1,0:T(8,128)} %v.5) | copy-start | bytes 1179652
  0.7 15.3 %copy-start.2 = (f32[8,96,128]{2,1,0:T(8,128)S(1)}, f32[8,96,128]{2,1,0:T(8,128)}, u32[]{:S(2)}) copy-start(f32[8,96,128]{2,1,0:T(8,128)} %u.5) | copy-start | bytes 1179652
  0.7 15.3 %copy-start.1 = (f32[8,96,128]{2,1,0:T(8,128)S(1)}, f32[8,96,128]{2,1,0:T(8,128)}, u32[]{:S(2)}) copy-start(f32[8,96,128]{2,1,0:T(8,128)} %s.5) | copy-start | bytes 1179652
  0.7 15.3 %copy-start = (f32[8,96,128]{2,1,0:T(8,128)S(1)}, f32[8,96,128]{2,1,0:T(8,128)}, u32[]{:S(2)}) copy-start(f32[8,96,128]{2,1,0:T(8,128)} %t.5) | copy-start | bytes 1179652
  2.0 16.7 %collective-permute-start = (f32[32,128]{1,0:T(8,128)S(1)}, f32[32,128]{1,0:T(8,128)S(1)}, u32[]{:S(2)}, u32[]{:S(2)}) collective-permute-start(f32[32,128]{1,0:T(8,128)S(1)} %get-tuple-element.41), channel_id=1, source_target_pairs={{0,1},{1,0},{2,3},{3,2},{4,5},{5,4},{6,7},{7,6},{8,9},{9,8},{10,11... | collective-permute-start | bytes 49160 | tf_op jit(solution)/shard_map/ppermute | solution.py:489
  3.9 14.8 %collective-permute-start.1 = (f32[32,128]{1,0:T(8,128)S(1)}, f32[32,128]{1,0:T(8,128)S(1)}, u32[]{:S(2)}, u32[]{:S(2)}) collective-permute-start(f32[32,128]{1,0:T(8,128)S(1)} %get-tuple-element.42), channel_id=1, source_target_pairs={{1,2},{2,1},{3,4},{4,3},{5,6},{6,5},{7,8},{8,7},{9,10},{10,9},{11,... | collective-permute-start | bytes 49160 | tf_op jit(solution)/shard_map/ppermute | solution.py:490
  18.8 10.1 %collective-permute-start.2 = (f32[32,128]{1,0:T(8,128)S(1)}, f32[32,128]{1,0:T(8,128)S(1)}, u32[]{:S(2)}, u32[]{:S(2)}) collective-permute-start(f32[32,128]{1,0:T(8,128)S(1)} %get-tuple-element.50), channel_id=1, source_target_pairs={{0,496},{16,32},{32,16},{48,64},{64,48},{80,96},{96,80},{112,128},... | collective-permute-start | bytes 49160 | tf_op jit(solution)/shard_map/ppermute | solution.py:513

commit v10 on v9

--- a/solution.py
+++ b/solution.py
@@ -218,7 +218,7 @@
         latitude = 10.0 + 78.0 * (row + 0.5) / total_rows
         turn = 2.0 * ROTATION * jnp.sin(latitude * (math.pi / 180.0))
         coriolis[rows, :] = turn
-        fields = [jnp.zeros((TILE, LANES), jnp.float32) for _ in range(8)]
+        fields = [jnp.zeros((TILE, LANES), jnp.float32) for _ in range(7)]
 
         def keep(number, k, x, source):
             target = number * LEVELS + k
@@ -234,7 +234,6 @@
             keep(4, k, heat, 0)
             keep(5, k, salt, 0)
             keep(6, k, spacing_x * v[k, rows, :] * face_y, 0)
-            keep(7, k, face_y, 0)
         total = jnp.where(lane == 68, turn, 0.0)
         for n, (x, source) in enumerate([(spacing_x, LANES - 1), (spacing_y, LANES - 1), (spacing_x, 0), (spacing_y, 0)]):
             total = jnp.where(lane == 64 + n, roll_lanes(x, 64 + n - source), total)
@@ -355,7 +354,7 @@
     return x
 
 
-def finish(t_early, s_early, u_early, v_early, t_part, s_part, u_part, v_part, count, own, lon_b, lon_a, t_out, s_out, u_out, v_out, turned, sides, *buffers_and_done):
+def finish(t_early, s_early, u_early, v_early, t_part, s_part, u_part, v_part, count, mf, own, lon_b, lon_a, t_out, s_out, u_out, v_out, turned, sides, *buffers_and_done):
     buffers, done = buffers_and_done[:4], buffers_and_done[4]
     lines = t_part.shape[1]
     even_i = lax.axis_index("lon") % 2 == 0
@@ -377,7 +376,7 @@
     def single(number):
         return own[64 + number : 65 + number, :]
 
-    u_last, g_last, t_first, s_first, face_first = mine(2), mine(3), mine(4), mine(5), mine(7)
+    u_last, g_last, t_first, s_first = mine(2), mine(3), mine(4), mine(5)
     turn = (0.25 * TIME_STEP) * single(4)
     push = -TIME_STEP * GRAVITY / REFERENCE_DENSITY
     inverse_x, inverse_y = 1.0 / single(0), 1.0 / single(1)
@@ -406,7 +405,7 @@
 
     turned[pl.ds(1, LEVELS, 2), :] = first_column(t_west, t_first)
     turned[pl.ds(17, LEVELS, 2), :] = first_column(s_west, s_first)
-    turned[pl.ds(33, LEVELS, 2), :] = -(turn * inverse_y) * (u_west + roll_lanes(u_west, -1)) * face_first
+    turned[pl.ds(33, LEVELS, 2), :] = -(turn * inverse_y) * (u_west + roll_lanes(u_west, -1))
     sides[...] = turned[...].T
 
     at_first, at_last = lane == 0, lane == LANES - 1
@@ -427,7 +426,7 @@
                     jnp.where(wet, roll_lanes(side, -(2 * k + 1)), 0.0),
                     jnp.where(wet, roll_lanes(side, -(2 * k + 17)), 0.0),
                     jnp.where(at_last, both, 0.0),
-                    jnp.where(at_first, both, 0.0),
+                    jnp.where(at_first & (mf[k, rows, :] > 0), both, 0.0),
                 )
                 for part, add, buffer in zip(early if 1 <= r < EARLY else parts, adds, buffers):
                     buffer[k, rows, :] = part[k, rows, :] + add
@@ -525,13 +524,13 @@
 
     return pl.pallas_call(
         finish,
-        in_specs=whole(12),
+        in_specs=whole(13),
         out_specs=[pl.BlockSpec(memory_space=pltpu.MemorySpace.HBM)] * 4,
         out_shape=[field] * 4,
         scratch_shapes=[square] * 2 + [VMEM(t.shape, f32)] * 4 + [pltpu.SemaphoreType.DMA((4 * CHUNKS,))],
         compiler_params=params,
         name="finish",
-    )(*early, *parts, count, own, lon_b, lon_a)
+    )(*early, *parts, count, mf, own, lon_b, lon_a)
 
 
 def solution(mesh):

time: 30.7 us -> 30.7 us (level)
  transfers between devices with their start and end apart: 3 -> 3, of which waited for: 0 -> 0; matrix products, arithmetic and copies ran while one was open for 0% -> 0% of each run, Pallas kernels for 12% -> 11%
where the time goes in v10:
time: 30.7 us; the launch traced here: 30.5 us
  starting transfers between devices  17.2 us (56%)
  Pallas kernels  6.38 us (21%)
  blocking collectives  6.07 us (20%)
  between operations  0.82 us (3%)
    ppermute x1, starting transfers between devices, per_device(): lat_b = lax.ppermute(lat_to_b, ('lon', 'lat'), pairs_b)  11.9 us
    all_gather x1, blocking collectives, per_device(): lax.all_gather(lon_to_a, 'lon', axis_index_groups=[[i, i + 1] for i in ra...  6.07 us
    ppermute x1, starting transfers between devices, per_device(): lax.ppermute(lon_to_b, 'lon', [(i, (i + 1 if i % 2 else i - 1) % lons) fo...  3.3 us
    pallas_call x1, Pallas kernels, per_device(): pl.pallas_call(front, in_specs=whole(9), out_specs=whole(15), out_shape=[...  2.61 us
    ppermute x1, starting transfers between devices, per_device(): lat_a = lax.ppermute(lat_to_a, 'lat', pairs_a)  1.92 us
    pallas_call x1, Pallas kernels, per_device(): pl.pallas_call(finish, in_specs=whole(13), out_specs=[pl.BlockSpec(memory...  1.6 us
    pallas_call x1, Pallas kernels, per_device(): pl.pallas_call(row_pack, in_specs=[pl.BlockSpec(memory_space=pl.ANY)] * 9...  1.28 us
    pallas_call x1, Pallas kernels, per_device(): pl.pallas_call(middle, in_specs=whole(19), out_specs=whole(4), out_shape=...  0.8 us
  transfers between devices with their start and end apart: 3, of which 0 were waited for; matrix products, arithmetic and copies ran while one was open for 0% of the time, Pallas kernels for 11%

profile of v10, /device:TPU:199, one launch (start us, length us, event | category | flops | bytes accessed | tf_op | source)
XLA Modules:
  0.0 30.5 jit_solution(6762841954761899901)
XLA Ops:
  0.6 0.0 copy-start
  0.6 0.0 copy-start.7
  0.7 0.0 copy-start.6
  0.7 0.0 copy-start.5
  0.7 0.0 copy-start.4
  0.7 0.0 copy-start.3
  0.7 0.0 copy-start.2
  0.7 0.0 copy-start.1
  0.7 1.3 %row_pack.1 = (f32[32,128]{1,0:T(8,128)S(1)}, f32[32,128]{1,0:T(8,128)S(1)}, s32[96,128]{1,0:T(8,128)S(1)}) custom-call(f32[8,96,128]{2,1,0:T(8,128)} %t.5, f32[8,96,128]{2,1,0:T(8,128)} %s.5, f32[8,96,128]{2,1,0:T(8,128)} %u.5, f32[8,96,128]{2,1,0:T(8,128)} %v.5, s32[8,96,128]{2,1,0:T(8,128)} %zf.5, s32[8,96,128]{2,1,0:T(8,128)} %mf.7, f32[96,128]{1,0:T(8,128)} %e1.5, ...), custom_call_target="tpu_custom_call" | custom-call | tf_op jit(solution)/shard_map/row_pack/pallas_call | solution.py:467
  2.0 1.9 %collective-permute-start = (f32[32,128]{1,0:T(8,128)S(1)}, f32[32,128]{1,0:T(8,128)S(1)}, u32[]{:S(2)}, u32[]{:S(2)}) collective-permute-start(f32[32,128]{1,0:T(8,128)S(1)} %get-tuple-element.41), channel_id=1, source_target_pairs={{0,1},{1,0},{2,3},{3,2},{4,5},{5,4},{6,7},{7,6},{8,9},{9,8},{10,11... | collective-permute-start | bytes 49160 | tf_op jit(solution)/shard_map/ppermute | solution.py:488
  3.9 11.9 %collective-permute-start.1 = (f32[32,128]{1,0:T(8,128)S(1)}, f32[32,128]{1,0:T(8,128)S(1)}, u32[]{:S(2)}, u32[]{:S(2)}) collective-permute-start(f32[32,128]{1,0:T(8,128)S(1)} %get-tuple-element.42), channel_id=1, source_target_pairs={{1,2},{2,1},{3,4},{4,3},{5,6},{6,5},{7,8},{8,7},{9,10},{10,9},{11,... | collective-permute-start | bytes 49160 | tf_op jit(solution)/shard_map/ppermute | solution.py:489
  15.9 0.0 copy-done
  15.9 0.0 copy-done.7
  15.9 0.0 copy-done.6
  15.9 0.0 copy-done.5
  15.9 0.0 copy-done.4
  15.9 0.0 copy-done.3
  15.9 0.0 copy-done.2
  16.0 0.0 copy-done.1
  16.0 2.6 %front.1 = (f32[32,128]{1,0:T(8,128)S(1)}, f32[32,128]{1,0:T(8,128)S(1)}, f32[72,128]{1,0:T(8,128)S(1)}, f32[96,128]{1,0:T(8,128)S(1)}, f32[8,112,128]{2,1,0:T(8...) custom-call(f32[8,96,128]{2,1,0:T(8,128)S(1)} %copy-done.1, ...), custom_call_target="tpu_custom_call" | custom-call | tf_op jit(solution)/shard_map/front/pallas_call | solution.py:493
  18.6 0.0 collective-permute-done.lat_a.from_a
  18.6 0.0 collective-permute-done.1.lat_b.from_b
  18.6 0.1 corner_pack.1
  18.7 3.3 %collective-permute-start.2 = (f32[32,128]{1,0:T(8,128)S(1)}, f32[32,128]{1,0:T(8,128)S(1)}, u32[]{:S(2)}, u32[]{:S(2)}) collective-permute-start(f32[32,128]{1,0:T(8,128)S(1)} %get-tuple-element.50), channel_id=1, source_target_pairs={{0,496},{16,32},{32,16},{48,64},{64,48},{80,96},{96,80},{112,128},... | collective-permute-start | bytes 49160 | tf_op jit(solution)/shard_map/ppermute | solution.py:512
  22.0 0.8 %middle.1 = (f32[8,96,128]{2,1,0:T(8,128)S(1)}, f32[8,96,128]{2,1,0:T(8,128)S(1)}, f32[8,96,128]{2,1,0:T(8,128)S(1)}, f32[8,96,128]{2,1,0:T(8,128)S(1)}) custom-call(f32[8,96,128]{2,1,0:T(8,128)S(1)} %copy-done.1, f32[8,96,128]{2,1,0:T(8,128)S(1)} %copy-done.2, f32[8,96,128]{2,1,0:T(8,128)S(1)} %copy-done.3, f32[8,96,128]{2,1,0:T(8,128)S(1)} %copy-done.4, ...), custom_call_target="tpu_custom_call" | custom-call | tf_op jit(solution)/shard_map/middle/pallas_call | solution.py:515
  22.8 6.1 %all_gather.3.lon_a = f32[64,128]{1,0:T(8,128)S(1)} all-gather(f32[32,128]{1,0:T(8,128)S(1)} %get-tuple-element.51), channel_id=1, replica_groups={{0,16},{32,48},{64,80},{96,112},{128,144},{160,176},{192,208},{224,240}..., dimensions={0}, use_global_device_ids=true | all-gather | bytes 49152 | tf_op jit(solution)/shard_map/all_gather | solution.py:513
  28.9 0.0 collective-permute-done.2.lon_b
  28.9 1.6 %finish.1 = (f32[8,96,128]{2,1,0:T(8,128)}, f32[8,96,128]{2,1,0:T(8,128)}, f32[8,96,128]{2,1,0:T(8,128)}, f32[8,96,128]{2,1,0:T(8,128)}) custom-call(f32[8,96,128]{2,1,0:T(8,128)S(1)} %get-tuple-element.29.t_early, f32[8,96,128]{2,1,0:T(8,128)S(1)} %get-tuple-element.30.s_early, f32[8,96,128]{2,1,0:T(8,128)S(1)} %get-tuple-element.31.u_early, ...), custom_call_target="tpu_custom_call" | custom-call | tf_op jit(solution)/shard_map/finish/pallas_call | solution.py:525
Async XLA Ops:
  0.6 15.3 %copy-start = (s32[8,96,128]{2,1,0:T(8,128)S(1)}, s32[8,96,128]{2,1,0:T(8,128)}, u32[]{:S(2)}) copy-start(s32[8,96,128]{2,1,0:T(8,128)} %mf.7) | copy-start | bytes 1179652
  0.6 15.3 %copy-start.7 = (f32[96,128]{1,0:T(8,128)S(1)}, f32[96,128]{1,0:T(8,128)}, u32[]{:S(2)}) copy-start(f32[96,128]{1,0:T(8,128)} %e2.5) | copy-start | bytes 147460
  0.7 15.3 %copy-start.6 = (f32[96,128]{1,0:T(8,128)S(1)}, f32[96,128]{1,0:T(8,128)}, u32[]{:S(2)}) copy-start(f32[96,128]{1,0:T(8,128)} %e1.5) | copy-start | bytes 147460
  0.7 15.3 %copy-start.5 = (s32[8,96,128]{2,1,0:T(8,128)S(1)}, s32[8,96,128]{2,1,0:T(8,128)}, u32[]{:S(2)}) copy-start(s32[8,96,128]{2,1,0:T(8,128)} %zf.5) | copy-start | bytes 1179652
  0.7 15.3 %copy-start.4 = (f32[8,96,128]{2,1,0:T(8,128)S(1)}, f32[8,96,128]{2,1,0:T(8,128)}, u32[]{:S(2)}) copy-start(f32[8,96,128]{2,1,0:T(8,128)} %v.5) | copy-start | bytes 1179652
  0.7 15.3 %copy-start.3 = (f32[8,96,128]{2,1,0:T(8,128)S(1)}, f32[8,96,128]{2,1,0:T(8,128)}, u32[]{:S(2)}) copy-start(f32[8,96,128]{2,1,0:T(8,128)} %u.5) | copy-start | bytes 1179652
  0.7 15.3 %copy-start.2 = (f32[8,96,128]{2,1,0:T(8,128)S(1)}, f32[8,96,128]{2,1,0:T(8,128)}, u32[]{:S(2)}) copy-start(f32[8,96,128]{2,1,0:T(8,128)} %s.5) | copy-start | bytes 1179652
  0.7 15.3 %copy-start.1 = (f32[8,96,128]{2,1,0:T(8,128)S(1)}, f32[8,96,128]{2,1,0:T(8,128)}, u32[]{:S(2)}) copy-start(f32[8,96,128]{2,1,0:T(8,128)} %t.5) | copy-start | bytes 1179652
  2.0 16.6 %collective-permute-start = (f32[32,128]{1,0:T(8,128)S(1)}, f32[32,128]{1,0:T(8,128)S(1)}, u32[]{:S(2)}, u32[]{:S(2)}) collective-permute-start(f32[32,128]{1,0:T(8,128)S(1)} %get-tuple-element.41), channel_id=1, source_target_pairs={{0,1},{1,0},{2,3},{3,2},{4,5},{5,4},{6,7},{7,6},{8,9},{9,8},{10,11... | collective-permute-start | bytes 49160 | tf_op jit(solution)/shard_map/ppermute | solution.py:488
  3.9 14.7 %collective-permute-start.1 = (f32[32,128]{1,0:T(8,128)S(1)}, f32[32,128]{1,0:T(8,128)S(1)}, u32[]{:S(2)}, u32[]{:S(2)}) collective-permute-start(f32[32,128]{1,0:T(8,128)S(1)} %get-tuple-element.42), channel_id=1, source_target_pairs={{1,2},{2,1},{3,4},{4,3},{5,6},{6,5},{7,8},{8,7},{9,10},{10,9},{11,... | collective-permute-start | bytes 49160 | tf_op jit(solution)/shard_map/ppermute | solution.py:489
  18.7 10.2 %collective-permute-start.2 = (f32[32,128]{1,0:T(8,128)S(1)}, f32[32,128]{1,0:T(8,128)S(1)}, u32[]{:S(2)}, u32[]{:S(2)}) collective-permute-start(f32[32,128]{1,0:T(8,128)S(1)} %get-tuple-element.50), channel_id=1, source_target_pairs={{0,496},{16,32},{32,16},{48,64},{64,48},{80,96},{96,80},{112,128},... | collective-permute-start | bytes 49160 | tf_op jit(solution)/shard_map/ppermute | solution.py:512
